TPU v7x, 32 devices: a whole 2x2x4 slice. The times are simulated.
32 devices in a mesh: expert: 8 (over z, y), dp: 4 (over x, core).
Axes of the slice: x: 2, y: 2, z: 4, core: 2. Of those that a mesh axis runs over, the one named last changes fastest.
Arguments:
- out_grad: bfloat16 [2, 2048, 1024], P(None, ('expert', 'dp')), may hold values from -6 to 6
- sub_inputs: bfloat16 [2, 2048, 1024], P(None, ('expert', 'dp')), may hold values from -6 to 6
- route: int32 [2, 2048, 4, 1], P(None, ('expert', 'dp')), may hold values from 0 to 7; in each aligned block of 256 rows (0 to 255, 256 to 511, ..., all dimensions but the last counted through in order) at most 64 rows name the same one
- gate_scale: float32 [2, 2048, 4], P(None, ('expert', 'dp')), may hold values from 0.2 to 1
- merge_weight: bfloat16 [1024, 1024], P('expert'), may hold values from -0.1875 to 0.1875
- split_weight: bfloat16 [1024, 1024], P('expert'), may hold values from -0.1875 to 0.1875
- expert_gate: bfloat16 [8, 256, 768], P('expert'), may hold values from -0.375 to 0.375
- expert_up: bfloat16 [8, 256, 768], P('expert'), may hold values from -0.375 to 0.375
- expert_down: bfloat16 [8, 768, 256], P('expert'), may hold values from -0.21875 to 0.21875
Outputs:
- d_tokens: bfloat16 [2, 2048, 1024], P(None, ('expert', 'dp'))
- grad_gate: float32 [8, 256, 768], P('expert', 'dp')
- grad_up: float32 [8, 256, 768], P('expert', 'dp')
- grad_down: float32 [8, 768, 256], P('expert', 'dp')
Inputs may be any that keep to these rules, and one draw needn't show every extreme that they name: `route`: in each micro-batch the 4 sub-tokens of one device's aligned block of 64 tokens name any one expert at most 64 times, and in some blocks exactly 64 times.
All inputs are finite; a program needn't handle non-finite values.
Results may differ from a plain program's by a relative error of at most 0.015.
Values may be sent and summed in bfloat16 or wider, within the bound.
No kernel may reach another device: no remote copies, remote signals or barrier semaphores. Data moves between devices by JAX's collectives and lax.ppermute only.
A program may use at most 64 MiB of HBM per device.

v0:
```python
import jax
import jax.numpy as jnp
from jax import lax
from jax.sharding import PartitionSpec as P


def transposed(left_rows, right_rows):
    return lax.dot_general(
        left_rows, right_rows, (((1,), (1,)), ((), ())), preferred_element_type=jnp.float32
    )


def leading(left_rows, right_rows):
    return lax.dot_general(
        left_rows, right_rows, (((0,), (0,)), ((), ())), preferred_element_type=jnp.float32
    )


def slot_numbers(expert_ids, expert_count):
    row_count = expert_ids.shape[0]
    onehot = (expert_ids[:, None] == jnp.arange(expert_count, dtype=jnp.int32)[None, :]).astype(
        jnp.bfloat16
    )
    earlier_mask = (jnp.arange(row_count)[:, None] > jnp.arange(row_count)[None, :]).astype(
        jnp.bfloat16
    )
    before = jnp.dot(earlier_mask, onehot, preferred_element_type=jnp.float32)
    return jnp.sum(before * onehot.astype(jnp.float32), axis=1).astype(jnp.int32)


def expert_backward(inputs, grad_rows, weight_gate, weight_up, weight_down):
    pre_gate = jnp.dot(inputs, weight_gate, preferred_element_type=jnp.float32)
    pre_up = jnp.dot(inputs, weight_up, preferred_element_type=jnp.float32)
    sigma = jax.nn.sigmoid(pre_gate)
    activation = pre_gate * sigma
    slope_value = sigma * (1.0 + pre_gate * (1.0 - sigma))
    hidden = (activation * pre_up).astype(jnp.bfloat16)
    d_hidden = transposed(grad_rows, weight_down)
    delta_gate = (d_hidden * pre_up * slope_value).astype(jnp.bfloat16)
    delta_up = (d_hidden * activation).astype(jnp.bfloat16)
    delta_input = (transposed(delta_gate, weight_gate) + transposed(delta_up, weight_up)).astype(
        jnp.bfloat16
    )
    return (
        delta_input,
        leading(inputs, delta_gate),
        leading(inputs, delta_up),
        leading(hidden, grad_rows),
    )


def on_device(
    out_grad,
    sub_inputs,
    route,
    gate_scale,
    merge_weight,
    split_weight,
    expert_gate,
    expert_up,
    expert_down,
):
    batch_count, tok_count, model_width = out_grad.shape
    head_count = route.shape[2]
    sub_width = model_width // head_count
    expert_count = lax.axis_size("expert")
    slots_per = 2 * tok_count * head_count // expert_count
    weight_gate = expert_gate[0]
    weight_up = expert_up[0]
    weight_down = expert_down[0]
    whole_merge, whole_split = (
        lax.all_gather(merge_weight, "expert", axis=0, tiled=True),
        lax.all_gather(split_weight, "expert", axis=0, tiled=True),
    )
    merged_all = transposed(out_grad.reshape(-1, model_width), whole_merge).astype(jnp.bfloat16)
    merged_all = merged_all.reshape(batch_count, tok_count, model_width)
    merged_list = [merged_all[batch_index] for batch_index in range(batch_count)]
    positions = []
    send_inputs = []
    send_grads = []
    for batch_index in range(batch_count):
        expert_ids = route[batch_index, :, :, 0].reshape(-1)
        slots = slot_numbers(expert_ids, expert_count)
        where_rows = expert_ids * slots_per + slots
        input_rows = sub_inputs[batch_index].reshape(-1, sub_width)
        grad_rows = (
            gate_scale[batch_index].reshape(-1, 1)
            * merged_list[batch_index].reshape(-1, sub_width).astype(jnp.float32)
        ).astype(jnp.bfloat16)
        empty_rows = jnp.zeros((expert_count * slots_per, sub_width), jnp.bfloat16)
        send_inputs.append(
            empty_rows.at[where_rows].set(input_rows).reshape(expert_count, slots_per, sub_width)
        )
        send_grads.append(
            empty_rows.at[where_rows].set(grad_rows).reshape(expert_count, slots_per, sub_width)
        )
        positions.append(where_rows)
    grad_gate = jnp.zeros(weight_gate.shape, jnp.float32)
    grad_up = jnp.zeros(weight_up.shape, jnp.float32)
    grad_down = jnp.zeros(weight_down.shape, jnp.float32)
    delta_list = []
    for batch_index in range(batch_count):
        recv_inputs, recv_grads = (
            lax.all_to_all(
                send_inputs[batch_index], "expert", split_axis=0, concat_axis=0, tiled=True
            ),
            lax.all_to_all(
                send_grads[batch_index], "expert", split_axis=0, concat_axis=0, tiled=True
            ),
        )
        delta_input, part_gate, part_up, part_down = expert_backward(
            recv_inputs.reshape(-1, sub_width),
            recv_grads.reshape(-1, sub_width),
            weight_gate,
            weight_up,
            weight_down,
        )
        grad_gate = grad_gate + part_gate
        grad_up = grad_up + part_up
        grad_down = grad_down + part_down
        delta_list.append(delta_input)
    returned_list = []
    for batch_index in range(batch_count):
        returned_list.append(
            lax.all_to_all(
                delta_list[batch_index].reshape(expert_count, slots_per, sub_width),
                "expert",
                split_axis=0,
                concat_axis=0,
                tiled=True,
            )
        )
    sub_list = []
    for batch_index in range(batch_count):
        flat_back = returned_list[batch_index].reshape(-1, sub_width)
        sub_list.append(flat_back[positions[batch_index]].reshape(tok_count, model_width))
    d_sub = jnp.stack(sub_list).reshape(-1, model_width)
    d_tokens = (
        transposed(d_sub, whole_split)
        .astype(jnp.bfloat16)
        .reshape(batch_count, tok_count, model_width)
    )
    shared_gate, shared_up, shared_down = (
        lax.psum_scatter(
            grad_gate[None].astype(jnp.bfloat16), "dp", scatter_dimension=1, tiled=True
        ).astype(jnp.float32),
        lax.psum_scatter(
            grad_up[None].astype(jnp.bfloat16), "dp", scatter_dimension=1, tiled=True
        ).astype(jnp.float32),
        lax.psum_scatter(
            grad_down[None].astype(jnp.bfloat16), "dp", scatter_dimension=1, tiled=True
        ).astype(jnp.float32),
    )
    return (d_tokens, shared_gate, shared_up, shared_down)


def solution(mesh):
    placed = (
        P(None, ("expert", "dp"), None),
        P(None, ("expert", "dp"), None),
        P(None, ("expert", "dp"), None, None),
        P(None, ("expert", "dp"), None),
        P("expert", None),
        P("expert", None),
        P("expert", None, None),
        P("expert", None, None),
        P("expert", None, None),
    )
    return jax.shard_map(
        on_device,
        mesh=mesh,
        in_specs=placed,
        out_specs=(
            P(None, ("expert", "dp"), None),
            P("expert", "dp", None),
            P("expert", "dp", None),
            P("expert", "dp", None),
        ),
        check_vma=False,
    )
```

profile of v0, /device:TPU:0, one launch (start us, length us, event | category | flops | bytes accessed | tf_op | source)
XLA Modules:
  0.0 197.6 jit_solution(3121709094047970735)
XLA Ops:
  10.4 2.1 %scatter_custom_fusion.3 = bf16[512,256]{1,0:T(8,128)(2,1)} fusion(s32[256]{0:T(256)S(1)} %bitcast.112, bf16[256,256]{1,0:T(8,128)(2,1)S(1)} %reshape.194, bf16[]{:T(256)} %constant.0.clone.1), kind=kCustom, calls=%fused_computation.64 | custom fusion | bytes 262146 | tf_op jit(solution)/shard_map/scatter | solution.py:92
  12.6 7.3 %all-to-all-start.4 = ((bf16[8,64,256]{2,1,0:T(8,128)(2,1)}), bf16[8,64,256]{2,1,0:T(8,128)(2,1)S(1)}, u32[]{:S(2)}, u32[]{:S(2)}) async-start(bf16[8,64,256]{2,1,0:T(8,128)(2,1)} %bitcast.16), calls=%async_computation.4 | async-start | bytes 524288 | tf_op jit(solution)/shard_map/all_to_all | solution.py:104
  21.8 2.1 %scatter_custom_fusion.1 = bf16[512,256]{1,0:T(8,128)(2,1)} fusion(s32[256]{0:T(256)S(1)} %bitcast.115, bf16[256,256]{1,0:T(8,128)(2,1)S(1)} %reshape.178, bf16[]{:T(256)} %constant.0.clone.1), kind=kCustom, calls=%fused_computation.67 | custom fusion | bytes 262146 | tf_op jit(solution)/shard_map/scatter | solution.py:92
  23.9 10.7 %all-to-all-done.4 = bf16[8,64,256]{2,1,0:T(8,128)(2,1)S(1)} async-done(((bf16[8,64,256]{2,1,0:T(8,128)(2,1)}), bf16[8,64,256]{2,1,0:T(8,128)(2,1)S(1)}, u32[]{:S(2)}, u32[]{:S(2)}) %all-to-all-start.4) | async-done | bytes 262176 | tf_op jit(solution)/shard_map/all_to_all | solution.py:104
  34.6 3.6 %all-to-all-start.1 = ((bf16[8,64,256]{2,1,0:T(8,128)(2,1)}), bf16[8,64,256]{2,1,0:T(8,128)(2,1)S(1)}, u32[]{:S(2)}, u32[]{:S(2)}) async-start(bf16[8,64,256]{2,1,0:T(8,128)(2,1)} %bitcast.6), calls=%async_computation.1 | async-start | bytes 524288 | tf_op jit(solution)/shard_map/all_to_all | solution.py:104
  38.5 26.7 %all-gather.3.cloned.1.call-done = bf16[1024,1024]{1,0:T(8,128)(2,1)} async-done(((bf16[128,1024]{1,0:T(8,128)(2,1)}), bf16[1024,1024]{1,0:T(8,128)(2,1)}) %all-gather.3.cloned.1.call-update) | async-done | bytes 2097168 | tf_op jit(solution)/shard_map/all_gather | solution.py:72
  65.2 2.4 %convolution_convert_fusion.1 = bf16[128,1024]{1,0:T(8,128)(2,1)S(1)} fusion(bf16[128,1024]{1,0:T(8,128)(2,1)S(1)} %bitcast.108, bf16[1024,1024]{1,0:T(8,128)(2,1)} %all-gather.3.cloned.1.call-done), kind=kOutput, calls=%fused_computation.30 | convolution fusion | flops 268566528 | bytes 2621440 | tf_op jit(solution)/shard_map/dot_general | solution.py:8
  70.2 2.6 %scatter_custom_fusion = bf16[512,256]{1,0:T(8,128)(2,1)} fusion(s32[256]{0:T(256)S(1)} %bitcast.116, f32[256,256]{1,0:T(8,128)} %reshape.148, f32[256]{0:T(256)S(1)} %mul.97, bf16[]{:T(256)} %constant.0.clone.1), kind=kCustom, calls=%fused_computation.58 | custom fusion | flops 131072 | bytes 525314 | tf_op jit(solution)/shard_map/scatter | solution.py:95
  72.8 4.0 %all-to-all-start = ((bf16[8,64,256]{2,1,0:T(8,128)(2,1)}), bf16[8,64,256]{2,1,0:T(8,128)(2,1)}, u32[]{:S(2)}, u32[]{:S(2)}) async-start(bf16[8,64,256]{2,1,0:T(8,128)(2,1)} %bitcast.107), calls=%async_computation | async-start | bytes 524288 | tf_op jit(solution)/shard_map/all_to_all | solution.py:107
  80.7 2.6 %scatter_custom_fusion.2 = bf16[512,256]{1,0:T(8,128)(2,1)} fusion(s32[256]{0:T(256)S(1)} %bitcast.113, f32[256,256]{1,0:T(8,128)} %reshape.149, f32[256]{0:T(256)S(1)} %mul.109, bf16[]{:T(256)} %constant.0.clone.1), kind=kCustom, calls=%fused_computation.59 | custom fusion | flops 131072 | bytes 525314 | tf_op jit(solution)/shard_map/scatter | solution.py:95
  83.4 8.6 %all-to-all-done = bf16[8,64,256]{2,1,0:T(8,128)(2,1)} async-done(((bf16[8,64,256]{2,1,0:T(8,128)(2,1)}), bf16[8,64,256]{2,1,0:T(8,128)(2,1)}, u32[]{:S(2)}, u32[]{:S(2)}) %all-to-all-start) | async-done | bytes 262176 | tf_op jit(solution)/shard_map/all_to_all | solution.py:107
  92.0 3.4 %all-to-all-start.3 = ((bf16[8,64,256]{2,1,0:T(8,128)(2,1)}), bf16[8,64,256]{2,1,0:T(8,128)(2,1)S(1)}, u32[]{:S(2)}, u32[]{:S(2)}) async-start(bf16[8,64,256]{2,1,0:T(8,128)(2,1)} %bitcast.14), calls=%async_computation.3 | async-start | bytes 524288 | tf_op jit(solution)/shard_map/all_to_all | solution.py:107
  97.1 2.4 %fusion.12 = f32[768,256]{1,0:T(8,128)} fusion(bf16[512,256]{1,0:T(8,128)(2,1)} %bitcast.4, f32[512,768]{1,0:T(8,128)S(1)} %fusion.25, f32[512,768]{1,0:T(8,128)S(1)} %copy-done.8), kind=kOutput, calls=%fused_computation.35 | convolution fusion | flops 203685888 | bytes 4194304 | tf_op jit(solution)/shard_map/dot_general | solution.py:14
  99.5 10.2 %all-to-all-done.3 = bf16[8,64,256]{2,1,0:T(8,128)(2,1)S(1)} async-done(((bf16[8,64,256]{2,1,0:T(8,128)(2,1)}), bf16[8,64,256]{2,1,0:T(8,128)(2,1)S(1)}, u32[]{:S(2)}, u32[]{:S(2)}) %all-to-all-start.3) | async-done | bytes 262176 | tf_op jit(solution)/shard_map/all_to_all | solution.py:107
  109.8 3.1 %fusion.5 = bf16[1,768,256]{2,1,0:T(8,128)(2,1)} fusion(f32[768,256]{1,0:T(8,128)} %fusion.12, bf16[512,256]{1,0:T(8,128)(2,1)S(1)} %bitcast.110, f32[512,768]{1,0:T(8,128)} %fusion.22, f32[512,768]{1,0:T(8,128)S(1)} %fusion.15), kind=kOutput, calls=%fused_computation.24 | convolution fusion | flops 204079104 | bytes 4587520 | tf_op jit(solution)/shard_map/dot_general | solution.py:14
  112.8 3.0 %multiply_convert_fusion.4 = (bf16[512,768]{1,0:T(8,128)(2,1)S(1)}, bf16[512,768]{1,0:T(8,128)(2,1)S(1)}) fusion(f32[512,768]{1,0:T(8,128)} %fusion.19, f32[512,768]{1,0:T(8,128)} %copy-done.9, bf16[512,256]{1,0:T(8,128)(2,1)} %bitcast.4, bf16[1,768,256]{2,1,0:T(8,128)(2,1)S(1)} %copy-done), kind=kOutput, calls=%fused_computation.12 | convolution fusion | flops 206438400 | bytes 5373952 | tf_op jit(solution)/shard_map/dot_general | solution.py:8
  122.5 4.1 %all-to-all-start.2 = ((bf16[8,64,256]{2,1,0:T(8,128)(2,1)}), bf16[8,64,256]{2,1,0:T(8,128)(2,1)S(1)}, u32[]{:S(2)}, u32[]{:S(2)}) async-start(bf16[8,64,256]{2,1,0:T(8,128)(2,1)} %bitcast.10), calls=%async_computation.2 | async-start | bytes 524288 | tf_op jit(solution)/shard_map/all_to_all | solution.py:125
  128.1 2.3 %fusion.9 = bf16[512,256]{1,0:T(8,128)(2,1)} fusion(f32[512,256]{1,0:T(8,128)S(1)} %fusion.13, bf16[512,768]{1,0:T(8,128)(2,1)} %get-tuple-element.6, bf16[1,256,768]{2,1,0:T(8,128)(2,1)S(1)} %copy-done.2), kind=kOutput, calls=%fused_computation.28 | convolution fusion | flops 201588736 | bytes 1966080 | tf_op jit(solution)/shard_map/dot_general | solution.py:8
  130.5 4.4 %all-to-all-done.2 = bf16[8,64,256]{2,1,0:T(8,128)(2,1)S(1)} async-done(((bf16[8,64,256]{2,1,0:T(8,128)(2,1)}), bf16[8,64,256]{2,1,0:T(8,128)(2,1)S(1)}, u32[]{:S(2)}, u32[]{:S(2)}) %all-to-all-start.2) | async-done | bytes 262176 | tf_op jit(solution)/shard_map/all_to_all | solution.py:125
  134.8 3.4 %all-to-all-start.5 = ((bf16[8,64,256]{2,1,0:T(8,128)(2,1)}), bf16[8,64,256]{2,1,0:T(8,128)(2,1)S(1)}, u32[]{:S(2)}, u32[]{:S(2)}) async-start(bf16[8,64,256]{2,1,0:T(8,128)(2,1)} %bitcast.18), calls=%async_computation.5 | async-start | bytes 524288 | tf_op jit(solution)/shard_map/all_to_all | solution.py:125
  140.8 5.7 %all-to-all-done.5 = bf16[8,64,256]{2,1,0:T(8,128)(2,1)S(1)} async-done(((bf16[8,64,256]{2,1,0:T(8,128)(2,1)}), bf16[8,64,256]{2,1,0:T(8,128)(2,1)S(1)}, u32[]{:S(2)}, u32[]{:S(2)}) %all-to-all-start.5) | async-done | bytes 262176 | tf_op jit(solution)/shard_map/all_to_all | solution.py:125
  147.7 3.1 %convolution_convert_fusion = bf16[128,1024]{1,0:T(8,128)(2,1)} fusion(bf16[128,1024]{1,0:T(8,128)(2,1)S(1)} %bitcast.106, bf16[1024,1024]{1,0:T(8,128)(2,1)} %all-gather.5.cloned.1.call-done), kind=kOutput, calls=%fused_computation.29 | convolution fusion | flops 268566528 | bytes 2621440 | tf_op jit(solution)/shard_map/dot_general | solution.py:8
  152.4 13.9 %reduce-scatter.6.cloned.1.call-done = bf16[1,64,768]{2,1,0:T(8,128)(2,1)} async-done(((bf16[1,256,768]{2,1,0:T(8,128)(2,1)}), bf16[1,64,768]{2,1,0:T(8,128)(2,1)}) %reduce-scatter.6.cloned.1.call-update) | async-done | bytes 98320 | tf_op jit(solution)/shard_map/reduce_scatter | solution.py:147
  167.9 21.6 %reduce-scatter.4.cloned.1.call-done = bf16[1,64,768]{2,1,0:T(8,128)(2,1)} async-done(((bf16[1,256,768]{2,1,0:T(8,128)(2,1)}), bf16[1,64,768]{2,1,0:T(8,128)(2,1)}) %reduce-scatter.4.cloned.1.call-update) | async-done | bytes 98320 | tf_op jit(solution)/shard_map/reduce_scatter | solution.py:144
  (85 shorter events, 30.0 us)
Async XLA Ops:
  7.2 105.7 %copy-start = (bf16[1,768,256]{2,1,0:T(8,128)(2,1)S(1)}, bf16[1,768,256]{2,1,0:T(8,128)(2,1)}, u32[]{:S(2)}) copy-start(bf16[1,768,256]{2,1,0:T(8,128)(2,1)} %param.17) | copy-start | bytes 1179652
  7.2 13.6 %copy-start.11 = (f32[2,64,4]{1,2,0:T(4,128)S(1)}, f32[2,64,4]{1,2,0:T(4,128)}, u32[]{:S(2)}) copy-start(f32[2,64,4]{1,2,0:T(4,128)} %param.12) | copy-start | bytes 6148
  7.2 58.1 %all-gather.3.cloned.1.call-start = ((), (), s32[]{:S(2)}) async-start(), calls=%async_computation.9 | async-start | bytes 2359296 | tf_op jit(solution)/shard_map/all_gather | solution.py:72
  9.3 28.9 %copy-start.1 = (bf16[1,256,768]{2,1,0:T(8,128)(2,1)S(1)}, bf16[1,256,768]{2,1,0:T(8,128)(2,1)}, u32[]{:S(2)}) copy-start(bf16[1,256,768]{2,1,0:T(8,128)(2,1)} %param.15) | copy-start | bytes 1179652
  12.6 22.0 %all-to-all-start.4 = ((bf16[8,64,256]{2,1,0:T(8,128)(2,1)}), bf16[8,64,256]{2,1,0:T(8,128)(2,1)S(1)}, u32[]{:S(2)}, u32[]{:S(2)}) async-start(bf16[8,64,256]{2,1,0:T(8,128)(2,1)} %bitcast.16), calls=%async_computation.4 | async-start | bytes 524288 | tf_op jit(solution)/shard_map/all_to_all | solution.py:104
  19.8 127.9 %all-gather.5.cloned.1.call-start = ((), (), s32[]{:S(2)}) async-start(), calls=%async_computation.10 | async-start | bytes 2359296 | tf_op jit(solution)/shard_map/all_gather | solution.py:73
  21.7 43.5 %copy-start.10 = (bf16[2,64,1024]{2,1,0:T(8,128)(2,1)S(1)}, bf16[2,64,1024]{2,1,0:T(8,128)(2,1)}, u32[]{:S(2)}) copy-start(bf16[2,64,1024]{2,1,0:T(8,128)(2,1)} %param.9) | copy-start | bytes 786436
  34.6 38.2 %all-to-all-start.1 = ((bf16[8,64,256]{2,1,0:T(8,128)(2,1)}), bf16[8,64,256]{2,1,0:T(8,128)(2,1)S(1)}, u32[]{:S(2)}, u32[]{:S(2)}) async-start(bf16[8,64,256]{2,1,0:T(8,128)(2,1)} %bitcast.6), calls=%async_computation.1 | async-start | bytes 524288 | tf_op jit(solution)/shard_map/all_to_all | solution.py:104
  38.5 71.2 %copy-start.5 = (f32[512,768]{1,0:T(8,128)}, f32[512,768]{1,0:T(8,128)S(1)}, u32[]{:S(2)}) copy-start(f32[512,768]{1,0:T(8,128)S(1)} %fusion.15) | copy-start | bytes 4718596
  67.7 9.2 %copy-start.2 = (bf16[1,256,768]{2,1,0:T(8,128)(2,1)S(1)}, bf16[1,256,768]{2,1,0:T(8,128)(2,1)}, u32[]{:S(2)}) copy-start(bf16[1,256,768]{2,1,0:T(8,128)(2,1)} %param.16) | copy-start | bytes 1179652
  72.8 19.2 %all-to-all-start = ((bf16[8,64,256]{2,1,0:T(8,128)(2,1)}), bf16[8,64,256]{2,1,0:T(8,128)(2,1)}, u32[]{:S(2)}, u32[]{:S(2)}) async-start(bf16[8,64,256]{2,1,0:T(8,128)(2,1)} %bitcast.107), calls=%async_computation | async-start | bytes 524288 | tf_op jit(solution)/shard_map/all_to_all | solution.py:107
  92.0 17.8 %all-to-all-start.3 = ((bf16[8,64,256]{2,1,0:T(8,128)(2,1)}), bf16[8,64,256]{2,1,0:T(8,128)(2,1)S(1)}, u32[]{:S(2)}, u32[]{:S(2)}) async-start(bf16[8,64,256]{2,1,0:T(8,128)(2,1)} %bitcast.14), calls=%async_computation.3 | async-start | bytes 524288 | tf_op jit(solution)/shard_map/all_to_all | solution.py:107
  95.4 55.5 %reduce-scatter.8.cloned.1.call-start = ((), (), s32[]{:S(2)}) async-start(), calls=%async_computation.13 | async-start | bytes 491520 | tf_op jit(solution)/shard_map/reduce_scatter | solution.py:150
  95.4 1.6 copy-start.8
  95.8 1.2 copy-start.9
  112.8 3.1 %copy-start.6 = (f32[512,768]{1,0:T(8,128)S(1)}, f32[512,768]{1,0:T(8,128)}, u32[]{:S(2)}) copy-start(f32[512,768]{1,0:T(8,128)} %copy-done.5) | copy-start | bytes 4718596
  112.8 3.1 %copy-start.7 = (f32[512,768]{1,0:T(8,128)S(1)}, f32[512,768]{1,0:T(8,128)}, u32[]{:S(2)}) copy-start(f32[512,768]{1,0:T(8,128)} %fusion.22) | copy-start | bytes 4718596
  118.0 48.3 %reduce-scatter.6.cloned.1.call-start = ((), (), s32[]{:S(2)}) async-start(), calls=%async_computation.12 | async-start | bytes 491520 | tf_op jit(solution)/shard_map/reduce_scatter | solution.py:147
  118.2 1.1 copy-start.4
  122.5 12.4 %all-to-all-start.2 = ((bf16[8,64,256]{2,1,0:T(8,128)(2,1)}), bf16[8,64,256]{2,1,0:T(8,128)(2,1)S(1)}, u32[]{:S(2)}, u32[]{:S(2)}) async-start(bf16[8,64,256]{2,1,0:T(8,128)(2,1)} %bitcast.10), calls=%async_computation.2 | async-start | bytes 524288 | tf_op jit(solution)/shard_map/all_to_all | solution.py:125
  128.1 10.2 %copy-start.3 = (bf16[512,768]{1,0:T(8,128)(2,1)S(1)}, bf16[512,768]{1,0:T(8,128)(2,1)}, u32[]{:S(2)}) copy-start(bf16[512,768]{1,0:T(8,128)(2,1)} %get-tuple-element.7) | copy-start | bytes 2359300
  134.8 11.6 %all-to-all-start.5 = ((bf16[8,64,256]{2,1,0:T(8,128)(2,1)}), bf16[8,64,256]{2,1,0:T(8,128)(2,1)S(1)}, u32[]{:S(2)}, u32[]{:S(2)}) async-start(bf16[8,64,256]{2,1,0:T(8,128)(2,1)} %bitcast.18), calls=%async_computation.5 | async-start | bytes 524288 | tf_op jit(solution)/shard_map/all_to_all | solution.py:125
  138.3 51.2 %reduce-scatter.4.cloned.1.call-start = ((), (), s32[]{:S(2)}) async-start(), calls=%async_computation.11 | async-start | bytes 491520 | tf_op jit(solution)/shard_map/reduce_scatter | solution.py:144
Sparse Core Ops, SparseCore 0:
  10.2 55.0 all-gather.2
  67.4 54.1 all-gather.4
  124.1 19.0 reduce-scatter.7
  145.5 20.7 reduce-scatter.5
  168.7 20.7 reduce-scatter.3
where the time goes:
time: 199 us; the launch traced here: 198 us
  waiting for transfers between devices  103 us (52%)
  matrix products  28.9 us (15%)
  starting transfers between devices  26.2 us (13%)
  between operations  14.1 us (7%)
  local copies, waits for them, and re-layouts  13.7 us (7%)
  other arithmetic  11.5 us (6%)
    all_gather x1, waiting for transfers between devices, on_device(): lax.all_gather(merge_weight, 'expert', axis=0, tiled=True)  26.7 us
    reduce_scatter x1, waiting for transfers between devices, on_device(): lax.psum_scatter(grad_gate[None].astype(jnp.bfloat16), 'dp', scatter_dime...  21.6 us
    all_to_all x2, waiting for transfers between devices, on_device(): lax.all_to_all(send_grads[batch_index], 'expert', split_axis=0, concat_ax...  18.9 us
    dot_general x8, matrix products, transposed(): lax.dot_general(left_rows, right_rows, (((1,), (1,)), ((), ())), preferre...  16.1 us
    reduce_scatter x1, waiting for transfers between devices, on_device(): lax.psum_scatter(grad_up[None].astype(jnp.bfloat16), 'dp', scatter_dimens...  13.9 us
    all_to_all x2, starting transfers between devices, on_device(): lax.all_to_all(send_inputs[batch_index], 'expert', split_axis=0, concat_a...  10.9 us
    all_to_all x2, waiting for transfers between devices, on_device(): lax.all_to_all(send_inputs[batch_index], 'expert', split_axis=0, concat_a...  10.7 us
    all_to_all x2, waiting for transfers between devices, on_device(): lax.all_to_all(delta_list[batch_index].reshape(expert_count, slots_per, s...  10 us
  transfers between devices with their start and end apart: 11, of which 8 were waited for; matrix products, arithmetic and copies ran while one was open for 26% of the time, Pallas kernels for 0%

commit v1 on v0

v1 whole, which is shorter than its diff:
```python
import jax
import jax.numpy as jnp
from jax import lax
from jax.experimental import pallas as pl
from jax.experimental.pallas import tpu as pltpu
from jax.sharding import PartitionSpec as P

LANES = 128
VMEM_BYTES = 40 * 1024 * 1024


def transposed(left_rows, right_rows):
    return lax.dot_general(
        left_rows, right_rows, (((1,), (1,)), ((), ())), preferred_element_type=jnp.float32
    )


def leading(left_rows, right_rows):
    return lax.dot_general(
        left_rows, right_rows, (((0,), (0,)), ((), ())), preferred_element_type=jnp.float32
    )


def plain(left_rows, right_rows):
    return jnp.dot(left_rows, right_rows, preferred_element_type=jnp.float32)


def power_of_two(number):
    return number & (number - 1) == 0


def swap(value, axis, offset):
    return lax.ppermute(
        value, axis, [(index, index ^ offset) for index in range(lax.axis_size(axis))]
    )


def params():
    return pltpu.CompilerParams(vmem_limit_bytes=VMEM_BYTES)


def cost(flops, moved):
    return pl.CostEstimate(flops=flops, bytes_accessed=moved, transcendentals=0)


def gather_blocks(block, axis):
    span = lax.axis_size(axis)
    offsets = [0]
    while span > 1:
        radix = 4 if span % 4 == 0 and axis == "expert" else 2
        span //= radix
        block = jnp.concatenate(
            [block] + [swap(block, axis, step * span) for step in range(1, radix)]
        )
        offsets = [old ^ (step * span) for step in range(radix) for old in offsets]
    return block, offsets


def route_kernel(batch_count, slots_per, key_count, ids_ref, rows_ref, send_ref, across_ref, down_ref):
    head_count, row_count = ids_ref.shape
    width = rows_ref.shape[1] // head_count
    lane = lax.broadcasted_iota(jnp.int32, (1, row_count), 1)
    batch = jnp.zeros((1, row_count), jnp.int32)
    for number in range(1, batch_count):
        batch = batch + (lane >= number * (row_count // batch_count)).astype(jnp.int32)
    keys = [ids_ref[head : head + 1, :] * batch_count + batch for head in range(head_count)]
    key = jnp.concatenate(keys, axis=1)
    total = head_count * row_count
    onehot = lax.broadcasted_iota(jnp.int32, (key_count, total), 0) == key
    earlier = lax.broadcasted_iota(jnp.int32, (total, total), 0) < lax.broadcasted_iota(
        jnp.int32, (total, total), 1
    )
    before = plain(
        onehot.astype(jnp.float32).astype(jnp.bfloat16),
        earlier.astype(jnp.float32).astype(jnp.bfloat16),
    )
    slot = jnp.sum(jnp.where(onehot, before, 0.0), axis=0, keepdims=True).astype(jnp.int32)
    target = key * slots_per + slot
    send_ref[...] = scatter_rows(
        target,
        [rows_ref[:, head * width : (head + 1) * width] for head in range(head_count)],
        send_ref.shape[0],
    )
    across = jnp.concatenate(
        [target[:, head * row_count : (head + 1) * row_count] for head in range(head_count)], axis=0
    )
    across_ref[...] = across
    down_ref[...] = across.astype(jnp.float32).T.astype(jnp.int32)


def scatter_rows(target, row_list, slot_count):
    total = target.shape[1]
    picked = lax.broadcasted_iota(jnp.int32, (slot_count, total), 0) == target
    return plain(
        picked.astype(jnp.float32).astype(jnp.bfloat16), jnp.concatenate(row_list, axis=0)
    ).astype(jnp.bfloat16)


def merge_kernel(offsets, block_rows, token_ref, weight_ref, *rest):
    out_refs, held = rest[:-1], rest[-1]
    here = lax.axis_index("expert")
    for place, offset in enumerate(offsets):
        start = pl.multiple_of((here ^ offset) * block_rows, block_rows)
        held[pl.ds(start, block_rows), :] = weight_ref[
            place * block_rows : (place + 1) * block_rows, :
        ]
    count = out_refs[0].shape[0]
    result = transposed(token_ref[...], held[...]).astype(jnp.bfloat16)
    for number, out_ref in enumerate(out_refs):
        out_ref[...] = result[number * count : (number + 1) * count]


def assemble(offsets, part_refs, width):
    here = lax.axis_index("dp")
    parts = [ref[...].astype(jnp.float32) for ref in part_refs]
    group = len(parts)
    rows, held = parts[0].shape
    lane = lax.broadcasted_iota(jnp.int32, (rows, LANES), 1)
    blocks = []
    for expert in range(held // width):
        base = expert * width // LANES * LANES
        inside = expert * width - base
        block = jnp.zeros((rows, LANES), jnp.float32)
        for offset, part in zip(offsets, parts):
            first = (here ^ offset) * width
            shift = lax.rem(first + LANES - inside, LANES)
            moved = pltpu.roll(part[:, base : base + LANES], shift, 1)
            block = jnp.where((lane >= first) & (lane < first + width), moved, block)
        blocks.append(block)
    return jnp.concatenate(blocks, axis=1)


def grad_kernel(offsets, width, scale_ref, across_ref, *rest):
    part_refs, send_ref = rest[:-1], rest[-1]
    merged = (
        part_refs[0][...].astype(jnp.float32)
        if offsets is None
        else assemble(offsets, part_refs, width)
    )
    head_count = across_ref.shape[0]
    sub_width = merged.shape[1] // head_count
    rows = [
        (
            scale_ref[:, head : head + 1] * merged[:, head * sub_width : (head + 1) * sub_width]
        ).astype(jnp.bfloat16)
        for head in range(head_count)
    ]
    target = jnp.concatenate([across_ref[head : head + 1, :] for head in range(head_count)], axis=1)
    send_ref[...] = scatter_rows(target, rows, send_ref.shape[0])


def delta_kernel(input_ref, grad_ref, gate_ref, up_ref, down_ref, delta_ref, both_ref, hidden_ref):
    inputs = input_ref[...]
    hidden_width = gate_ref.shape[1]
    pre_gate = plain(inputs, gate_ref[...])
    pre_up = plain(inputs, up_ref[...])
    d_hidden = transposed(grad_ref[...], down_ref[...])
    sigma = jax.nn.sigmoid(pre_gate)
    activation = pre_gate * sigma
    slope_value = sigma * (1.0 + pre_gate * (1.0 - sigma))
    hidden_ref[...] = (activation * pre_up).astype(jnp.bfloat16)
    delta_gate = (d_hidden * pre_up * slope_value).astype(jnp.bfloat16)
    delta_up = (d_hidden * activation).astype(jnp.bfloat16)
    both_ref[:, :hidden_width] = delta_gate
    both_ref[:, hidden_width:] = delta_up
    delta_ref[...] = (
        transposed(delta_gate, gate_ref[...]) + transposed(delta_up, up_ref[...])
    ).astype(jnp.bfloat16)


def weight_kernel(
    group, input_ref, grad_ref, both_ref, hidden_ref, keep_a, keep_b, send_a, send_b, held_a, held_b
):
    here = lax.axis_index("dp")
    held_a[...] = leading(input_ref[...], both_ref[...])
    held_b[...] = leading(hidden_ref[...], grad_ref[...])
    for held, keep, send in ((held_a, keep_a, send_a), (held_b, keep_b, send_b)):
        rows = held.shape[0] // group
        for place in range(group // 2):
            own = pl.multiple_of((here ^ (2 * place)) * rows, rows)
            keep[place] = held[pl.ds(own, rows), :]
            other = pl.multiple_of((here ^ (2 * place + 1)) * rows, rows)
            send[place] = held[pl.ds(other, rows), :].astype(jnp.bfloat16)


def halve_kernel(keep_a, keep_b, got_a, got_b, next_a, next_b, send_a, send_b):
    for keep, got, own, send in (
        (keep_a, got_a, next_a, send_a),
        (keep_b, got_b, next_b, send_b),
    ):
        count = own.shape[0]
        for place in range(count):
            own[place] = keep[2 * place] + got[2 * place].astype(jnp.float32)
            send[place] = (keep[2 * place + 1] + got[2 * place + 1].astype(jnp.float32)).astype(
                jnp.bfloat16
            )


def last_kernel(keep_a, keep_b, got_a, got_b, gate_ref, up_ref, down_ref):
    width = gate_ref.shape[2]
    summed = keep_a[0] + got_a[0].astype(jnp.float32)
    gate_ref[0] = summed[:, :width]
    up_ref[0] = summed[:, width:]
    down_ref[0] = keep_b[0] + got_b[0].astype(jnp.float32)


def order_kernel(dp_offsets, offsets, block_rows, weight_ref, out_ref):
    here, group = lax.axis_index("expert"), lax.axis_index("dp")
    place = 0
    for dp_offset in dp_offsets:
        for offset in offsets:
            start = ((here ^ offset) * len(dp_offsets) + (group ^ dp_offset)) * block_rows
            out_ref[pl.ds(pl.multiple_of(start, block_rows), block_rows), :] = weight_ref[
                place * block_rows : (place + 1) * block_rows, :
            ]
            place += 1


def split_kernel(down_ref, back_ref, weight_ref, out_ref):
    row_count, head_count = down_ref.shape
    slot_count, width = back_ref.shape
    lane = lax.broadcasted_iota(jnp.int32, (row_count, slot_count), 1)
    picked = jnp.concatenate(
        [
            (lane == down_ref[:, head : head + 1]).astype(jnp.float32).astype(jnp.bfloat16)
            for head in range(head_count)
        ],
        axis=0,
    )
    rows = plain(picked, back_ref[...]).astype(jnp.bfloat16)
    d_sub = jnp.concatenate(
        [rows[head * row_count : (head + 1) * row_count] for head in range(head_count)], axis=1
    )
    out_ref[...] = transposed(d_sub, weight_ref[...]).astype(jnp.bfloat16)


def on_device(
    out_grad,
    sub_inputs,
    route,
    gate_scale,
    merge_weight,
    split_weight,
    expert_gate,
    expert_up,
    expert_down,
):
    batch_count, tok_count, model_width = out_grad.shape
    head_count = route.shape[2]
    sub_width = model_width // head_count
    expert_count = lax.axis_size("expert")
    group = lax.axis_size("dp")
    here = lax.axis_index("dp")
    slots_per = 2 * tok_count * head_count // expert_count
    row_count = batch_count * tok_count
    key_count = expert_count * batch_count
    slot_count = key_count * slots_per
    shard_rows = merge_weight.shape[0]
    hidden_width = expert_gate.shape[2]
    bf16, f32 = jnp.bfloat16, jnp.float32
    block_rows = shard_rows // group
    in_blocks = (
        shard_rows == LANES
        and block_rows % 16 == 0
        and power_of_two(expert_count)
        and power_of_two(group)
    )
    shape = jax.ShapeDtypeStruct
    tokens = out_grad.reshape(row_count, model_width)
    rows_in = sub_inputs.reshape(row_count, model_width)
    scale = gate_scale.reshape(row_count, head_count)
    ids = route.reshape(row_count, head_count).T

    if in_blocks:
        merge_block = lax.dynamic_slice_in_dim(merge_weight, here * block_rows, block_rows, 0)
        split_block = lax.dynamic_slice_in_dim(split_weight, here * block_rows, block_rows, 0)
        merge_part, offsets = gather_blocks(merge_block, "expert")
        tokens_all, dp_offsets = gather_blocks(tokens, "dp")
    else:
        whole_merge = lax.all_gather(merge_weight, "expert", axis=0, tiled=True)
        whole_split = lax.all_gather(split_weight, "expert", axis=0, tiled=True)

    def route_body(*refs):
        route_kernel(batch_count, slots_per, key_count, *refs)

    send_inputs, across, down = pl.pallas_call(
        route_body,
        out_shape=(
            shape((slot_count, sub_width), bf16),
            shape((head_count, row_count), jnp.int32),
            shape((row_count, head_count), jnp.int32),
        ),
        compiler_params=params(),
        cost_estimate=cost(2 * slot_count * row_count * model_width, 2 * slot_count * sub_width),
    )(ids, rows_in)

    def exchange(rows):
        return lax.all_to_all(
            rows.reshape(expert_count, -1, sub_width), "expert", 0, 0, tiled=True
        ).reshape(slot_count, sub_width)

    recv_inputs = exchange(send_inputs)

    if in_blocks:

        def merge_body(*refs):
            merge_kernel(offsets, block_rows, *refs)

        part_width = expert_count * block_rows
        parts = pl.pallas_call(
            merge_body,
            out_shape=tuple(shape((row_count, part_width), bf16) for _ in range(group)),
            scratch_shapes=[pltpu.VMEM((part_width, model_width), bf16)],
            compiler_params=params(),
            cost_estimate=cost(
                2 * group * row_count * part_width * model_width, 2 * group * row_count * model_width
            ),
        )(tokens_all, merge_part)
        parts = [
            part if offset == 0 else swap(part, "dp", offset)
            for part, offset in zip(parts, dp_offsets)
        ]
    else:
        dp_offsets = None
        parts = [transposed(tokens, whole_merge).astype(bf16)]

    def grad_body(*refs):
        grad_kernel(dp_offsets, block_rows, *refs)

    send_grads = pl.pallas_call(
        grad_body,
        out_shape=shape((slot_count, sub_width), bf16),
        compiler_params=params(),
        cost_estimate=cost(2 * slot_count * row_count * model_width, 2 * slot_count * sub_width),
    )(scale, across, *parts)
    recv_grads = exchange(send_grads)

    weight_gate = expert_gate[0]
    weight_up = expert_up[0]
    weight_down = expert_down[0]
    steps = 4
    chunk = slot_count // steps
    by_rows = lambda width: pl.BlockSpec((chunk, width), lambda step: (step, 0))
    held = lambda array: pl.BlockSpec(array.shape, lambda step: (0, 0))
    delta, both, hidden = pl.pallas_call(
        delta_kernel,
        grid=(steps,),
        in_specs=[
            by_rows(sub_width),
            by_rows(sub_width),
            held(weight_gate),
            held(weight_up),
            held(weight_down),
        ],
        out_specs=(by_rows(sub_width), by_rows(2 * hidden_width), by_rows(hidden_width)),
        out_shape=(
            shape((slot_count, sub_width), bf16),
            shape((slot_count, 2 * hidden_width), bf16),
            shape((slot_count, hidden_width), bf16),
        ),
        compiler_params=params(),
        cost_estimate=cost(10 * slot_count * sub_width * hidden_width, 8 * slot_count * hidden_width),
    )(recv_inputs, recv_grads, weight_gate, weight_up, weight_down)
    returned = exchange(delta)

    half = group // 2
    gate_rows, down_rows = sub_width // group, hidden_width // group

    def weight_body(*refs):
        weight_kernel(group, *refs)

    keep_a, keep_b, send_a, send_b = pl.pallas_call(
        weight_body,
        out_shape=(
            shape((half, gate_rows, 2 * hidden_width), f32),
            shape((half, down_rows, sub_width), f32),
            shape((half, gate_rows, 2 * hidden_width), bf16),
            shape((half, down_rows, sub_width), bf16),
        ),
        scratch_shapes=[
            pltpu.VMEM((sub_width, 2 * hidden_width), f32),
            pltpu.VMEM((hidden_width, sub_width), f32),
        ],
        compiler_params=params(),
        cost_estimate=cost(6 * slot_count * sub_width * hidden_width, 8 * slot_count * hidden_width),
    )(recv_inputs, recv_grads, both, hidden)
    offset = 1
    while 2 * offset < group:
        half //= 2
        got_a, got_b = swap(send_a, "dp", offset), swap(send_b, "dp", offset)
        keep_a, keep_b, send_a, send_b = pl.pallas_call(
            halve_kernel,
            out_shape=(
                shape((half, gate_rows, 2 * hidden_width), f32),
                shape((half, down_rows, sub_width), f32),
                shape((half, gate_rows, 2 * hidden_width), bf16),
                shape((half, down_rows, sub_width), bf16),
            ),
            compiler_params=params(),
        )(keep_a, keep_b, got_a, got_b)
        offset *= 2
    got_a, got_b = swap(send_a, "dp", offset), swap(send_b, "dp", offset)
    shared_gate, shared_up, shared_down = pl.pallas_call(
        last_kernel,
        out_shape=(
            shape((1, gate_rows, hidden_width), f32),
            shape((1, gate_rows, hidden_width), f32),
            shape((1, down_rows, sub_width), f32),
        ),
        compiler_params=params(),
    )(keep_a, keep_b, got_a, got_b)

    if in_blocks:
        split_part, _ = gather_blocks(split_block, "expert")
        split_all, _ = gather_blocks(split_part, "dp")

        def order_body(*refs):
            order_kernel(dp_offsets, offsets, block_rows, *refs)

        whole_split = pl.pallas_call(
            order_body,
            out_shape=shape((model_width, model_width), bf16),
            compiler_params=params(),
        )(split_all)
    d_tokens = pl.pallas_call(
        split_kernel,
        out_shape=shape((row_count, model_width), bf16),
        compiler_params=params(),
    )(down, returned, whole_split).reshape(batch_count, tok_count, model_width)
    return (d_tokens, shared_gate, shared_up, shared_down)


def solution(mesh):
    placed = (
        P(None, ("expert", "dp"), None),
        P(None, ("expert", "dp"), None),
        P(None, ("expert", "dp"), None, None),
        P(None, ("expert", "dp"), None),
        P("expert", None),
        P("expert", None),
        P("expert", None, None),
        P("expert", None, None),
        P("expert", None, None),
    )
    return jax.shard_map(
        on_device,
        mesh=mesh,
        in_specs=placed,
        out_specs=(
            P(None, ("expert", "dp"), None),
            P("expert", "dp", None),
            P("expert", "dp", None),
            P("expert", "dp", None),
        ),
        check_vma=False,
    )
```

time: 199 us -> 115 us (0.58)
  waiting for transfers between devices: 103 us -> 30.9 us
  matrix products: 28.9 us -> 0 us
  local copies, waits for them, and re-layouts: 13.7 us -> 28.6 us
  between operations: 14.1 us -> 0.84 us
  Pallas kernels: 0 us -> 13 us
  starting transfers between devices: 26.2 us -> 36 us
  other arithmetic: 11.5 us -> 4.58 us
    all_to_all x6 -> x3, waiting for transfers between devices: 39.6 us -> 0.01 us  [exchange(): lax.all_to_all(rows.reshape(expert_count, -1, sub_width), 'expert', 0, 0,...]
    reduce_scatter x3 -> x0, waiting for transfers between devices: 35.5 us -> none  [the longest x1 21.6 us: on_device(): lax.psum_scatter(grad_gate[None].astype(jnp.bfloat16), 'dp', scatter_dime...]
    ppermute x0 -> x19, waiting for transfers between devices: none -> 30.9 us  [swap(): lax.ppermute(value, axis, [(index, index ^ offset) for index in range(lax...]
    dot_general x20 -> x0, matrix products: 28.9 us -> none  [the longest x8 16.1 us: transposed(): lax.dot_general(left_rows, right_rows, (((1,), (1,)), ((), ())), preferre...]
    all_gather x2 -> x0, waiting for transfers between devices: 26.7 us -> none  [the longest x1 26.7 us: on_device(): lax.all_gather(merge_weight, 'expert', axis=0, tiled=True)]
    unnamed x24 -> x52, local copies, waits for them, and re-layouts: 2.02 us -> 26.3 us
    ppermute x0 -> x19, starting transfers between devices: none -> 21 us  [swap(): lax.ppermute(value, axis, [(index, index ^ offset) for index in range(lax...]
    pallas_call x0 -> x9, Pallas kernels: none -> 13 us  [the longest x1 4.19 us: on_device(): pl.pallas_call(delta_kernel, grid=(steps,), in_specs=[by_rows(sub_width),...]
  transfers between devices with their start and end apart: 11 -> 22, of which waited for: 8 -> 6; matrix products, arithmetic and copies ran while one was open for 26% -> 16% of each run, Pallas kernels for 0% -> 9%
where the time goes in v1:
time: 115 us; the launch traced here: 114 us
  starting transfers between devices  36 us (31%)
  waiting for transfers between devices  30.9 us (27%)
  local copies, waits for them, and re-layouts  28.6 us (25%)
  Pallas kernels  13 us (11%)
  other arithmetic  4.58 us (4%)
    ppermute x19, waiting for transfers between devices, swap(): lax.ppermute(value, axis, [(index, index ^ offset) for index in range(lax...  30.9 us
    unnamed x52, local copies, waits for them, and re-layouts  26.3 us
    ppermute x19, starting transfers between devices, swap(): lax.ppermute(value, axis, [(index, index ^ offset) for index in range(lax...  21 us
    all_to_all x3, starting transfers between devices, exchange(): lax.all_to_all(rows.reshape(expert_count, -1, sub_width), 'expert', 0, 0,...  15 us
    concatenate x4, other arithmetic, gather_blocks(): jnp.concatenate([block] + [swap(block, axis, step * span) for step in ran...  4.58 us
    pallas_call x1, Pallas kernels, on_device(): pl.pallas_call(delta_kernel, grid=(steps,), in_specs=[by_rows(sub_width),...  4.19 us
    pallas_call x1, Pallas kernels, on_device(): pl.pallas_call(split_kernel, out_shape=shape((row_count, model_width), bf...  3.25 us
  transfers between devices with their start and end apart: 22, of which 6 were waited for; matrix products, arithmetic and copies ran while one was open for 16% of the time, Pallas kernels for 9%

profile of v1, /device:TPU:0, one launch (start us, length us, event | category | flops | bytes accessed | tf_op | source)
XLA Modules:
  0.0 113.9 jit_solution(11223904722010256973)
XLA Ops:
  0.6 1.5 %constant_dynamic-update-slice_fusion.4 = (bf16[256,1024]{1,0:T(8,128)(2,1)S(1)}, bf16[32,1024]{1,0:T(8,128)(2,1)}) fusion(bf16[128,1024]{1,0:T(8,128)(2,1)} %param.13, s32[]{:T(128)S(6)} %select_n.4), kind=kLoop, calls=%fused_computation.8 | loop fusion | bytes 196612
  2.1 3.0 %collective-permute-start.2 = (bf16[32,1024]{1,0:T(8,128)(2,1)}, bf16[32,1024]{1,0:T(8,128)(2,1)}, u32[]{:S(2)}, u32[]{:S(2)}) collective-permute-start(bf16[32,1024]{1,0:T(8,128)(2,1)} %get-tuple-element.49), channel_id=1, source_target_pairs={{0,8},{4,12},{8,0},{12,4},{16,24},{20,28},{24,16},{28,20},{1,9},{5... | collective-permute-start | bytes 196616 | tf_op jit(solution)/shard_map/ppermute | solution.py:33
  5.2 2.6 %collective-permute-start.3 = (bf16[32,1024]{1,0:T(8,128)(2,1)}, bf16[32,1024]{1,0:T(8,128)(2,1)}, u32[]{:S(2)}, u32[]{:S(2)}) collective-permute-start(bf16[32,1024]{1,0:T(8,128)(2,1)} %get-tuple-element.49), channel_id=1, source_target_pairs={{0,16},{4,20},{8,24},{12,28},{16,0},{20,4},{24,8},{28,12},{1,17},{... | collective-permute-start | bytes 196616 | tf_op jit(solution)/shard_map/ppermute | solution.py:33
  7.7 1.7 %collective-permute-start = (bf16[128,1024]{1,0:T(8,128)(2,1)}, bf16[128,1024]{1,0:T(8,128)(2,1)}, u32[]{:S(2)}, u32[]{:S(2)}) collective-permute-start(bf16[128,1024]{1,0:T(8,128)(2,1)} %bitcast.28), channel_id=1, source_target_pairs={{0,2},{1,3},{2,0},{3,1},{4,6},{5,7},{6,4},{7,5},{8,10},{9,11},{10,... | collective-permute-start | bytes 786440 | tf_op jit(solution)/shard_map/ppermute | solution.py:33
  12.6 5.8 %all-to-all-start = ((bf16[8,128,256]{2,1,0:T(8,128)(2,1)}), bf16[8,128,256]{2,1,0:T(8,128)(2,1)S(1)}, u32[]{:S(2)}, u32[]{:S(2)}) async-start(bf16[8,128,256]{2,1,0:T(8,128)(2,1)} %bitcast.2), calls=%async_computation | async-start | bytes 1048576 | tf_op jit(solution)/shard_map/all_to_all | solution.py:298
  18.4 1.5 %constant_dynamic-update-slice_fusion.15 = (bf16[512,1024]{1,0:T(8,128)(2,1)}, bf16[32,1024]{1,0:T(8,128)(2,1)}) fusion(bf16[128,1024]{1,0:T(8,128)(2,1)} %param.14, s32[]{:T(128)S(6)} %select_n.4), kind=kLoop, calls=%fused_computation.19 | loop fusion | bytes 196612
  19.9 2.0 %collective-permute-start.9 = (bf16[32,1024]{1,0:T(8,128)(2,1)}, bf16[32,1024]{1,0:T(8,128)(2,1)}, u32[]{:S(2)}, u32[]{:S(2)}) collective-permute-start(bf16[32,1024]{1,0:T(8,128)(2,1)} %get-tuple-element.47), channel_id=1, source_target_pairs={{0,8},{4,12},{8,0},{12,4},{16,24},{20,28},{24,16},{28,20},{1,9},{5... | collective-permute-start | bytes 196616 | tf_op jit(solution)/shard_map/ppermute | solution.py:33
  21.9 1.5 %constant_dynamic-update-slice_fusion.9 = (bf16[256,1024]{1,0:T(8,128)(2,1)}, bf16[1024,1024]{1,0:T(8,128)(2,1)S(1)}) fusion(bf16[32,1024]{1,0:T(8,128)(2,1)} %get-tuple-element.47), kind=kLoop, calls=%fused_computation.13 | loop fusion | bytes 196608
  23.6 2.4 %collective-permute-start.10 = (bf16[32,1024]{1,0:T(8,128)(2,1)}, bf16[32,1024]{1,0:T(8,128)(2,1)S(1)}, u32[]{:S(2)}, u32[]{:S(2)}) collective-permute-start(bf16[32,1024]{1,0:T(8,128)(2,1)} %get-tuple-element.47), channel_id=1, source_target_pairs={{0,16},{4,20},{8,24},{12,28},{16,0},{20,4},{24,8},{28,12},{1,17},{... | collective-permute-start | bytes 196616 | tf_op jit(solution)/shard_map/ppermute | solution.py:33
  27.0 2.0 %collective-permute-start.5 = (bf16[128,1024]{1,0:T(8,128)(2,1)S(1)}, bf16[128,1024]{1,0:T(8,128)(2,1)S(1)}, u32[]{:S(2)}, u32[]{:S(2)}) collective-permute-start(bf16[128,1024]{1,0:T(8,128)(2,1)S(1)} %pad_maximum_fusion.2), channel_id=1, source_target_pairs={{0,4},{4,0},{8,12},{12,8},{16,20},{20,16},{24,28},{28,24},{1,5},{5... | collective-permute-start | bytes 786440 | tf_op jit(solution)/shard_map/ppermute | solution.py:33
  29.0 7.6 %collective-permute-done.10 = bf16[32,1024]{1,0:T(8,128)(2,1)S(1)} collective-permute-done((bf16[32,1024]{1,0:T(8,128)(2,1)}, bf16[32,1024]{1,0:T(8,128)(2,1)S(1)}, u32[]{:S(2)}, u32[]{:S(2)}) %collective-permute-start.10) | collective-permute-done | bytes 65568 | tf_op jit(solution)/shard_map/ppermute | solution.py:33
  36.7 1.6 %pad_maximum_fusion.3 = bf16[128,1024]{1,0:T(8,128)(2,1)} fusion(bf16[32,1024]{1,0:T(8,128)(2,1)S(1)} %collective-permute-done.11, bf16[32,1024]{1,0:T(8,128)(2,1)S(1)} %collective-permute-done.10, bf16[32,1024]{1,0:T(8,128)(2,1)} %collective-permute-done.9, bf16[32,1024]{1,0:T(8,128)(2,1)} %get-tuple-element.47), kind=kLoop, calls=%fused_computation.3 | loop fusion | flops 1048576 | bytes 524288 | tf_op jit(solution)/shard_map/concatenate | solution.py:52
  38.3 1.5 %collective-permute-start.12 = (bf16[128,1024]{1,0:T(8,128)(2,1)}, bf16[128,1024]{1,0:T(8,128)(2,1)}, u32[]{:S(2)}, u32[]{:S(2)}) collective-permute-start(bf16[128,1024]{1,0:T(8,128)(2,1)} %pad_maximum_fusion.3), channel_id=1, source_target_pairs={{0,4},{4,0},{8,12},{12,8},{16,20},{20,16},{24,28},{28,24},{1,5},{5... | collective-permute-start | bytes 786440 | tf_op jit(solution)/shard_map/ppermute | solution.py:33
  43.4 1.5 %constant_dynamic-update-slice_fusion.14 = (bf16[512,1024]{1,0:T(8,128)(2,1)}, bf16[1024,1024]{1,0:T(8,128)(2,1)S(1)}, bf16[256,1024]{1,0:T(8,128)(2,1)}) fusion(bf16[512,1024]{1,0:T(8,128)(2,1)} %get-tuple-element.46, bf16[32,1024]{1,0:T(8,128)(2,1)} %collective-permute-done.9, bf16[1024,1024]{1,0:T(8,128)(2,1)S(1)} %get-tuple-element.65, ...), kind=kLoop, calls=%fused_computation.18 | loop fusion | bytes 262144
  49.4 2.1 %collective-permute-done.6.refs_3_ = bf16[128,256]{1,0:T(8,128)(2,1)S(1)} collective-permute-done((bf16[128,256]{1,0:T(8,128)(2,1)S(1)}, bf16[128,256]{1,0:T(8,128)(2,1)S(1)}, u32[]{:S(2)}, u32[]{:S(2)}) %collective-permute-start.6) | collective-permute-done | bytes 65568 | tf_op jit(solution)/shard_map/ppermute | solution.py:33
  53.7 3.5 %all-to-all-start.1 = ((bf16[8,128,256]{2,1,0:T(8,128)(2,1)}), bf16[8,128,256]{2,1,0:T(8,128)(2,1)S(1)}, u32[]{:S(2)}, u32[]{:S(2)}) async-start(bf16[8,128,256]{2,1,0:T(8,128)(2,1)} %bitcast.21), calls=%async_computation.1 | async-start | bytes 1048576 | tf_op jit(solution)/shard_map/all_to_all | solution.py:298
  57.9 1.8 %constant_dynamic-update-slice_fusion.11 = (bf16[512,1024]{1,0:T(8,128)(2,1)}, bf16[1024,1024]{1,0:T(8,128)(2,1)S(1)}, bf16[256,1024]{1,0:T(8,128)(2,1)}) fusion(bf16[512,1024]{1,0:T(8,128)(2,1)} %get-tuple-element.55, bf16[128,1024]{1,0:T(8,128)(2,1)} %collective-permute-done.12, bf16[1024,1024]{1,0:T(8,128)(2,1)S(1)} %get-tuple-element.56, ...), kind=kLoop, calls=%fused_computation.15 | loop fusion | bytes 1048576
  60.5 13.5 %collective-permute-done.13 = bf16[256,1024]{1,0:T(8,128)(2,1)S(1)} collective-permute-done((bf16[256,1024]{1,0:T(8,128)(2,1)}, bf16[256,1024]{1,0:T(8,128)(2,1)S(1)}, u32[]{:S(2)}, u32[]{:S(2)}) %collective-permute-start.13) | collective-permute-done | bytes 524320 | tf_op jit(solution)/shard_map/ppermute | solution.py:33
  81.6 4.2 %shard_map.123 = (bf16[1024,256]{1,0:T(8,128)(2,1)S(1)}, bf16[1024,1536]{1,0:T(8,128)(2,1)S(1)}, bf16[1024,768]{1,0:T(8,128)(2,1)S(1)}) custom-call(bf16[1024,256]{1,0:T(8,128)(2,1)S(1)} %bitcast.16, bf16[1024,256]{1,0:T(8,128)(2,1)S(1)} %bitcast.18, bf16[256,768]{1,0:T(8,128)(2,1)S(1)} %bitcast.24, bf16[256,768]{1,0:T(8,128)(2,1)S(1)} %bitcast.25, ...), custom_call_target="tpu_custom_call" | custom-call | flops 2013265920 | bytes 6291456 | tf_op jit(solution)/shard_map/pallas_call | solution.py:345
  87.8 5.6 %all-to-all-start.2 = ((bf16[8,128,256]{2,1,0:T(8,128)(2,1)}), bf16[8,128,256]{2,1,0:T(8,128)(2,1)}, u32[]{:S(2)}, u32[]{:S(2)}) async-start(bf16[8,128,256]{2,1,0:T(8,128)(2,1)} %bitcast.20), calls=%async_computation.2 | async-start | bytes 1048576 | tf_op jit(solution)/shard_map/all_to_all | solution.py:298
  96.9 1.6 %shard_map.126 = (f32[2,64,1536]{2,1,0:T(8,128)S(1)}, f32[2,192,256]{2,1,0:T(8,128)S(1)}, bf16[2,64,1536]{2,1,0:T(8,128)(2,1)S(1)}, bf16[2,192,256]{2,1,0:T(8,128)(2,1)S(1)}) custom-call(bf16[1024,256]{1,0:T(8,128)(2,1)S(1)} %bitcast.17, bf16[1024,256]{1,0:T(8,128)(2,1)S(1)} %bitcast.19, bf16[1024,1536]{1,0:T(8,128)(2,1)S(1)} %get-tuple-element.33.refs_2_, ...), custom_call_target="tpu_custom_call" | custom-call | flops 1207959552 | bytes 6291456 | tf_op jit(solution)/shard_map/pallas_call | solution.py:372
  99.1 1.5 %collective-permute-done.16.got_b = bf16[2,192,256]{2,1,0:T(8,128)(2,1)S(1)} collective-permute-done((bf16[2,192,256]{2,1,0:T(8,128)(2,1)S(1)}, bf16[2,192,256]{2,1,0:T(8,128)(2,1)S(1)}, u32[]{:S(2)}, u32[]{:S(2)}) %collective-permute-start.16) | collective-permute-done | bytes 196640 | tf_op jit(solution)/shard_map/ppermute | solution.py:33
  104.2 5.5 %collective-permute-done.18.got_b = bf16[1,192,256]{2,1,0:T(8,128)(2,1)S(1)} collective-permute-done((bf16[1,192,256]{2,1,0:T(8,128)(2,1)S(1)}, bf16[1,192,256]{2,1,0:T(8,128)(2,1)S(1)}, u32[]{:S(2)}, u32[]{:S(2)}) %collective-permute-start.18) | collective-permute-done | bytes 98336 | tf_op jit(solution)/shard_map/ppermute | solution.py:33
  110.6 3.3 %shard_map.125 = bf16[128,1024]{1,0:T(8,128)(2,1)} custom-call(s32[128,4]{1,0:T(8,128)S(1)} %get-tuple-element.25.down_ref, bf16[1024,256]{1,0:T(8,128)(2,1)} %bitcast.12.back_ref, bf16[1024,1024]{1,0:T(8,128)(2,1)S(1)} %shard_map.124.weight_ref), custom_call_target="tpu_custom_call" | custom-call | tf_op jit(solution)/shard_map/pallas_call | solution.py:425
  (89 shorter events, 34.1 us)
Async XLA Ops:
  0.6 22.8 %copy-start.19 = (f32[2,64,4]{1,2,0:T(4,128)S(1)}, f32[2,64,4]{1,2,0:T(4,128)}, u32[]{:S(2)}) copy-start(f32[2,64,4]{1,2,0:T(4,128)} %param.12) | copy-start | bytes 6148
  2.1 21.4 %collective-permute-start.2 = (bf16[32,1024]{1,0:T(8,128)(2,1)}, bf16[32,1024]{1,0:T(8,128)(2,1)}, u32[]{:S(2)}, u32[]{:S(2)}) collective-permute-start(bf16[32,1024]{1,0:T(8,128)(2,1)} %get-tuple-element.49), channel_id=1, source_target_pairs={{0,8},{4,12},{8,0},{12,4},{16,24},{20,28},{24,16},{28,20},{1,9},{5... | collective-permute-start | bytes 196616 | tf_op jit(solution)/shard_map/ppermute | solution.py:33
  5.2 20.8 %collective-permute-start.3 = (bf16[32,1024]{1,0:T(8,128)(2,1)}, bf16[32,1024]{1,0:T(8,128)(2,1)}, u32[]{:S(2)}, u32[]{:S(2)}) collective-permute-start(bf16[32,1024]{1,0:T(8,128)(2,1)} %get-tuple-element.49), channel_id=1, source_target_pairs={{0,16},{4,20},{8,24},{12,28},{16,0},{20,4},{24,8},{28,12},{1,17},{... | collective-permute-start | bytes 196616 | tf_op jit(solution)/shard_map/ppermute | solution.py:33
  7.7 18.3 %collective-permute-start.4 = (bf16[32,1024]{1,0:T(8,128)(2,1)}, bf16[32,1024]{1,0:T(8,128)(2,1)}, u32[]{:S(2)}, u32[]{:S(2)}) collective-permute-start(bf16[32,1024]{1,0:T(8,128)(2,1)} %get-tuple-element.49), channel_id=1, source_target_pairs={{0,24},{4,28},{8,16},{12,20},{16,8},{20,12},{24,0},{28,4},{1,25},{... | collective-permute-start | bytes 196616 | tf_op jit(solution)/shard_map/ppermute | solution.py:33
  7.7 32.0 %collective-permute-start = (bf16[128,1024]{1,0:T(8,128)(2,1)}, bf16[128,1024]{1,0:T(8,128)(2,1)}, u32[]{:S(2)}, u32[]{:S(2)}) collective-permute-start(bf16[128,1024]{1,0:T(8,128)(2,1)} %bitcast.28), channel_id=1, source_target_pairs={{0,2},{1,3},{2,0},{3,1},{4,6},{5,7},{6,4},{7,5},{8,10},{9,11},{10,... | collective-permute-start | bytes 786440 | tf_op jit(solution)/shard_map/ppermute | solution.py:33
  11.2 28.6 %copy-start.16 = (bf16[2,64,1024]{2,1,0:T(8,128)(2,1)S(1)}, bf16[2,64,1024]{2,1,0:T(8,128)(2,1)}, u32[]{:S(2)}) copy-start(bf16[2,64,1024]{2,1,0:T(8,128)(2,1)} %param.9) | copy-start | bytes 786436
  12.6 41.2 %all-to-all-start = ((bf16[8,128,256]{2,1,0:T(8,128)(2,1)}), bf16[8,128,256]{2,1,0:T(8,128)(2,1)S(1)}, u32[]{:S(2)}, u32[]{:S(2)}) async-start(bf16[8,128,256]{2,1,0:T(8,128)(2,1)} %bitcast.2), calls=%async_computation | async-start | bytes 1048576 | tf_op jit(solution)/shard_map/all_to_all | solution.py:298
  19.9 9.1 %collective-permute-start.9 = (bf16[32,1024]{1,0:T(8,128)(2,1)}, bf16[32,1024]{1,0:T(8,128)(2,1)}, u32[]{:S(2)}, u32[]{:S(2)}) collective-permute-start(bf16[32,1024]{1,0:T(8,128)(2,1)} %get-tuple-element.47), channel_id=1, source_target_pairs={{0,8},{4,12},{8,0},{12,4},{16,24},{20,28},{24,16},{28,20},{1,9},{5... | collective-permute-start | bytes 196616 | tf_op jit(solution)/shard_map/ppermute | solution.py:33
  23.6 13.1 %collective-permute-start.10 = (bf16[32,1024]{1,0:T(8,128)(2,1)}, bf16[32,1024]{1,0:T(8,128)(2,1)S(1)}, u32[]{:S(2)}, u32[]{:S(2)}) collective-permute-start(bf16[32,1024]{1,0:T(8,128)(2,1)} %get-tuple-element.47), channel_id=1, source_target_pairs={{0,16},{4,20},{8,24},{12,28},{16,0},{20,4},{24,8},{28,12},{1,17},{... | collective-permute-start | bytes 196616 | tf_op jit(solution)/shard_map/ppermute | solution.py:33
  26.0 10.7 %collective-permute-start.11 = (bf16[32,1024]{1,0:T(8,128)(2,1)}, bf16[32,1024]{1,0:T(8,128)(2,1)S(1)}, u32[]{:S(2)}, u32[]{:S(2)}) collective-permute-start(bf16[32,1024]{1,0:T(8,128)(2,1)} %get-tuple-element.47), channel_id=1, source_target_pairs={{0,24},{4,28},{8,16},{12,20},{16,8},{20,12},{24,0},{28,4},{1,25},{... | collective-permute-start | bytes 196616 | tf_op jit(solution)/shard_map/ppermute | solution.py:33
  27.0 17.9 %collective-permute-start.5 = (bf16[128,1024]{1,0:T(8,128)(2,1)S(1)}, bf16[128,1024]{1,0:T(8,128)(2,1)S(1)}, u32[]{:S(2)}, u32[]{:S(2)}) collective-permute-start(bf16[128,1024]{1,0:T(8,128)(2,1)S(1)} %pad_maximum_fusion.2), channel_id=1, source_target_pairs={{0,4},{4,0},{8,12},{12,8},{16,20},{20,16},{24,28},{28,24},{1,5},{5... | collective-permute-start | bytes 786440 | tf_op jit(solution)/shard_map/ppermute | solution.py:33
  38.3 19.6 %collective-permute-start.12 = (bf16[128,1024]{1,0:T(8,128)(2,1)}, bf16[128,1024]{1,0:T(8,128)(2,1)}, u32[]{:S(2)}, u32[]{:S(2)}) collective-permute-start(bf16[128,1024]{1,0:T(8,128)(2,1)} %pad_maximum_fusion.3), channel_id=1, source_target_pairs={{0,4},{4,0},{8,12},{12,8},{16,20},{20,16},{24,28},{28,24},{1,5},{5... | collective-permute-start | bytes 786440 | tf_op jit(solution)/shard_map/ppermute | solution.py:33
  40.8 4.1 %collective-permute-start.1 = (bf16[256,1024]{1,0:T(8,128)(2,1)S(1)}, bf16[256,1024]{1,0:T(8,128)(2,1)S(1)}, u32[]{:S(2)}, u32[]{:S(2)}) collective-permute-start(bf16[256,1024]{1,0:T(8,128)(2,1)S(1)} %pad_maximum_fusion.1), channel_id=1, source_target_pairs={{0,1},{1,0},{2,3},{3,2},{4,5},{5,4},{6,7},{7,6},{8,9},{9,8},{10,11... | collective-permute-start | bytes 1572872 | tf_op jit(solution)/shard_map/ppermute | solution.py:33
  46.5 5.0 %collective-permute-start.6 = (bf16[128,256]{1,0:T(8,128)(2,1)S(1)}, bf16[128,256]{1,0:T(8,128)(2,1)S(1)}, u32[]{:S(2)}, u32[]{:S(2)}) collective-permute-start(bf16[128,256]{1,0:T(8,128)(2,1)S(1)} %get-tuple-element.29), channel_id=1, source_target_pairs={{0,2},{1,3},{2,0},{3,1},{4,6},{5,7},{6,4},{7,5},{8,10},{9,11},{10,... | collective-permute-start | bytes 196616 | tf_op jit(solution)/shard_map/ppermute | solution.py:33
  47.1 4.4 %collective-permute-start.7 = (bf16[128,256]{1,0:T(8,128)(2,1)S(1)}, bf16[128,256]{1,0:T(8,128)(2,1)S(1)}, u32[]{:S(2)}, u32[]{:S(2)}) collective-permute-start(bf16[128,256]{1,0:T(8,128)(2,1)S(1)} %get-tuple-element.30), channel_id=1, source_target_pairs={{0,1},{1,0},{2,3},{3,2},{4,5},{5,4},{6,7},{7,6},{8,9},{9,8},{10,11... | collective-permute-start | bytes 196616 | tf_op jit(solution)/shard_map/ppermute | solution.py:33
  47.3 4.8 %collective-permute-start.8 = (bf16[128,256]{1,0:T(8,128)(2,1)S(1)}, bf16[128,256]{1,0:T(8,128)(2,1)S(1)}, u32[]{:S(2)}, u32[]{:S(2)}) collective-permute-start(bf16[128,256]{1,0:T(8,128)(2,1)S(1)} %get-tuple-element.31), channel_id=1, source_target_pairs={{0,3},{1,2},{2,1},{3,0},{4,7},{5,6},{6,5},{7,4},{8,11},{9,10},{10,... | collective-permute-start | bytes 196616 | tf_op jit(solution)/shard_map/ppermute | solution.py:33
  53.7 21.2 %all-to-all-start.1 = ((bf16[8,128,256]{2,1,0:T(8,128)(2,1)}), bf16[8,128,256]{2,1,0:T(8,128)(2,1)S(1)}, u32[]{:S(2)}, u32[]{:S(2)}) async-start(bf16[8,128,256]{2,1,0:T(8,128)(2,1)} %bitcast.21), calls=%async_computation.1 | async-start | bytes 1048576 | tf_op jit(solution)/shard_map/all_to_all | solution.py:298
  59.8 14.3 %collective-permute-start.13 = (bf16[256,1024]{1,0:T(8,128)(2,1)}, bf16[256,1024]{1,0:T(8,128)(2,1)S(1)}, u32[]{:S(2)}, u32[]{:S(2)}) collective-permute-start(bf16[256,1024]{1,0:T(8,128)(2,1)} %get-tuple-element.54), channel_id=1, source_target_pairs={{0,2},{1,3},{2,0},{3,1},{4,6},{5,7},{6,4},{7,5},{8,10},{9,11},{10,... | collective-permute-start | bytes 1572872 | tf_op jit(solution)/shard_map/ppermute | solution.py:33
  75.0 27.8 %collective-permute-start.14 = (bf16[512,1024]{1,0:T(8,128)(2,1)}, bf16[512,1024]{1,0:T(8,128)(2,1)}, u32[]{:S(2)}, u32[]{:S(2)}) collective-permute-start(bf16[512,1024]{1,0:T(8,128)(2,1)} %get-tuple-element.50), channel_id=1, source_target_pairs={{0,1},{1,0},{2,3},{3,2},{4,5},{5,4},{6,7},{7,6},{8,9},{9,8},{10,11... | collective-permute-start | bytes 3145736 | tf_op jit(solution)/shard_map/ppermute | solution.py:33
  87.8 22.9 %all-to-all-start.2 = ((bf16[8,128,256]{2,1,0:T(8,128)(2,1)}), bf16[8,128,256]{2,1,0:T(8,128)(2,1)}, u32[]{:S(2)}, u32[]{:S(2)}) async-start(bf16[8,128,256]{2,1,0:T(8,128)(2,1)} %bitcast.20), calls=%async_computation.2 | async-start | bytes 1048576 | tf_op jit(solution)/shard_map/all_to_all | solution.py:298
  98.5 2.1 %collective-permute-start.15 = (bf16[2,64,1536]{2,1,0:T(8,128)(2,1)S(1)}, bf16[2,64,1536]{2,1,0:T(8,128)(2,1)S(1)}, u32[]{:S(2)}, u32[]{:S(2)}) collective-permute-start(bf16[2,64,1536]{2,1,0:T(8,128)(2,1)S(1)} %get-tuple-element.37), channel_id=1, source_target_pairs={{0,1},{1,0},{2,3},{3,2},{4,5},{5,4},{6,7},{7,6},{8,9},{9,8},{10,11... | collective-permute-start | bytes 1179656 | tf_op jit(solution)/shard_map/ppermute | solution.py:33
  98.6 2.0 %collective-permute-start.16 = (bf16[2,192,256]{2,1,0:T(8,128)(2,1)S(1)}, bf16[2,192,256]{2,1,0:T(8,128)(2,1)S(1)}, u32[]{:S(2)}, u32[]{:S(2)}) collective-permute-start(bf16[2,192,256]{2,1,0:T(8,128)(2,1)S(1)} %get-tuple-element.38), channel_id=1, source_target_pairs={{0,1},{1,0},{2,3},{3,2},{4,5},{5,4},{6,7},{7,6},{8,9},{9,8},{10,11... | collective-permute-start | bytes 589832 | tf_op jit(solution)/shard_map/ppermute | solution.py:33
  100.7 9.1 %collective-permute-start.17 = (bf16[1,64,1536]{2,1,0:T(8,128)(2,1)S(1)}, bf16[1,64,1536]{2,1,0:T(8,128)(2,1)S(1)}, u32[]{:S(2)}, u32[]{:S(2)}) collective-permute-start(bf16[1,64,1536]{2,1,0:T(8,128)(2,1)S(1)} %get-tuple-element.41), channel_id=1, source_target_pairs={{0,2},{1,3},{2,0},{3,1},{4,6},{5,7},{6,4},{7,5},{8,10},{9,11},{10,... | collective-permute-start | bytes 589832 | tf_op jit(solution)/shard_map/ppermute | solution.py:33
  101.4 8.3 %collective-permute-start.18 = (bf16[1,192,256]{2,1,0:T(8,128)(2,1)S(1)}, bf16[1,192,256]{2,1,0:T(8,128)(2,1)S(1)}, u32[]{:S(2)}, u32[]{:S(2)}) collective-permute-start(bf16[1,192,256]{2,1,0:T(8,128)(2,1)S(1)} %get-tuple-element.42), channel_id=1, source_target_pairs={{0,2},{1,3},{2,0},{3,1},{4,6},{5,7},{6,4},{7,5},{8,10},{9,11},{10,... | collective-permute-start | bytes 294920 | tf_op jit(solution)/shard_map/ppermute | solution.py:33
  (18 other events, 62.7 us)

commit v2 on v1

--- a/solution.py
+++ b/solution.py
@@ -6,7 +6,8 @@
 from jax.sharding import PartitionSpec as P
 
 LANES = 128
-VMEM_BYTES = 40 * 1024 * 1024
+MERGE_COST = 5000000000
+VMEM_BYTES = 16 * 1024 * 1024
 
 
 def transposed(left_rows, right_rows):
@@ -39,24 +40,65 @@
     return pltpu.CompilerParams(vmem_limit_bytes=VMEM_BYTES)
 
 
+def in_hbm(*arrays):
+    return [pltpu.with_memory_space_constraint(array, pltpu.HBM) for array in arrays]
+
+
+def in_vmem(*arrays):
+    return [pltpu.with_memory_space_constraint(array, pltpu.VMEM) for array in arrays]
+
+
+def after(value, *earlier):
+    return lax.optimization_barrier((value, *earlier))[0]
+
+
 def cost(flops, moved):
     return pl.CostEstimate(flops=flops, bytes_accessed=moved, transcendentals=0)
 
 
-def gather_blocks(block, axis):
+def gather_blocks(block, axis, *gate):
     span = lax.axis_size(axis)
-    offsets = [0]
+    blocks, offsets = [block], [0]
     while span > 1:
-        radix = 4 if span % 4 == 0 and axis == "expert" else 2
+        radix = 4 if span % 4 == 0 else 2
         span //= radix
-        block = jnp.concatenate(
-            [block] + [swap(block, axis, step * span) for step in range(1, radix)]
-        )
-        offsets = [old ^ (step * span) for step in range(radix) for old in offsets]
-    return block, offsets
-
-
-def route_kernel(batch_count, slots_per, key_count, ids_ref, rows_ref, send_ref, across_ref, down_ref):
+        block = jnp.concatenate(blocks) if len(blocks) > 1 else blocks[0]
+        if span == 1 and gate:
+            block = after(block, *gate)
+        steps = [step * span for step in range(1, radix)]
+        blocks = [block] + [swap(block, axis, step) for step in steps]
+        offsets = offsets + [old ^ step for step in steps for old in offsets]
+    return blocks, offsets
+
+
+def gather_parts(block, axis):
+    span = lax.axis_size(axis)
+    blocks, offsets = [block], [0]
+    while span > 1:
+        span //= 2
+        blocks = blocks + [swap(old, axis, span) for old in blocks]
+        offsets = offsets + [old ^ span for old in offsets]
+    return blocks, offsets
+
+
+def place_rows(offsets, count, block_refs, out_ref):
+    here = lax.axis_index("expert")
+    held = [(ref, row) for ref in block_refs for row in range(0, ref.shape[0], count)]
+    for offset, (ref, row) in zip(offsets, held):
+        start = pl.multiple_of((here ^ offset) * count, count)
+        out_ref[pl.ds(start, count), :] = ref[row : row + count, :]
+
+
+def route_kernel(
+    batch_count, slots_per, key_count, ids_ref, rows_ref, weight_refs, send_ref, across_ref, down_ref, block_refs, sems
+):
+    here = lax.axis_index("dp")
+    copies = []
+    for number, (weight_ref, block_ref) in enumerate(zip(weight_refs, block_refs)):
+        count = block_ref.shape[0]
+        own = weight_ref.at[pl.ds(pl.multiple_of(here * count, count), count), :]
+        copies.append(pltpu.make_async_copy(own, block_ref, sems.at[number]))
+        copies[-1].start()
     head_count, row_count = ids_ref.shape
     width = rows_ref.shape[1] // head_count
     lane = lax.broadcasted_iota(jnp.int32, (1, row_count), 1)
@@ -86,6 +128,8 @@
     )
     across_ref[...] = across
     down_ref[...] = across.astype(jnp.float32).T.astype(jnp.int32)
+    for copy in copies:
+        copy.wait()
 
 
 def scatter_rows(target, row_list, slot_count):
@@ -96,18 +140,10 @@
     ).astype(jnp.bfloat16)
 
 
-def merge_kernel(offsets, block_rows, token_ref, weight_ref, *rest):
-    out_refs, held = rest[:-1], rest[-1]
-    here = lax.axis_index("expert")
-    for place, offset in enumerate(offsets):
-        start = pl.multiple_of((here ^ offset) * block_rows, block_rows)
-        held[pl.ds(start, block_rows), :] = weight_ref[
-            place * block_rows : (place + 1) * block_rows, :
-        ]
-    count = out_refs[0].shape[0]
-    result = transposed(token_ref[...], held[...]).astype(jnp.bfloat16)
-    for number, out_ref in enumerate(out_refs):
-        out_ref[...] = result[number * count : (number + 1) * count]
+def merge_kernel(offsets, count, token_refs, weight_refs, out_refs, held):
+    place_rows(offsets, count, weight_refs, held)
+    for token_ref, out_ref in zip(token_refs, out_refs):
+        out_ref[...] = transposed(token_ref[...], held[...]).astype(jnp.bfloat16)
 
 
 def assemble(offsets, part_refs, width):
@@ -149,31 +185,134 @@
     send_ref[...] = scatter_rows(target, rows, send_ref.shape[0])
 
 
-def delta_kernel(input_ref, grad_ref, gate_ref, up_ref, down_ref, delta_ref, both_ref, hidden_ref):
-    inputs = input_ref[...]
+def chunks(count, chunk):
+    return [slice(start, start + chunk) for start in range(0, count, chunk)]
+
+
+def fetch(source_ref, held_ref, sems, rows):
+    copies = [
+        pltpu.make_async_copy(source_ref.at[part, :], held_ref.at[part, :], sems.at[number])
+        for number, part in enumerate(rows)
+    ]
+    for copy in copies:
+        copy.start()
+    return copies
+
+
+def send_out(source_ref, target_ref, part, sem):
+    copy = pltpu.make_async_copy(source_ref.at[part, :], target_ref.at[part, :], sem)
+    copy.start()
+    return copy
+
+
+def forward_kernel(
+    rows, input_ref, gate_ref, up_ref, inputs_out, hidden_out, slope_out, activation_out,
+    inputs_held, gate_held, up_held, hidden, slope, activation_held, sems, weight_sems, out_sems
+):
+    copies = fetch(input_ref, inputs_held, sems, rows)
+    weights = [
+        pltpu.make_async_copy(gate_ref, gate_held, weight_sems.at[0]),
+        pltpu.make_async_copy(up_ref, up_held, weight_sems.at[1]),
+    ]
+    for copy in weights:
+        copy.start()
+    for copy in weights:
+        copy.wait()
+    outs = []
+    for number, (part, copy) in enumerate(zip(rows, copies)):
+        copy.wait()
+        inputs = inputs_held[part, :]
+        pre_gate = plain(inputs, gate_held[...])
+        pre_up = plain(inputs, up_held[...])
+        sigma = jax.nn.sigmoid(pre_gate)
+        activation = pre_gate * sigma
+        slope_value = sigma * (1.0 + pre_gate * (1.0 - sigma))
+        hidden[part, :] = (activation * pre_up).astype(jnp.bfloat16)
+        slope[part, :] = (pre_up * slope_value).astype(jnp.bfloat16)
+        activation_held[part, :] = activation.astype(jnp.bfloat16)
+        for place, (source, target) in enumerate(
+            (
+                (inputs_held, inputs_out),
+                (hidden, hidden_out),
+                (slope, slope_out),
+                (activation_held, activation_out),
+            )
+        ):
+            outs.append(send_out(source, target, part, out_sems.at[place, number]))
+    for copy in outs:
+        copy.wait()
+
+
+def delta_kernel(
+    rows, grad_ref, slope_ref, activation_ref, gate_ref, up_ref, down_ref,
+    both_ref, delta_ref, grads_out,
+    slope, activation, gate_held, up_held, down_held, out, sems, weight_sems, out_sems
+):
     hidden_width = gate_ref.shape[1]
-    pre_gate = plain(inputs, gate_ref[...])
-    pre_up = plain(inputs, up_ref[...])
-    d_hidden = transposed(grad_ref[...], down_ref[...])
-    sigma = jax.nn.sigmoid(pre_gate)
-    activation = pre_gate * sigma
-    slope_value = sigma * (1.0 + pre_gate * (1.0 - sigma))
-    hidden_ref[...] = (activation * pre_up).astype(jnp.bfloat16)
-    delta_gate = (d_hidden * pre_up * slope_value).astype(jnp.bfloat16)
-    delta_up = (d_hidden * activation).astype(jnp.bfloat16)
-    both_ref[:, :hidden_width] = delta_gate
-    both_ref[:, hidden_width:] = delta_up
-    delta_ref[...] = (
-        transposed(delta_gate, gate_ref[...]) + transposed(delta_up, up_ref[...])
-    ).astype(jnp.bfloat16)
+    weights = [
+        pltpu.make_async_copy(source, target, weight_sems.at[number])
+        for number, (source, target) in enumerate(
+            ((down_ref, down_held), (gate_ref, gate_held), (up_ref, up_held))
+        )
+    ]
+    copies = []
+    weights[0].start()
+    for number, part in enumerate(rows):
+        copies.append(
+            [
+                send_out(source, target, part, sems.at[place, number])
+                for place, (source, target) in enumerate(
+                    ((slope_ref, slope), (activation_ref, activation))
+                )
+            ]
+        )
+        if number == 0:
+            weights[1].start()
+            weights[2].start()
+    weights[0].wait()
+    outs = []
+    for number, (part, arrived) in enumerate(zip(rows, copies)):
+        d_hidden = transposed(grad_ref[part, :], down_held[...])
+        arrived[0].wait()
+        arrived[1].wait()
+        delta_gate = (d_hidden * slope[part, :].astype(jnp.float32)).astype(jnp.bfloat16)
+        delta_up = (d_hidden * activation[part, :].astype(jnp.float32)).astype(jnp.bfloat16)
+        both_ref[part, :hidden_width] = delta_gate
+        both_ref[part, hidden_width:] = delta_up
+        if number == 0:
+            weights[1].wait()
+            weights[2].wait()
+        out[part, :] = (
+            transposed(delta_gate, gate_held[...]) + transposed(delta_up, up_held[...])
+        ).astype(jnp.bfloat16)
+        outs.append(send_out(out, delta_ref, part, out_sems.at[0, number]))
+        outs.append(send_out(grad_ref, grads_out, part, out_sems.at[1, number]))
+    for copy in outs:
+        copy.wait()
 
 
 def weight_kernel(
-    group, input_ref, grad_ref, both_ref, hidden_ref, keep_a, keep_b, send_a, send_b, held_a, held_b
+    group, input_ref, grad_ref, both_ref, hidden_ref, keep_a, keep_b, send_a, send_b,
+    inputs_held, grads_held, hidden_held, held_a, held_b, sems
 ):
     here = lax.axis_index("dp")
-    held_a[...] = leading(input_ref[...], both_ref[...])
-    held_b[...] = leading(hidden_ref[...], grad_ref[...])
+    copies = [
+        pltpu.make_async_copy(source, target, sems.at[number])
+        for number, (source, target) in enumerate(
+            ((input_ref, inputs_held), (grad_ref, grads_held), (hidden_ref, hidden_held))
+        )
+    ]
+    for copy in copies:
+        copy.start()
+    copies[0].wait()
+    held_a[...] = leading(inputs_held[...], both_ref[...])
+    copies[1].wait()
+    copies[2].wait()
+    held_b[...] = leading(hidden_held[...], grads_held[...])
+    give_weights(group, here, held_a, held_b, keep_a, keep_b, send_a, send_b)
+
+
+def give_weights(group, here, held_a, held_b, keep_a, keep_b, send_a, send_b):
     for held, keep, send in ((held_a, keep_a, send_a), (held_b, keep_b, send_b)):
         rows = held.shape[0] // group
         for place in range(group // 2):
@@ -204,21 +343,20 @@
     down_ref[0] = keep_b[0] + got_b[0].astype(jnp.float32)
 
 
-def order_kernel(dp_offsets, offsets, block_rows, weight_ref, out_ref):
-    here, group = lax.axis_index("expert"), lax.axis_index("dp")
-    place = 0
-    for dp_offset in dp_offsets:
-        for offset in offsets:
-            start = ((here ^ offset) * len(dp_offsets) + (group ^ dp_offset)) * block_rows
-            out_ref[pl.ds(pl.multiple_of(start, block_rows), block_rows), :] = weight_ref[
-                place * block_rows : (place + 1) * block_rows, :
+def interleave_kernel(offsets, count, part_refs, out_ref):
+    here = lax.axis_index("dp")
+    for offset, part_ref in zip(offsets, part_refs):
+        for place in range(part_ref.shape[0] // count):
+            start = (place * len(offsets) + (here ^ offset)) * count
+            out_ref[pl.ds(pl.multiple_of(start, count), count), :] = part_ref[
+                place * count : (place + 1) * count, :
             ]
-            place += 1
-
-
-def split_kernel(down_ref, back_ref, weight_ref, out_ref):
+
+
+def split_kernel(down_ref, back_ref, weight_ref, out_ref, back, held, sems):
     row_count, head_count = down_ref.shape
     slot_count, width = back_ref.shape
+    (copy,) = fetch(back_ref, back, sems, [slice(0, slot_count)])
     lane = lax.broadcasted_iota(jnp.int32, (row_count, slot_count), 1)
     picked = jnp.concatenate(
         [
@@ -227,11 +365,11 @@
         ],
         axis=0,
     )
-    rows = plain(picked, back_ref[...]).astype(jnp.bfloat16)
-    d_sub = jnp.concatenate(
-        [rows[head * row_count : (head + 1) * row_count] for head in range(head_count)], axis=1
-    )
-    out_ref[...] = transposed(d_sub, weight_ref[...]).astype(jnp.bfloat16)
+    copy.wait()
+    rows = plain(picked, back[...]).astype(jnp.bfloat16)
+    for head in range(head_count):
+        held[:, head * width : (head + 1) * width] = rows[head * row_count : (head + 1) * row_count]
+    out_ref[...] = transposed(held[...], weight_ref[...]).astype(jnp.bfloat16)
 
 
 def on_device(
@@ -273,26 +411,45 @@
 
     if in_blocks:
         merge_block = lax.dynamic_slice_in_dim(merge_weight, here * block_rows, block_rows, 0)
-        split_block = lax.dynamic_slice_in_dim(split_weight, here * block_rows, block_rows, 0)
-        merge_part, offsets = gather_blocks(merge_block, "expert")
-        tokens_all, dp_offsets = gather_blocks(tokens, "dp")
-    else:
-        whole_merge = lax.all_gather(merge_weight, "expert", axis=0, tiled=True)
-        whole_split = lax.all_gather(split_weight, "expert", axis=0, tiled=True)
+        merge_blocks, offsets = gather_blocks(merge_block, "expert")
 
     def route_body(*refs):
-        route_kernel(batch_count, slots_per, key_count, *refs)
-
-    send_inputs, across, down = pl.pallas_call(
+        count = 1 if in_blocks else 0
+        route_kernel(
+            batch_count,
+            slots_per,
+            key_count,
+            refs[0],
+            refs[1],
+            refs[2 : 2 + count],
+            *refs[2 + count : 5 + count],
+            refs[5 + count : -1],
+            refs[-1],
+        )
+
+    block_shape = shape((block_rows, model_width), bf16)
+    send_inputs, across, down, *blocks = pl.pallas_call(
         route_body,
         out_shape=(
             shape((slot_count, sub_width), bf16),
             shape((head_count, row_count), jnp.int32),
             shape((row_count, head_count), jnp.int32),
-        ),
+        )
+        + ((block_shape,) if in_blocks else ()),
+        in_specs=[pl.BlockSpec(memory_space=pltpu.VMEM)] * 2
+        + [pl.BlockSpec(memory_space=pl.ANY)] * (1 if in_blocks else 0),
+        scratch_shapes=[pltpu.SemaphoreType.DMA((1,))],
         compiler_params=params(),
         cost_estimate=cost(2 * slot_count * row_count * model_width, 2 * slot_count * sub_width),
-    )(ids, rows_in)
+    )(ids, *in_hbm(rows_in), *(in_hbm(split_weight) if in_blocks else ()))
+
+    if in_blocks:
+        split_joined = gather_blocks(after(blocks[0], merge_blocks[0]), "expert")[0]
+        token_parts, dp_offsets = gather_parts(after(tokens, send_inputs), "dp")
+        send_inputs = after(send_inputs, split_joined[0])
+    else:
+        whole_merge = lax.all_gather(merge_weight, "expert", axis=0, tiled=True)
+        whole_split = lax.all_gather(split_weight, "expert", axis=0, tiled=True)
 
     def exchange(rows):
         return lax.all_to_all(
@@ -304,7 +461,10 @@
     if in_blocks:
 
         def merge_body(*refs):
-            merge_kernel(offsets, block_rows, *refs)
+            last = group + len(merge_blocks)
+            merge_kernel(
+                offsets, block_rows, refs[:group], refs[group:last], refs[last:-1], refs[-1]
+            )
 
         part_width = expert_count * block_rows
         parts = pl.pallas_call(
@@ -312,10 +472,8 @@
             out_shape=tuple(shape((row_count, part_width), bf16) for _ in range(group)),
             scratch_shapes=[pltpu.VMEM((part_width, model_width), bf16)],
             compiler_params=params(),
-            cost_estimate=cost(
-                2 * group * row_count * part_width * model_width, 2 * group * row_count * model_width
-            ),
-        )(tokens_all, merge_part)
+            cost_estimate=cost(MERGE_COST, 1),
+        )(*token_parts, *merge_blocks)
         parts = [
             part if offset == 0 else swap(part, "dp", offset)
             for part, offset in zip(parts, dp_offsets)
@@ -333,34 +491,73 @@
         compiler_params=params(),
         cost_estimate=cost(2 * slot_count * row_count * model_width, 2 * slot_count * sub_width),
     )(scale, across, *parts)
-    recv_grads = exchange(send_grads)
-
     weight_gate = expert_gate[0]
     weight_up = expert_up[0]
     weight_down = expert_down[0]
-    steps = 4
-    chunk = slot_count // steps
-    by_rows = lambda width: pl.BlockSpec((chunk, width), lambda step: (step, 0))
-    held = lambda array: pl.BlockSpec(array.shape, lambda step: (0, 0))
-    delta, both, hidden = pl.pallas_call(
-        delta_kernel,
-        grid=(steps,),
-        in_specs=[
-            by_rows(sub_width),
-            by_rows(sub_width),
-            held(weight_gate),
-            held(weight_up),
-            held(weight_down),
+    rows = chunks(slot_count, slot_count // 4)
+    anywhere = pl.BlockSpec(memory_space=pl.ANY)
+    inside = pl.BlockSpec(memory_space=pltpu.VMEM)
+    wide = pltpu.VMEM((slot_count, hidden_width), bf16)
+    narrow = pltpu.VMEM((slot_count, sub_width), bf16)
+    upright = pltpu.VMEM(weight_gate.shape, bf16)
+    lying = pltpu.VMEM(weight_down.shape, bf16)
+    sems = lambda *dims: pltpu.SemaphoreType.DMA(dims)
+    steps = len(rows)
+    wide_out = pltpu.HBM((slot_count, hidden_width), bf16)
+    narrow_out = pltpu.HBM((slot_count, sub_width), bf16)
+
+    if in_blocks:
+        split_far = swap(after(split_joined[0], parts[-1]), "expert", 1)
+        recv_grads = exchange(after(send_grads, recv_inputs, split_far))
+
+        def order_body(*refs):
+            place_rows(offsets, block_rows, refs[:-1], refs[-1])
+
+        column = pl.pallas_call(
+            order_body,
+            out_shape=shape((part_width, model_width), bf16),
+            compiler_params=params(),
+        )(split_joined[0], split_far)
+        split_parts, _ = gather_parts(column, "dp")
+        seen_inputs = after(recv_inputs, send_grads)
+        seen_grads = after(recv_grads, split_parts[1])
+    else:
+        recv_grads = exchange(after(send_grads, recv_inputs))
+        seen_inputs = after(recv_inputs, send_grads)
+        seen_grads = recv_grads
+
+    def forward_body(*refs):
+        forward_kernel(rows, *refs)
+
+    kept_inputs, hidden, slope, activation = pl.pallas_call(
+        forward_body,
+        in_specs=[anywhere] * 3,
+        out_specs=(anywhere,) * 4,
+        out_shape=(narrow_out, wide_out, wide_out, wide_out),
+        scratch_shapes=[
+            narrow, upright, upright, wide, wide, wide, sems(steps), sems(2), sems(4, steps),
         ],
-        out_specs=(by_rows(sub_width), by_rows(2 * hidden_width), by_rows(hidden_width)),
+        compiler_params=params(),
+    )(seen_inputs, *in_hbm(weight_gate, weight_up))
+
+    def delta_body(*refs):
+        delta_kernel(rows, *refs)
+
+    both, delta, kept_grads = pl.pallas_call(
+        delta_body,
+        in_specs=[inside] + [anywhere] * 5,
+        out_specs=(inside, anywhere, anywhere),
         out_shape=(
-            shape((slot_count, sub_width), bf16),
-            shape((slot_count, 2 * hidden_width), bf16),
-            shape((slot_count, hidden_width), bf16),
+            pltpu.VMEM((slot_count, 2 * hidden_width), bf16),
+            narrow_out,
+            narrow_out,
         ),
+        scratch_shapes=[
+            wide, wide, upright, upright, lying, narrow,
+            sems(2, steps), sems(3), sems(2, steps),
+        ],
         compiler_params=params(),
-        cost_estimate=cost(10 * slot_count * sub_width * hidden_width, 8 * slot_count * hidden_width),
-    )(recv_inputs, recv_grads, weight_gate, weight_up, weight_down)
+    )(*in_vmem(seen_grads), *in_hbm(slope, activation, weight_gate, weight_up, weight_down))
     returned = exchange(delta)
 
     half = group // 2
@@ -369,25 +566,29 @@
     def weight_body(*refs):
         weight_kernel(group, *refs)
 
+    grad_shapes = ((half, gate_rows, 2 * hidden_width), (half, down_rows, sub_width))
     keep_a, keep_b, send_a, send_b = pl.pallas_call(
         weight_body,
-        out_shape=(
-            shape((half, gate_rows, 2 * hidden_width), f32),
-            shape((half, down_rows, sub_width), f32),
-            shape((half, gate_rows, 2 * hidden_width), bf16),
-            shape((half, down_rows, sub_width), bf16),
-        ),
+        in_specs=[anywhere, anywhere, inside, anywhere],
+        out_shape=tuple(shape(dims, f32) for dims in grad_shapes)
+        + tuple(shape(dims, bf16) for dims in grad_shapes),
         scratch_shapes=[
+            narrow,
+            narrow,
+            wide,
             pltpu.VMEM((sub_width, 2 * hidden_width), f32),
             pltpu.VMEM((hidden_width, sub_width), f32),
+            pltpu.SemaphoreType.DMA((3,)),
         ],
         compiler_params=params(),
         cost_estimate=cost(6 * slot_count * sub_width * hidden_width, 8 * slot_count * hidden_width),
-    )(recv_inputs, recv_grads, both, hidden)
+    )(*in_hbm(kept_inputs, kept_grads), *in_vmem(both), *in_hbm(hidden))
     offset = 1
     while 2 * offset < group:
         half //= 2
         got_a, got_b = swap(send_a, "dp", offset), swap(send_b, "dp", offset)
+        if in_blocks and offset == 1:
+            got_b = after(got_b, split_parts[1])
         keep_a, keep_b, send_a, send_b = pl.pallas_call(
             halve_kernel,
             out_shape=(
@@ -399,7 +600,29 @@
             compiler_params=params(),
         )(keep_a, keep_b, got_a, got_b)
         offset *= 2
+    if in_blocks:
+        def interleave_body(*refs):
+            interleave_kernel(dp_offsets, block_rows, refs[:-1], refs[-1])
+
+        whole_split = pl.pallas_call(
+            interleave_body,
+            out_shape=pltpu.VMEM((model_width, model_width), bf16),
+            compiler_params=params(),
+        )(*split_parts)
+        (whole_split,) = in_vmem(whole_split)
+    d_tokens = pl.pallas_call(
+        split_kernel,
+        in_specs=[inside, anywhere, inside],
+        out_shape=shape((row_count, model_width), bf16),
+        scratch_shapes=[
+            narrow,
+            pltpu.VMEM((row_count, model_width), bf16),
+            pltpu.SemaphoreType.DMA((1,)),
+        ],
+        compiler_params=params(),
+    )(down, returned, whole_split).reshape(batch_count, tok_count, model_width)
     got_a, got_b = swap(send_a, "dp", offset), swap(send_b, "dp", offset)
+    got_b = after(got_b, d_tokens)
     shared_gate, shared_up, shared_down = pl.pallas_call(
         last_kernel,
         out_shape=(
@@ -410,23 +633,6 @@
         compiler_params=params(),
     )(keep_a, keep_b, got_a, got_b)
 
-    if in_blocks:
-        split_part, _ = gather_blocks(split_block, "expert")
-        split_all, _ = gather_blocks(split_part, "dp")
-
-        def order_body(*refs):
-            order_kernel(dp_offsets, offsets, block_rows, *refs)
-
-        whole_split = pl.pallas_call(
-            order_body,
-            out_shape=shape((model_width, model_width), bf16),
-            compiler_params=params(),
-        )(split_all)
-    d_tokens = pl.pallas_call(
-        split_kernel,
-        out_shape=shape((row_count, model_width), bf16),
-        compiler_params=params(),
-    )(down, returned, whole_split).reshape(batch_count, tok_count, model_width)
     return (d_tokens, shared_gate, shared_up, shared_down)
 
 

time: 115 us -> 94.2 us (0.82)
  local copies, waits for them, and re-layouts: 28.6 us -> 3.71 us
  Pallas kernels: 13 us -> 25.2 us
  waiting for transfers between devices: 30.9 us -> 22 us
  starting transfers between devices: 36 us -> 41.8 us
  other arithmetic: 4.58 us -> 0.02 us
    unnamed x52 -> x19, local copies, waits for them, and re-layouts: 26.3 us -> 3.61 us
    ppermute x19 -> x21, waiting for transfers between devices: 30.9 us -> 19.5 us  [swap(): lax.ppermute(value, axis, [(index, index ^ offset) for index in range(lax...]
    pallas_call x4 -> x6, Pallas kernels: 9.22 us -> 18 us  [the longest x1 5.37 us: on_device(): pl.pallas_call(delta_body, in_specs=[inside] + [anywhere] * 5, out_specs=...]
    ppermute x19 -> x21, starting transfers between devices: 21 us -> 26.3 us  [swap(): lax.ppermute(value, axis, [(index, index ^ offset) for index in range(lax...]
    concatenate x4 -> x1, other arithmetic: 4.58 us -> 0.02 us  [gather_blocks(): block = jnp.concatenate(blocks) if len(blocks) > 1 else blocks[0]]
    all_to_all x3, waiting for transfers between devices: 0.01 us -> 2.44 us  [exchange(): lax.all_to_all(rows.reshape(expert_count, -1, sub_width), 'expert', 0, 0,...]
    concatenate x3 -> x1, local copies, waits for them, and re-layouts: 2.24 us -> 0.01 us  [gather_blocks(): block = jnp.concatenate(blocks) if len(blocks) > 1 else blocks[0]]
    pallas_call x1, Pallas kernels: 1.39 us -> 3.12 us  [on_device(): pl.pallas_call(route_body, out_shape=(shape((slot_count, sub_width), bf16...]
  transfers between devices with their start and end apart: 22 -> 24, of which waited for: 6 -> 9; matrix products, arithmetic and copies ran while one was open for 16% -> 1% of each run, Pallas kernels for 9% -> 20%
where the time goes in v2:
time: 94.2 us; the launch traced here: 93.5 us
  starting transfers between devices  41.8 us (44%)
  Pallas kernels  25.2 us (27%)
  waiting for transfers between devices  22 us (23%)
  local copies, waits for them, and re-layouts  3.71 us (4%)
    ppermute x21, starting transfers between devices, swap(): lax.ppermute(value, axis, [(index, index ^ offset) for index in range(lax...  26.3 us
    ppermute x21, waiting for transfers between devices, swap(): lax.ppermute(value, axis, [(index, index ^ offset) for index in range(lax...  19.5 us
    all_to_all x3, starting transfers between devices, exchange(): lax.all_to_all(rows.reshape(expert_count, -1, sub_width), 'expert', 0, 0,...  15.5 us
    pallas_call x1, Pallas kernels, on_device(): pl.pallas_call(delta_body, in_specs=[inside] + [anywhere] * 5, out_specs=...  5.37 us
    pallas_call x1, Pallas kernels, on_device(): pl.pallas_call(forward_body, in_specs=[anywhere] * 3, out_specs=(anywhere...  5.2 us
    unnamed x19, local copies, waits for them, and re-layouts  3.61 us
    pallas_call x1, Pallas kernels, on_device(): pl.pallas_call(split_kernel, in_specs=[inside, anywhere, inside], out_sha...  3.23 us
    pallas_call x1, Pallas kernels, on_device(): pl.pallas_call(route_body, out_shape=(shape((slot_count, sub_width), bf16...  3.12 us
  transfers between devices with their start and end apart: 24, of which 9 were waited for; matrix products, arithmetic and copies ran while one was open for 1% of the time, Pallas kernels for 20%

profile of v2, /device:TPU:0, one launch (start us, length us, event | category | flops | bytes accessed | tf_op | source)
XLA Modules:
  0.0 93.5 jit_solution(13845285028196715565)
XLA Ops:
  1.6 5.1 %collective-permute-start.5 = (bf16[32,1024]{1,0:T(8,128)(2,1)S(1)}, bf16[32,1024]{1,0:T(8,128)(2,1)S(1)}, u32[]{:S(2)}, u32[]{:S(2)}) collective-permute-start(bf16[32,1024]{1,0:T(8,128)(2,1)S(1)} %constant_dynamic-slice_fusion), channel_id=1, source_target_pairs={{0,24},{4,28},{8,16},{12,20},{16,8},{20,12},{24,0},{28,4},{1,25},{... | collective-permute-start | bytes 196616 | tf_op jit(solution)/shard_map/ppermute | solution.py:34
  8.1 3.1 %shard_map.120 = (bf16[1024,256]{1,0:T(8,128)(2,1)}, s32[4,128]{1,0:T(4,128)S(1)}, s32[128,4]{1,0:T(8,128)S(1)}, bf16[32,1024]{1,0:T(8,128)(2,1)S(1)}) custom-call(s32[4,128]{1,0:T(4,128)S(1)} %bitcast.19, bf16[128,1024]{1,0:T(8,128)(2,1)} %bitcast.30, bf16[128,1024]{1,0:T(8,128)(2,1)} %refs_2_.1), custom_call_target="tpu_custom_call" | custom-call | flops 268435456 | bytes 524288 | tf_op jit(solution)/shard_map/pallas_call | solution.py:431
  11.2 1.7 %collective-permute-start = (bf16[128,1024]{1,0:T(8,128)(2,1)}, bf16[128,1024]{1,0:T(8,128)(2,1)S(1)}, u32[]{:S(2)}, u32[]{:S(2)}) collective-permute-start(bf16[128,1024]{1,0:T(8,128)(2,1)} %bitcast.20), channel_id=1, source_target_pairs={{0,2},{1,3},{2,0},{3,1},{4,6},{5,7},{6,4},{7,5},{8,10},{9,11},{10,... | collective-permute-start | bytes 786440 | tf_op jit(solution)/shard_map/ppermute | solution.py:34
  13.0 1.6 %collective-permute-start.6 = (bf16[128,1024]{1,0:T(8,128)(2,1)S(1)}, bf16[128,1024]{1,0:T(8,128)(2,1)S(1)}, u32[]{:S(2)}, u32[]{:S(2)}) collective-permute-start(bf16[128,1024]{1,0:T(8,128)(2,1)S(1)} %pad_maximum_fusion.refs_4_), channel_id=1, source_target_pairs={{0,4},{4,0},{8,12},{12,8},{16,20},{20,16},{24,28},{28,24},{1,5},{5... | collective-permute-start | bytes 786440 | tf_op jit(solution)/shard_map/ppermute | solution.py:34
  15.8 2.9 %collective-permute-start.11 = (bf16[32,1024]{1,0:T(8,128)(2,1)S(1)}, bf16[32,1024]{1,0:T(8,128)(2,1)S(1)}, u32[]{:S(2)}, u32[]{:S(2)}) collective-permute-start(bf16[32,1024]{1,0:T(8,128)(2,1)S(1)} %get-tuple-element.48), channel_id=1, source_target_pairs={{0,16},{4,20},{8,24},{12,28},{16,0},{20,4},{24,8},{28,12},{1,17},{... | collective-permute-start | bytes 196616 | tf_op jit(solution)/shard_map/ppermute | solution.py:34
  18.9 4.8 %collective-permute-start.12 = (bf16[32,1024]{1,0:T(8,128)(2,1)S(1)}, bf16[32,1024]{1,0:T(8,128)(2,1)S(1)}, u32[]{:S(2)}, u32[]{:S(2)}) collective-permute-start(bf16[32,1024]{1,0:T(8,128)(2,1)S(1)} %get-tuple-element.48), channel_id=1, source_target_pairs={{0,24},{4,28},{8,16},{12,20},{16,8},{20,12},{24,0},{28,4},{1,25},{... | collective-permute-start | bytes 196616 | tf_op jit(solution)/shard_map/ppermute | solution.py:34
  23.8 2.1 %collective-permute-done.12 = bf16[32,1024]{1,0:T(8,128)(2,1)S(1)} collective-permute-done((bf16[32,1024]{1,0:T(8,128)(2,1)S(1)}, bf16[32,1024]{1,0:T(8,128)(2,1)S(1)}, u32[]{:S(2)}, u32[]{:S(2)}) %collective-permute-start.12) | collective-permute-done | bytes 65568 | tf_op jit(solution)/shard_map/ppermute | solution.py:34
  25.9 5.1 %all-to-all-start = ((bf16[8,128,256]{2,1,0:T(8,128)(2,1)}), bf16[8,128,256]{2,1,0:T(8,128)(2,1)S(1)}, u32[]{:S(2)}, u32[]{:S(2)}) async-start(bf16[8,128,256]{2,1,0:T(8,128)(2,1)} %bitcast.4), calls=%async_computation | async-start | bytes 1048576 | tf_op jit(solution)/shard_map/all_to_all | solution.py:455
  32.0 3.7 %collective-permute-done.9.refs_5_ = bf16[128,256]{1,0:T(8,128)(2,1)S(1)} collective-permute-done((bf16[128,256]{1,0:T(8,128)(2,1)S(1)}, bf16[128,256]{1,0:T(8,128)(2,1)S(1)}, u32[]{:S(2)}, u32[]{:S(2)}) %collective-permute-start.9) | collective-permute-done | bytes 65568 | tf_op jit(solution)/shard_map/ppermute | solution.py:34
  35.7 2.0 %collective-permute-start.13 = (bf16[128,1024]{1,0:T(8,128)(2,1)S(1)}, bf16[128,1024]{1,0:T(8,128)(2,1)S(1)}, u32[]{:S(2)}, u32[]{:S(2)}) collective-permute-start(bf16[128,1024]{1,0:T(8,128)(2,1)S(1)} %constant_dynamic-update-slice_fusion.refs_0_), channel_id=1, source_target_pairs={{0,4},{4,0},{8,12},{12,8},{16,20},{20,16},{24,28},{28,24},{1,5},{5... | collective-permute-start | bytes 786440 | tf_op jit(solution)/shard_map/ppermute | solution.py:34
  39.0 3.0 %collective-permute-done.7.refs_3_ = bf16[128,256]{1,0:T(8,128)(2,1)S(1)} collective-permute-done((bf16[128,256]{1,0:T(8,128)(2,1)S(1)}, bf16[128,256]{1,0:T(8,128)(2,1)S(1)}, u32[]{:S(2)}, u32[]{:S(2)}) %collective-permute-start.7) | collective-permute-done | bytes 65568 | tf_op jit(solution)/shard_map/ppermute | solution.py:34
  42.0 1.7 %shard_map.122 = bf16[1024,256]{1,0:T(8,128)(2,1)} custom-call(f32[128,4]{1,0:T(8,128)S(1)} %bitcast.18, s32[4,128]{1,0:T(4,128)S(1)} %get-tuple-element.40.refs_1_, bf16[128,256]{1,0:T(8,128)(2,1)S(1)} %get-tuple-element.43.refs_2_, bf16[128,256]{1,0:T(8,128)(2,1)S(1)} %collective-permute-done.7.refs_3_, ...), custom_call_target="tpu_custom_call" | custom-call | flops 268435456 | bytes 524288 | tf_op jit(solution)/shard_map/pallas_call | solution.py:488
  43.7 1.5 %collective-permute-done.13.refs_1_ = bf16[128,1024]{1,0:T(8,128)(2,1)S(1)} collective-permute-done((bf16[128,1024]{1,0:T(8,128)(2,1)S(1)}, bf16[128,1024]{1,0:T(8,128)(2,1)S(1)}, u32[]{:S(2)}, u32[]{:S(2)}) %collective-permute-start.13) | collective-permute-done | bytes 262176 | tf_op jit(solution)/shard_map/ppermute | solution.py:34
  45.1 4.7 %all-to-all-start.1 = ((bf16[8,128,256]{2,1,0:T(8,128)(2,1)}), bf16[8,128,256]{2,1,0:T(8,128)(2,1)S(1)}, u32[]{:S(2)}, u32[]{:S(2)}) async-start(bf16[8,128,256]{2,1,0:T(8,128)(2,1)} %bitcast.6), calls=%async_computation.1 | async-start | bytes 1048576 | tf_op jit(solution)/shard_map/all_to_all | solution.py:455
  49.9 1.8 %collective-permute-start.14 = (bf16[256,1024]{1,0:T(8,128)(2,1)S(1)}, bf16[256,1024]{1,0:T(8,128)(2,1)}, u32[]{:S(2)}, u32[]{:S(2)}) collective-permute-start(bf16[256,1024]{1,0:T(8,128)(2,1)S(1)} %shard_map.123.refs_0_), channel_id=1, source_target_pairs={{0,2},{1,3},{2,0},{3,1},{4,6},{5,7},{6,4},{7,5},{8,10},{9,11},{10,... | collective-permute-start | bytes 1572872 | tf_op jit(solution)/shard_map/ppermute | solution.py:34
  51.7 5.2 %shard_map.124 = (bf16[1024,256]{1,0:T(8,128)(2,1)}, bf16[1024,768]{1,0:T(8,128)(2,1)}, bf16[1024,768]{1,0:T(8,128)(2,1)}, bf16[1024,768]{1,0:T(8,128)(2,1)}) custom-call(bf16[1024,256]{1,0:T(8,128)(2,1)S(1)} %bitcast.17, bf16[256,768]{1,0:T(8,128)(2,1)} %bitcast.23, bf16[256,768]{1,0:T(8,128)(2,1)} %bitcast.25), custom_call_target="tpu_custom_call" | custom-call | tf_op jit(solution)/shard_map/pallas_call | solution.py:532
  56.9 6.3 %collective-permute-done.14.refs_1_ = bf16[256,1024]{1,0:T(8,128)(2,1)} collective-permute-done((bf16[256,1024]{1,0:T(8,128)(2,1)S(1)}, bf16[256,1024]{1,0:T(8,128)(2,1)}, u32[]{:S(2)}, u32[]{:S(2)}) %collective-permute-start.14) | collective-permute-done | bytes 524320 | tf_op jit(solution)/shard_map/ppermute | solution.py:34
  65.1 5.4 %shard_map.125 = (bf16[1024,1536]{1,0:T(8,128)(2,1)S(1)}, bf16[1024,256]{1,0:T(8,128)(2,1)}, bf16[1024,256]{1,0:T(8,128)(2,1)}) custom-call(bf16[1024,256]{1,0:T(8,128)(2,1)S(1)} %bitcast.16, bf16[1024,768]{1,0:T(8,128)(2,1)} %get-tuple-element.54.refs_1_, bf16[1024,768]{1,0:T(8,128)(2,1)} %get-tuple-element.55.refs_2_, bf16[256,768]{1,0:T(8,128)(2,1)} %bitcast.24, ...), custom_call_target="tpu_custom_call" | custom-call | tf_op jit(solution)/shard_map/pallas_call | solution.py:546
  70.4 5.7 %all-to-all-start.2 = ((bf16[8,128,256]{2,1,0:T(8,128)(2,1)}), bf16[8,128,256]{2,1,0:T(8,128)(2,1)}, u32[]{:S(2)}, u32[]{:S(2)}) async-start(bf16[8,128,256]{2,1,0:T(8,128)(2,1)} %bitcast.27), calls=%async_computation.2 | async-start | bytes 1048576 | tf_op jit(solution)/shard_map/all_to_all | solution.py:455
  76.2 2.9 %shard_map.128 = (f32[2,64,1536]{2,1,0:T(8,128)S(1)}, f32[2,192,256]{2,1,0:T(8,128)S(1)}, bf16[2,64,1536]{2,1,0:T(8,128)(2,1)S(1)}, bf16[2,192,256]{2,1,0:T(8,128)(2,1)S(1)}) custom-call(bf16[1024,256]{1,0:T(8,128)(2,1)} %get-tuple-element.57.refs_0_, bf16[1024,256]{1,0:T(8,128)(2,1)} %get-tuple-element.58.refs_1_, ...), custom_call_target="tpu_custom_call" | custom-call | flops 1207959552 | bytes 6291456 | tf_op jit(solution)/shard_map/pallas_call | solution.py:570
  80.2 2.5 %collective-permute-done.18.got_b = bf16[2,192,256]{2,1,0:T(8,128)(2,1)S(1)} collective-permute-done((bf16[2,192,256]{2,1,0:T(8,128)(2,1)S(1)}, bf16[2,192,256]{2,1,0:T(8,128)(2,1)S(1)}, u32[]{:S(2)}, u32[]{:S(2)}) %collective-permute-start.18) | collective-permute-done | bytes 196640 | tf_op jit(solution)/shard_map/ppermute | solution.py:34
  83.4 1.7 %collective-permute-start.19 = (bf16[1,64,1536]{2,1,0:T(8,128)(2,1)}, bf16[1,64,1536]{2,1,0:T(8,128)(2,1)S(1)}, u32[]{:S(2)}, u32[]{:S(2)}) collective-permute-start(bf16[1,64,1536]{2,1,0:T(8,128)(2,1)} %get-tuple-element.68), channel_id=1, source_target_pairs={{0,2},{1,3},{2,0},{3,1},{4,6},{5,7},{6,4},{7,5},{8,10},{9,11},{10,... | collective-permute-start | bytes 589832 | tf_op jit(solution)/shard_map/ppermute | solution.py:34
  86.7 2.4 %all-to-all-done.2 = bf16[8,128,256]{2,1,0:T(8,128)(2,1)} async-done(((bf16[8,128,256]{2,1,0:T(8,128)(2,1)}), bf16[8,128,256]{2,1,0:T(8,128)(2,1)}, u32[]{:S(2)}, u32[]{:S(2)}) %all-to-all-start.2) | async-done | bytes 524320 | tf_op jit(solution)/shard_map/all_to_all | solution.py:455
  89.1 3.2 %shard_map.127 = bf16[128,1024]{1,0:T(8,128)(2,1)} custom-call(s32[128,4]{1,0:T(8,128)S(1)} %get-tuple-element.39.down_ref, bf16[1024,256]{1,0:T(8,128)(2,1)} %bitcast.12.back_ref, bf16[1024,1024]{1,0:T(8,128)(2,1)S(1)} %shard_map.126.weight_ref), custom_call_target="tpu_custom_call" | custom-call | tf_op jit(solution)/shard_map/pallas_call | solution.py:613
  (58 shorter events, 12.6 us)
Async XLA Ops:
  1.6 11.4 %collective-permute-start.5 = (bf16[32,1024]{1,0:T(8,128)(2,1)S(1)}, bf16[32,1024]{1,0:T(8,128)(2,1)S(1)}, u32[]{:S(2)}, u32[]{:S(2)}) collective-permute-start(bf16[32,1024]{1,0:T(8,128)(2,1)S(1)} %constant_dynamic-slice_fusion), channel_id=1, source_target_pairs={{0,24},{4,28},{8,16},{12,20},{16,8},{20,12},{24,0},{28,4},{1,25},{... | collective-permute-start | bytes 196616 | tf_op jit(solution)/shard_map/ppermute | solution.py:34
  6.7 6.3 %collective-permute-start.4 = (bf16[32,1024]{1,0:T(8,128)(2,1)S(1)}, bf16[32,1024]{1,0:T(8,128)(2,1)S(1)}, u32[]{:S(2)}, u32[]{:S(2)}) collective-permute-start(bf16[32,1024]{1,0:T(8,128)(2,1)S(1)} %constant_dynamic-slice_fusion), channel_id=1, source_target_pairs={{0,16},{4,20},{8,24},{12,28},{16,0},{20,4},{24,8},{28,12},{1,17},{... | collective-permute-start | bytes 196616 | tf_op jit(solution)/shard_map/ppermute | solution.py:34
  6.7 6.3 %collective-permute-start.3 = (bf16[32,1024]{1,0:T(8,128)(2,1)S(1)}, bf16[32,1024]{1,0:T(8,128)(2,1)S(1)}, u32[]{:S(2)}, u32[]{:S(2)}) collective-permute-start(bf16[32,1024]{1,0:T(8,128)(2,1)S(1)} %constant_dynamic-slice_fusion), channel_id=1, source_target_pairs={{0,8},{4,12},{8,0},{12,4},{16,24},{20,28},{24,16},{28,20},{1,9},{5... | collective-permute-start | bytes 196616 | tf_op jit(solution)/shard_map/ppermute | solution.py:34
  11.2 12.4 %collective-permute-start = (bf16[128,1024]{1,0:T(8,128)(2,1)}, bf16[128,1024]{1,0:T(8,128)(2,1)S(1)}, u32[]{:S(2)}, u32[]{:S(2)}) collective-permute-start(bf16[128,1024]{1,0:T(8,128)(2,1)} %bitcast.20), channel_id=1, source_target_pairs={{0,2},{1,3},{2,0},{3,1},{4,6},{5,7},{6,4},{7,5},{8,10},{9,11},{10,... | collective-permute-start | bytes 786440 | tf_op jit(solution)/shard_map/ppermute | solution.py:34
  12.9 18.1 %collective-permute-start.1 = (bf16[128,1024]{1,0:T(8,128)(2,1)}, bf16[128,1024]{1,0:T(8,128)(2,1)S(1)}, u32[]{:S(2)}, u32[]{:S(2)}) collective-permute-start(bf16[128,1024]{1,0:T(8,128)(2,1)} %bitcast.21), channel_id=1, source_target_pairs={{0,1},{1,0},{2,3},{3,2},{4,5},{5,4},{6,7},{7,6},{8,9},{9,8},{10,11... | collective-permute-start | bytes 786440 | tf_op jit(solution)/shard_map/ppermute | solution.py:34
  13.0 18.1 %collective-permute-start.6 = (bf16[128,1024]{1,0:T(8,128)(2,1)S(1)}, bf16[128,1024]{1,0:T(8,128)(2,1)S(1)}, u32[]{:S(2)}, u32[]{:S(2)}) collective-permute-start(bf16[128,1024]{1,0:T(8,128)(2,1)S(1)} %pad_maximum_fusion.refs_4_), channel_id=1, source_target_pairs={{0,4},{4,0},{8,12},{12,8},{16,20},{20,16},{24,28},{28,24},{1,5},{5... | collective-permute-start | bytes 786440 | tf_op jit(solution)/shard_map/ppermute | solution.py:34
  14.6 4.3 %collective-permute-start.10 = (bf16[32,1024]{1,0:T(8,128)(2,1)S(1)}, bf16[32,1024]{1,0:T(8,128)(2,1)S(1)}, u32[]{:S(2)}, u32[]{:S(2)}) collective-permute-start(bf16[32,1024]{1,0:T(8,128)(2,1)S(1)} %get-tuple-element.48), channel_id=1, source_target_pairs={{0,8},{4,12},{8,0},{12,4},{16,24},{20,28},{24,16},{28,20},{1,9},{5... | collective-permute-start | bytes 196616 | tf_op jit(solution)/shard_map/ppermute | solution.py:34
  15.8 8.0 %collective-permute-start.11 = (bf16[32,1024]{1,0:T(8,128)(2,1)S(1)}, bf16[32,1024]{1,0:T(8,128)(2,1)S(1)}, u32[]{:S(2)}, u32[]{:S(2)}) collective-permute-start(bf16[32,1024]{1,0:T(8,128)(2,1)S(1)} %get-tuple-element.48), channel_id=1, source_target_pairs={{0,16},{4,20},{8,24},{12,28},{16,0},{20,4},{24,8},{28,12},{1,17},{... | collective-permute-start | bytes 196616 | tf_op jit(solution)/shard_map/ppermute | solution.py:34
  18.9 7.1 %collective-permute-start.12 = (bf16[32,1024]{1,0:T(8,128)(2,1)S(1)}, bf16[32,1024]{1,0:T(8,128)(2,1)S(1)}, u32[]{:S(2)}, u32[]{:S(2)}) collective-permute-start(bf16[32,1024]{1,0:T(8,128)(2,1)S(1)} %get-tuple-element.48), channel_id=1, source_target_pairs={{0,24},{4,28},{8,16},{12,20},{16,8},{20,12},{24,0},{28,4},{1,25},{... | collective-permute-start | bytes 196616 | tf_op jit(solution)/shard_map/ppermute | solution.py:34
  23.7 7.4 %collective-permute-start.2 = (bf16[128,1024]{1,0:T(8,128)(2,1)S(1)}, bf16[128,1024]{1,0:T(8,128)(2,1)S(1)}, u32[]{:S(2)}, u32[]{:S(2)}) collective-permute-start(bf16[128,1024]{1,0:T(8,128)(2,1)S(1)} %collective-permute-done.refs_1_), channel_id=1, source_target_pairs={{0,1},{1,0},{2,3},{3,2},{4,5},{5,4},{6,7},{7,6},{8,9},{9,8},{10,11... | collective-permute-start | bytes 786440 | tf_op jit(solution)/shard_map/ppermute | solution.py:34
  25.9 19.2 %all-to-all-start = ((bf16[8,128,256]{2,1,0:T(8,128)(2,1)}), bf16[8,128,256]{2,1,0:T(8,128)(2,1)S(1)}, u32[]{:S(2)}, u32[]{:S(2)}) async-start(bf16[8,128,256]{2,1,0:T(8,128)(2,1)} %bitcast.4), calls=%async_computation | async-start | bytes 1048576 | tf_op jit(solution)/shard_map/all_to_all | solution.py:455
  31.9 3.8 %collective-permute-start.9 = (bf16[128,256]{1,0:T(8,128)(2,1)S(1)}, bf16[128,256]{1,0:T(8,128)(2,1)S(1)}, u32[]{:S(2)}, u32[]{:S(2)}) collective-permute-start(bf16[128,256]{1,0:T(8,128)(2,1)S(1)} %get-tuple-element.46), channel_id=1, source_target_pairs={{0,3},{1,2},{2,1},{3,0},{4,7},{5,6},{6,5},{7,4},{8,11},{9,10},{10,... | collective-permute-start | bytes 196616 | tf_op jit(solution)/shard_map/ppermute | solution.py:34
  35.7 9.4 %collective-permute-start.13 = (bf16[128,1024]{1,0:T(8,128)(2,1)S(1)}, bf16[128,1024]{1,0:T(8,128)(2,1)S(1)}, u32[]{:S(2)}, u32[]{:S(2)}) collective-permute-start(bf16[128,1024]{1,0:T(8,128)(2,1)S(1)} %constant_dynamic-update-slice_fusion.refs_0_), channel_id=1, source_target_pairs={{0,4},{4,0},{8,12},{12,8},{16,20},{20,16},{24,28},{28,24},{1,5},{5... | collective-permute-start | bytes 786440 | tf_op jit(solution)/shard_map/ppermute | solution.py:34
  37.7 4.3 %collective-permute-start.7 = (bf16[128,256]{1,0:T(8,128)(2,1)S(1)}, bf16[128,256]{1,0:T(8,128)(2,1)S(1)}, u32[]{:S(2)}, u32[]{:S(2)}) collective-permute-start(bf16[128,256]{1,0:T(8,128)(2,1)S(1)} %get-tuple-element.44), channel_id=1, source_target_pairs={{0,2},{1,3},{2,0},{3,1},{4,6},{5,7},{6,4},{7,5},{8,10},{9,11},{10,... | collective-permute-start | bytes 196616 | tf_op jit(solution)/shard_map/ppermute | solution.py:34
  38.9 3.1 %collective-permute-start.8 = (bf16[128,256]{1,0:T(8,128)(2,1)S(1)}, bf16[128,256]{1,0:T(8,128)(2,1)S(1)}, u32[]{:S(2)}, u32[]{:S(2)}) collective-permute-start(bf16[128,256]{1,0:T(8,128)(2,1)S(1)} %get-tuple-element.45), channel_id=1, source_target_pairs={{0,1},{1,0},{2,3},{3,2},{4,5},{5,4},{6,7},{7,6},{8,9},{9,8},{10,11... | collective-permute-start | bytes 196616 | tf_op jit(solution)/shard_map/ppermute | solution.py:34
  45.1 18.1 %all-to-all-start.1 = ((bf16[8,128,256]{2,1,0:T(8,128)(2,1)}), bf16[8,128,256]{2,1,0:T(8,128)(2,1)S(1)}, u32[]{:S(2)}, u32[]{:S(2)}) async-start(bf16[8,128,256]{2,1,0:T(8,128)(2,1)} %bitcast.6), calls=%async_computation.1 | async-start | bytes 1048576 | tf_op jit(solution)/shard_map/all_to_all | solution.py:455
  49.9 13.3 %collective-permute-start.14 = (bf16[256,1024]{1,0:T(8,128)(2,1)S(1)}, bf16[256,1024]{1,0:T(8,128)(2,1)}, u32[]{:S(2)}, u32[]{:S(2)}) collective-permute-start(bf16[256,1024]{1,0:T(8,128)(2,1)S(1)} %shard_map.123.refs_0_), channel_id=1, source_target_pairs={{0,2},{1,3},{2,0},{3,1},{4,6},{5,7},{6,4},{7,5},{8,10},{9,11},{10,... | collective-permute-start | bytes 1572872 | tf_op jit(solution)/shard_map/ppermute | solution.py:34
  70.4 18.6 %all-to-all-start.2 = ((bf16[8,128,256]{2,1,0:T(8,128)(2,1)}), bf16[8,128,256]{2,1,0:T(8,128)(2,1)}, u32[]{:S(2)}, u32[]{:S(2)}) async-start(bf16[8,128,256]{2,1,0:T(8,128)(2,1)} %bitcast.27), calls=%async_computation.2 | async-start | bytes 1048576 | tf_op jit(solution)/shard_map/all_to_all | solution.py:455
  79.1 3.6 %collective-permute-start.17 = (bf16[2,64,1536]{2,1,0:T(8,128)(2,1)S(1)}, bf16[2,64,1536]{2,1,0:T(8,128)(2,1)S(1)}, u32[]{:S(2)}, u32[]{:S(2)}) collective-permute-start(bf16[2,64,1536]{2,1,0:T(8,128)(2,1)S(1)} %get-tuple-element.63), channel_id=1, source_target_pairs={{0,1},{1,0},{2,3},{3,2},{4,5},{5,4},{6,7},{7,6},{8,9},{9,8},{10,11... | collective-permute-start | bytes 1179656 | tf_op jit(solution)/shard_map/ppermute | solution.py:34
  79.2 6.3 %collective-permute-start.15 = (bf16[256,1024]{1,0:T(8,128)(2,1)S(1)}, bf16[256,1024]{1,0:T(8,128)(2,1)S(1)}, u32[]{:S(2)}, u32[]{:S(2)}) collective-permute-start(bf16[256,1024]{1,0:T(8,128)(2,1)S(1)} %copy-done.4), channel_id=1, source_target_pairs={{0,1},{1,0},{2,3},{3,2},{4,5},{5,4},{6,7},{7,6},{8,9},{9,8},{10,11... | collective-permute-start | bytes 1572872 | tf_op jit(solution)/shard_map/ppermute | solution.py:34
  79.7 5.8 %collective-permute-start.16 = (bf16[256,1024]{1,0:T(8,128)(2,1)}, bf16[256,1024]{1,0:T(8,128)(2,1)S(1)}, u32[]{:S(2)}, u32[]{:S(2)}) collective-permute-start(bf16[256,1024]{1,0:T(8,128)(2,1)} %collective-permute-done.14.refs_1_), channel_id=1, source_target_pairs={{0,1},{1,0},{2,3},{3,2},{4,5},{5,4},{6,7},{7,6},{8,9},{9,8},{10,11... | collective-permute-start | bytes 1572872 | tf_op jit(solution)/shard_map/ppermute | solution.py:34
  79.8 2.9 %collective-permute-start.18 = (bf16[2,192,256]{2,1,0:T(8,128)(2,1)S(1)}, bf16[2,192,256]{2,1,0:T(8,128)(2,1)S(1)}, u32[]{:S(2)}, u32[]{:S(2)}) collective-permute-start(bf16[2,192,256]{2,1,0:T(8,128)(2,1)S(1)} %get-tuple-element.64), channel_id=1, source_target_pairs={{0,1},{1,0},{2,3},{3,2},{4,5},{5,4},{6,7},{7,6},{8,9},{9,8},{10,11... | collective-permute-start | bytes 589832 | tf_op jit(solution)/shard_map/ppermute | solution.py:34
  83.4 9.3 %collective-permute-start.19 = (bf16[1,64,1536]{2,1,0:T(8,128)(2,1)}, bf16[1,64,1536]{2,1,0:T(8,128)(2,1)S(1)}, u32[]{:S(2)}, u32[]{:S(2)}) collective-permute-start(bf16[1,64,1536]{2,1,0:T(8,128)(2,1)} %get-tuple-element.68), channel_id=1, source_target_pairs={{0,2},{1,3},{2,0},{3,1},{4,6},{5,7},{6,4},{7,5},{8,10},{9,11},{10,... | collective-permute-start | bytes 589832 | tf_op jit(solution)/shard_map/ppermute | solution.py:34
  85.2 7.5 %collective-permute-start.20 = (bf16[1,192,256]{2,1,0:T(8,128)(2,1)S(1)}, bf16[1,192,256]{2,1,0:T(8,128)(2,1)S(1)}, u32[]{:S(2)}, u32[]{:S(2)}) collective-permute-start(bf16[1,192,256]{2,1,0:T(8,128)(2,1)S(1)} %get-tuple-element.69), channel_id=1, source_target_pairs={{0,2},{1,3},{2,0},{3,1},{4,6},{5,7},{6,4},{7,5},{8,10},{9,11},{10,... | collective-permute-start | bytes 294920 | tf_op jit(solution)/shard_map/ppermute | solution.py:34
  (7 other events, 50.2 us)

commit v3 on v2

--- a/solution.py
+++ b/solution.py
@@ -6,7 +6,9 @@
 from jax.sharding import PartitionSpec as P
 
 LANES = 128
-MERGE_COST = 5000000000
+MERGE_COST = 20000000000
+ROUTE_COST = 1
+GRAD_COST = 1
 VMEM_BYTES = 16 * 1024 * 1024
 
 
@@ -90,15 +92,8 @@
 
 
 def route_kernel(
-    batch_count, slots_per, key_count, ids_ref, rows_ref, weight_refs, send_ref, across_ref, down_ref, block_refs, sems
+    batch_count, slots_per, key_count, ids_ref, rows_ref, send_ref, across_ref, down_ref
 ):
-    here = lax.axis_index("dp")
-    copies = []
-    for number, (weight_ref, block_ref) in enumerate(zip(weight_refs, block_refs)):
-        count = block_ref.shape[0]
-        own = weight_ref.at[pl.ds(pl.multiple_of(here * count, count), count), :]
-        copies.append(pltpu.make_async_copy(own, block_ref, sems.at[number]))
-        copies[-1].start()
     head_count, row_count = ids_ref.shape
     width = rows_ref.shape[1] // head_count
     lane = lax.broadcasted_iota(jnp.int32, (1, row_count), 1)
@@ -128,8 +123,6 @@
     )
     across_ref[...] = across
     down_ref[...] = across.astype(jnp.float32).T.astype(jnp.int32)
-    for copy in copies:
-        copy.wait()
 
 
 def scatter_rows(target, row_list, slot_count):
@@ -246,7 +239,7 @@
 def delta_kernel(
     rows, grad_ref, slope_ref, activation_ref, gate_ref, up_ref, down_ref,
     both_ref, delta_ref, grads_out,
-    slope, activation, gate_held, up_held, down_held, out, sems, weight_sems, out_sems
+    grads_held, slope, activation, gate_held, up_held, down_held, out, sems, weight_sems, out_sems
 ):
     hidden_width = gate_ref.shape[1]
     weights = [
@@ -255,26 +248,33 @@
             ((down_ref, down_held), (gate_ref, gate_held), (up_ref, up_held))
         )
     ]
-    copies = []
-    weights[0].start()
-    for number, part in enumerate(rows):
-        copies.append(
-            [
-                send_out(source, target, part, sems.at[place, number])
+    arriving = {}
+
+    def bring(number):
+        if number < len(rows):
+            arriving[number] = [
+                send_out(source, target, rows[number], sems.at[place, number])
                 for place, (source, target) in enumerate(
-                    ((slope_ref, slope), (activation_ref, activation))
+                    ((grad_ref, grads_held), (slope_ref, slope), (activation_ref, activation))
                 )
             ]
-        )
-        if number == 0:
-            weights[1].start()
-            weights[2].start()
+
+    weights[0].start()
+    bring(0)
+    weights[1].start()
+    weights[2].start()
     weights[0].wait()
     outs = []
-    for number, (part, arrived) in enumerate(zip(rows, copies)):
-        d_hidden = transposed(grad_ref[part, :], down_held[...])
-        arrived[0].wait()
-        arrived[1].wait()
+    for number, part in enumerate(rows):
+        arriving[number][0].wait()
+        d_hidden = transposed(grads_held[part, :], down_held[...])
+        arriving[number][1].wait()
+        arriving[number][2].wait()
+        if number == 0:
+            bring(1)
+            bring(2)
+        else:
+            bring(number + 2)
         delta_gate = (d_hidden * slope[part, :].astype(jnp.float32)).astype(jnp.bfloat16)
         delta_up = (d_hidden * activation[part, :].astype(jnp.float32)).astype(jnp.bfloat16)
         both_ref[part, :hidden_width] = delta_gate
@@ -286,7 +286,7 @@
             transposed(delta_gate, gate_held[...]) + transposed(delta_up, up_held[...])
         ).astype(jnp.bfloat16)
         outs.append(send_out(out, delta_ref, part, out_sems.at[0, number]))
-        outs.append(send_out(grad_ref, grads_out, part, out_sems.at[1, number]))
+        outs.append(send_out(grads_held, grads_out, part, out_sems.at[1, number]))
     for copy in outs:
         copy.wait()
 
@@ -410,43 +410,33 @@
     ids = route.reshape(row_count, head_count).T
 
     if in_blocks:
-        merge_block = lax.dynamic_slice_in_dim(merge_weight, here * block_rows, block_rows, 0)
-        merge_blocks, offsets = gather_blocks(merge_block, "expert")
+        own_block = lambda weight: lax.dynamic_slice_in_dim(
+            weight, here * block_rows, block_rows, 0
+        )
+        pair = jnp.stack([own_block(merge_weight), own_block(split_weight)])
+        pairs = [pair] + [swap(pair, "expert", step * (expert_count // 4)) for step in range(1, 4)]
+        merge_joined = jnp.concatenate([one[0] for one in pairs])
+        split_joined = [jnp.concatenate([one[1] for one in pairs])]
+        merge_blocks = [merge_joined, swap(merge_joined, "expert", 1)]
+        offsets = [0, 2, 4, 6, 1, 3, 5, 7]
+        ids = after(ids, pairs[1])
 
     def route_body(*refs):
-        count = 1 if in_blocks else 0
-        route_kernel(
-            batch_count,
-            slots_per,
-            key_count,
-            refs[0],
-            refs[1],
-            refs[2 : 2 + count],
-            *refs[2 + count : 5 + count],
-            refs[5 + count : -1],
-            refs[-1],
-        )
-
-    block_shape = shape((block_rows, model_width), bf16)
-    send_inputs, across, down, *blocks = pl.pallas_call(
+        route_kernel(batch_count, slots_per, key_count, *refs)
+
+    send_inputs, across, down = pl.pallas_call(
         route_body,
         out_shape=(
             shape((slot_count, sub_width), bf16),
             shape((head_count, row_count), jnp.int32),
             shape((row_count, head_count), jnp.int32),
-        )
-        + ((block_shape,) if in_blocks else ()),
-        in_specs=[pl.BlockSpec(memory_space=pltpu.VMEM)] * 2
-        + [pl.BlockSpec(memory_space=pl.ANY)] * (1 if in_blocks else 0),
-        scratch_shapes=[pltpu.SemaphoreType.DMA((1,))],
+        ),
         compiler_params=params(),
-        cost_estimate=cost(2 * slot_count * row_count * model_width, 2 * slot_count * sub_width),
-    )(ids, *in_hbm(rows_in), *(in_hbm(split_weight) if in_blocks else ()))
+        cost_estimate=cost(ROUTE_COST, 1),
+    )(ids, *in_hbm(rows_in))
 
     if in_blocks:
-        split_joined = gather_blocks(after(blocks[0], merge_blocks[0]), "expert")[0]
-        token_parts, dp_offsets = gather_parts(after(tokens, send_inputs), "dp")
-        send_inputs = after(send_inputs, split_joined[0])
+        token_parts, dp_offsets = gather_parts(after(tokens, across), "dp")
     else:
         whole_merge = lax.all_gather(merge_weight, "expert", axis=0, tiled=True)
         whole_split = lax.all_gather(split_weight, "expert", axis=0, tiled=True)
@@ -489,12 +479,12 @@
         grad_body,
         out_shape=shape((slot_count, sub_width), bf16),
         compiler_params=params(),
-        cost_estimate=cost(2 * slot_count * row_count * model_width, 2 * slot_count * sub_width),
+        cost_estimate=cost(GRAD_COST, 1),
     )(scale, across, *parts)
     weight_gate = expert_gate[0]
     weight_up = expert_up[0]
     weight_down = expert_down[0]
-    rows = chunks(slot_count, slot_count // 4)
+    rows = chunks(slot_count, slot_count // 2)
     anywhere = pl.BlockSpec(memory_space=pl.ANY)
     inside = pl.BlockSpec(memory_space=pltpu.VMEM)
     wide = pltpu.VMEM((slot_count, hidden_width), bf16)
@@ -507,7 +497,7 @@
     narrow_out = pltpu.HBM((slot_count, sub_width), bf16)
 
     if in_blocks:
-        split_far = swap(after(split_joined[0], parts[-1]), "expert", 1)
+        split_far = swap(after(split_joined[0], parts[0]), "expert", 1)
         recv_grads = exchange(after(send_grads, recv_inputs, split_far))
 
         def order_body(*refs):
@@ -545,7 +535,7 @@
 
     both, delta, kept_grads = pl.pallas_call(
         delta_body,
-        in_specs=[inside] + [anywhere] * 5,
+        in_specs=[anywhere] * 6,
         out_specs=(inside, anywhere, anywhere),
         out_shape=(
             pltpu.VMEM((slot_count, 2 * hidden_width), bf16),
@@ -553,11 +543,11 @@
             narrow_out,
         ),
         scratch_shapes=[
-            wide, wide, upright, upright, lying, narrow,
-            sems(2, steps), sems(3), sems(2, steps),
+            narrow, wide, wide, upright, upright, lying, narrow,
+            sems(3, steps), sems(3), sems(2, steps),
         ],
         compiler_params=params(),
-    )(*in_vmem(seen_grads), *in_hbm(slope, activation, weight_gate, weight_up, weight_down))
+    )(*in_hbm(seen_grads), *in_hbm(slope, activation, weight_gate, weight_up, weight_down))
     returned = exchange(delta)
 
     half = group // 2

time: 94.2 us -> 88.2 us (0.936)
  starting transfers between devices: 41.8 us -> 30.6 us
  waiting for transfers between devices: 22 us -> 30.5 us
  Pallas kernels: 25.2 us -> 23 us
  local copies, waits for them, and re-layouts: 3.71 us -> 2.64 us
    ppermute x21 -> x18, starting transfers between devices: 26.3 us -> 17.4 us  [swap(): lax.ppermute(value, axis, [(index, index ^ offset) for index in range(lax...]
    ppermute x21 -> x18, waiting for transfers between devices: 19.5 us -> 25.1 us  [swap(): lax.ppermute(value, axis, [(index, index ^ offset) for index in range(lax...]
    all_to_all x3, waiting for transfers between devices: 2.44 us -> 5.4 us  [exchange(): lax.all_to_all(rows.reshape(expert_count, -1, sub_width), 'expert', 0, 0,...]
    all_to_all x3, starting transfers between devices: 15.5 us -> 13.2 us  [exchange(): lax.all_to_all(rows.reshape(expert_count, -1, sub_width), 'expert', 0, 0,...]
    unnamed x19 -> x12, local copies, waits for them, and re-layouts: 3.61 us -> 1.64 us
  transfers between devices with their start and end apart: 24 -> 21, of which waited for: 9 -> 12; matrix products, arithmetic and copies ran while one was open for 1% -> 1% of each run, Pallas kernels for 20% -> 19%
where the time goes in v3:
time: 88.2 us; the launch traced here: 87.6 us
  starting transfers between devices  30.6 us (35%)
  waiting for transfers between devices  30.5 us (35%)
  Pallas kernels  23 us (26%)
  local copies, waits for them, and re-layouts  2.64 us (3%)
    ppermute x18, waiting for transfers between devices, swap(): lax.ppermute(value, axis, [(index, index ^ offset) for index in range(lax...  25.1 us
    ppermute x18, starting transfers between devices, swap(): lax.ppermute(value, axis, [(index, index ^ offset) for index in range(lax...  17.4 us
    all_to_all x3, starting transfers between devices, exchange(): lax.all_to_all(rows.reshape(expert_count, -1, sub_width), 'expert', 0, 0,...  13.2 us
    pallas_call x1, Pallas kernels, on_device(): pl.pallas_call(delta_body, in_specs=[anywhere] * 6, out_specs=(inside, an...  5.49 us
    all_to_all x3, waiting for transfers between devices, exchange(): lax.all_to_all(rows.reshape(expert_count, -1, sub_width), 'expert', 0, 0,...  5.4 us
    pallas_call x1, Pallas kernels, on_device(): pl.pallas_call(forward_body, in_specs=[anywhere] * 3, out_specs=(anywhere...  4.27 us
    pallas_call x1, Pallas kernels, on_device(): pl.pallas_call(split_kernel, in_specs=[inside, anywhere, inside], out_sha...  3.23 us
    pallas_call x1, Pallas kernels, on_device(): pl.pallas_call(weight_body, in_specs=[anywhere, anywhere, inside, anywher...  2.91 us
  transfers between devices with their start and end apart: 21, of which 12 were waited for; matrix products, arithmetic and copies ran while one was open for 1% of the time, Pallas kernels for 19%

profile of v3, /device:TPU:0, one launch (start us, length us, event | category | flops | bytes accessed | tf_op | source)
XLA Modules:
  0.0 87.6 jit_solution(3363214750707760773)
XLA Ops:
  1.5 3.1 %collective-permute-start = (bf16[2,32,1024]{2,1,0:T(8,128)(2,1)S(1)}, bf16[2,32,1024]{2,1,0:T(8,128)(2,1)S(1)}, u32[]{:S(2)}, u32[]{:S(2)}) collective-permute-start(bf16[2,32,1024]{2,1,0:T(8,128)(2,1)S(1)} %pad_maximum_fusion.2), channel_id=1, source_target_pairs={{0,8},{4,12},{8,0},{12,4},{16,24},{20,28},{24,16},{28,20},{1,9},{5... | collective-permute-start | bytes 393224 | tf_op jit(solution)/shard_map/ppermute | solution.py:36
  4.6 2.5 %collective-permute-start.5 = (bf16[2,32,1024]{2,1,0:T(8,128)(2,1)S(1)}, bf16[2,32,1024]{2,1,0:T(8,128)(2,1)S(1)}, u32[]{:S(2)}, u32[]{:S(2)}) collective-permute-start(bf16[2,32,1024]{2,1,0:T(8,128)(2,1)S(1)} %pad_maximum_fusion.2), channel_id=1, source_target_pairs={{0,24},{4,28},{8,16},{12,20},{16,8},{20,12},{24,0},{28,4},{1,25},{... | collective-permute-start | bytes 393224 | tf_op jit(solution)/shard_map/ppermute | solution.py:36
  8.1 2.4 %shard_map.120 = (bf16[1024,256]{1,0:T(8,128)(2,1)}, s32[4,128]{1,0:T(4,128)S(1)}, s32[128,4]{1,0:T(8,128)S(1)}) custom-call(s32[4,128]{1,0:T(4,128)S(1)} %bitcast.32, bf16[128,1024]{1,0:T(8,128)(2,1)} %bitcast.46), custom_call_target="tpu_custom_call" | custom-call | flops 1 | bytes 1 | tf_op jit(solution)/shard_map/pallas_call | solution.py:427
  10.5 1.7 %collective-permute-start.1 = (bf16[128,1024]{1,0:T(8,128)(2,1)}, bf16[128,1024]{1,0:T(8,128)(2,1)S(1)}, u32[]{:S(2)}, u32[]{:S(2)}) collective-permute-start(bf16[128,1024]{1,0:T(8,128)(2,1)} %bitcast.33), channel_id=1, source_target_pairs={{0,2},{1,3},{2,0},{3,1},{4,6},{5,7},{6,4},{7,5},{8,10},{9,11},{10,... | collective-permute-start | bytes 786440 | tf_op jit(solution)/shard_map/ppermute | solution.py:36
  12.2 2.2 %collective-permute-done.5 = bf16[2,32,1024]{2,1,0:T(8,128)(2,1)S(1)} collective-permute-done((bf16[2,32,1024]{2,1,0:T(8,128)(2,1)S(1)}, bf16[2,32,1024]{2,1,0:T(8,128)(2,1)S(1)}, u32[]{:S(2)}, u32[]{:S(2)}) %collective-permute-start.5) | collective-permute-done | bytes 131104 | tf_op jit(solution)/shard_map/ppermute | solution.py:36
  14.4 4.5 %collective-permute-done.4 = bf16[2,32,1024]{2,1,0:T(8,128)(2,1)S(1)} collective-permute-done((bf16[2,32,1024]{2,1,0:T(8,128)(2,1)S(1)}, bf16[2,32,1024]{2,1,0:T(8,128)(2,1)S(1)}, u32[]{:S(2)}, u32[]{:S(2)}) %collective-permute-start.4) | collective-permute-done | bytes 131104 | tf_op jit(solution)/shard_map/ppermute | solution.py:36
  18.9 1.6 %collective-permute-start.6 = (bf16[128,1024]{1,0:T(8,128)(2,1)S(1)}, bf16[128,1024]{1,0:T(8,128)(2,1)S(1)}, u32[]{:S(2)}, u32[]{:S(2)}) collective-permute-start(bf16[128,1024]{1,0:T(8,128)(2,1)S(1)} %pad_maximum_fusion.refs_4_), channel_id=1, source_target_pairs={{0,4},{4,0},{8,12},{12,8},{16,20},{20,16},{24,28},{28,24},{1,5},{5... | collective-permute-start | bytes 786440 | tf_op jit(solution)/shard_map/ppermute | solution.py:36
  20.5 4.7 %all-to-all-start = ((bf16[8,128,256]{2,1,0:T(8,128)(2,1)}), bf16[8,128,256]{2,1,0:T(8,128)(2,1)S(1)}, u32[]{:S(2)}, u32[]{:S(2)}) async-start(bf16[8,128,256]{2,1,0:T(8,128)(2,1)} %bitcast.9), calls=%async_computation | async-start | bytes 1048576 | tf_op jit(solution)/shard_map/all_to_all | solution.py:445
  27.3 1.6 %collective-permute-start.10 = (bf16[128,1024]{1,0:T(8,128)(2,1)S(1)}, bf16[128,1024]{1,0:T(8,128)(2,1)S(1)}, u32[]{:S(2)}, u32[]{:S(2)}) collective-permute-start(bf16[128,1024]{1,0:T(8,128)(2,1)S(1)} %pad_maximum_fusion.1.refs_0_), channel_id=1, source_target_pairs={{0,4},{4,0},{8,12},{12,8},{16,20},{20,16},{24,28},{28,24},{1,5},{5... | collective-permute-start | bytes 786440 | tf_op jit(solution)/shard_map/ppermute | solution.py:36
  28.9 1.5 %collective-permute-start.7 = (bf16[128,256]{1,0:T(8,128)(2,1)S(1)}, bf16[128,256]{1,0:T(8,128)(2,1)S(1)}, u32[]{:S(2)}, u32[]{:S(2)}) collective-permute-start(bf16[128,256]{1,0:T(8,128)(2,1)S(1)} %get-tuple-element.42), channel_id=1, source_target_pairs={{0,2},{1,3},{2,0},{3,1},{4,6},{5,7},{6,4},{7,5},{8,10},{9,11},{10,... | collective-permute-start | bytes 196616 | tf_op jit(solution)/shard_map/ppermute | solution.py:36
  31.1 2.0 %collective-permute-done.7.refs_3_ = bf16[128,256]{1,0:T(8,128)(2,1)S(1)} collective-permute-done((bf16[128,256]{1,0:T(8,128)(2,1)S(1)}, bf16[128,256]{1,0:T(8,128)(2,1)S(1)}, u32[]{:S(2)}, u32[]{:S(2)}) %collective-permute-start.7) | collective-permute-done | bytes 65568 | tf_op jit(solution)/shard_map/ppermute | solution.py:36
  34.1 1.7 %shard_map.122 = bf16[1024,256]{1,0:T(8,128)(2,1)} custom-call(f32[128,4]{1,0:T(8,128)S(1)} %bitcast.31, s32[4,128]{1,0:T(4,128)S(1)} %get-tuple-element.39.refs_1_, bf16[128,256]{1,0:T(8,128)(2,1)S(1)} %get-tuple-element.41.refs_2_, bf16[128,256]{1,0:T(8,128)(2,1)S(1)} %collective-permute-done.7.refs_3_, ...), custom_call_target="tpu_custom_call" | custom-call | flops 1 | bytes 1 | tf_op jit(solution)/shard_map/pallas_call | solution.py:478
  35.8 3.7 %collective-permute-done.10.refs_1_ = bf16[128,1024]{1,0:T(8,128)(2,1)S(1)} collective-permute-done((bf16[128,1024]{1,0:T(8,128)(2,1)S(1)}, bf16[128,1024]{1,0:T(8,128)(2,1)S(1)}, u32[]{:S(2)}, u32[]{:S(2)}) %collective-permute-start.10) | collective-permute-done | bytes 262176 | tf_op jit(solution)/shard_map/ppermute | solution.py:36
  40.3 3.7 %all-to-all-start.1 = ((bf16[8,128,256]{2,1,0:T(8,128)(2,1)}), bf16[8,128,256]{2,1,0:T(8,128)(2,1)S(1)}, u32[]{:S(2)}, u32[]{:S(2)}) async-start(bf16[8,128,256]{2,1,0:T(8,128)(2,1)} %bitcast.14), calls=%async_computation.1 | async-start | bytes 1048576 | tf_op jit(solution)/shard_map/all_to_all | solution.py:445
  44.1 1.6 %collective-permute-start.11 = (bf16[256,1024]{1,0:T(8,128)(2,1)S(1)}, bf16[256,1024]{1,0:T(8,128)(2,1)}, u32[]{:S(2)}, u32[]{:S(2)}) collective-permute-start(bf16[256,1024]{1,0:T(8,128)(2,1)S(1)} %shard_map.123.refs_0_), channel_id=1, source_target_pairs={{0,2},{1,3},{2,0},{3,1},{4,6},{5,7},{6,4},{7,5},{8,10},{9,11},{10,... | collective-permute-start | bytes 1572872 | tf_op jit(solution)/shard_map/ppermute | solution.py:36
  45.6 4.3 %shard_map.124 = (bf16[1024,256]{1,0:T(8,128)(2,1)}, bf16[1024,768]{1,0:T(8,128)(2,1)}, bf16[1024,768]{1,0:T(8,128)(2,1)}, bf16[1024,768]{1,0:T(8,128)(2,1)}) custom-call(bf16[1024,256]{1,0:T(8,128)(2,1)S(1)} %bitcast.30, bf16[256,768]{1,0:T(8,128)(2,1)} %bitcast.37, bf16[256,768]{1,0:T(8,128)(2,1)} %bitcast.39), custom_call_target="tpu_custom_call" | custom-call | tf_op jit(solution)/shard_map/pallas_call | solution.py:522
  49.9 7.9 %collective-permute-done.11.refs_1_ = bf16[256,1024]{1,0:T(8,128)(2,1)} collective-permute-done((bf16[256,1024]{1,0:T(8,128)(2,1)S(1)}, bf16[256,1024]{1,0:T(8,128)(2,1)}, u32[]{:S(2)}, u32[]{:S(2)}) %collective-permute-start.11) | collective-permute-done | bytes 524320 | tf_op jit(solution)/shard_map/ppermute | solution.py:36
  59.5 5.5 %shard_map.125 = (bf16[1024,1536]{1,0:T(8,128)(2,1)S(1)}, bf16[1024,256]{1,0:T(8,128)(2,1)}, bf16[1024,256]{1,0:T(8,128)(2,1)}) custom-call(bf16[1024,256]{1,0:T(8,128)(2,1)} %bitcast.36, bf16[1024,768]{1,0:T(8,128)(2,1)} %get-tuple-element.50.refs_1_, bf16[1024,768]{1,0:T(8,128)(2,1)} %get-tuple-element.51.refs_2_, bf16[256,768]{1,0:T(8,128)(2,1)} %bitcast.38, ...), custom_call_target="tpu_custom_call" | custom-call | tf_op jit(solution)/shard_map/pallas_call | solution.py:536
  65.0 4.9 %all-to-all-start.2 = ((bf16[8,128,256]{2,1,0:T(8,128)(2,1)}), bf16[8,128,256]{2,1,0:T(8,128)(2,1)}, u32[]{:S(2)}, u32[]{:S(2)}) async-start(bf16[8,128,256]{2,1,0:T(8,128)(2,1)} %bitcast.43), calls=%async_computation.2 | async-start | bytes 1048576 | tf_op jit(solution)/shard_map/all_to_all | solution.py:445
  69.9 2.9 %shard_map.128 = (f32[2,64,1536]{2,1,0:T(8,128)S(1)}, f32[2,192,256]{2,1,0:T(8,128)S(1)}, bf16[2,64,1536]{2,1,0:T(8,128)(2,1)S(1)}, bf16[2,192,256]{2,1,0:T(8,128)(2,1)S(1)}) custom-call(bf16[1024,256]{1,0:T(8,128)(2,1)} %get-tuple-element.53.refs_0_, bf16[1024,256]{1,0:T(8,128)(2,1)} %get-tuple-element.54.refs_1_, ...), custom_call_target="tpu_custom_call" | custom-call | flops 1207959552 | bytes 6291456 | tf_op jit(solution)/shard_map/pallas_call | solution.py:560
  73.9 2.5 %collective-permute-done.15.got_b = bf16[2,192,256]{2,1,0:T(8,128)(2,1)S(1)} collective-permute-done((bf16[2,192,256]{2,1,0:T(8,128)(2,1)S(1)}, bf16[2,192,256]{2,1,0:T(8,128)(2,1)S(1)}, u32[]{:S(2)}, u32[]{:S(2)}) %collective-permute-start.15) | collective-permute-done | bytes 196640 | tf_op jit(solution)/shard_map/ppermute | solution.py:36
  76.5 1.6 %collective-permute-start.16 = (bf16[1,64,1536]{2,1,0:T(8,128)(2,1)S(1)}, bf16[1,64,1536]{2,1,0:T(8,128)(2,1)S(1)}, u32[]{:S(2)}, u32[]{:S(2)}) collective-permute-start(bf16[1,64,1536]{2,1,0:T(8,128)(2,1)S(1)} %get-tuple-element.64), channel_id=1, source_target_pairs={{0,2},{1,3},{2,0},{3,1},{4,6},{5,7},{6,4},{7,5},{8,10},{9,11},{10,... | collective-permute-start | bytes 589832 | tf_op jit(solution)/shard_map/ppermute | solution.py:36
  79.8 3.7 %all-to-all-done.2 = bf16[8,128,256]{2,1,0:T(8,128)(2,1)} async-done(((bf16[8,128,256]{2,1,0:T(8,128)(2,1)}), bf16[8,128,256]{2,1,0:T(8,128)(2,1)}, u32[]{:S(2)}, u32[]{:S(2)}) %all-to-all-start.2) | async-done | bytes 524320 | tf_op jit(solution)/shard_map/all_to_all | solution.py:445
  83.5 3.2 %shard_map.127 = bf16[128,1024]{1,0:T(8,128)(2,1)} custom-call(s32[128,4]{1,0:T(8,128)S(1)} %get-tuple-element.38.down_ref, bf16[1024,256]{1,0:T(8,128)(2,1)} %bitcast.20.back_ref, bf16[1024,1024]{1,0:T(8,128)(2,1)S(1)} %shard_map.126.weight_ref), custom_call_target="tpu_custom_call" | custom-call | tf_op jit(solution)/shard_map/pallas_call | solution.py:603
  (49 shorter events, 12.1 us)
Async XLA Ops:
  1.5 6.6 %collective-permute-start = (bf16[2,32,1024]{2,1,0:T(8,128)(2,1)S(1)}, bf16[2,32,1024]{2,1,0:T(8,128)(2,1)S(1)}, u32[]{:S(2)}, u32[]{:S(2)}) collective-permute-start(bf16[2,32,1024]{2,1,0:T(8,128)(2,1)S(1)} %pad_maximum_fusion.2), channel_id=1, source_target_pairs={{0,8},{4,12},{8,0},{12,4},{16,24},{20,28},{24,16},{28,20},{1,9},{5... | collective-permute-start | bytes 393224 | tf_op jit(solution)/shard_map/ppermute | solution.py:36
  4.6 9.7 %collective-permute-start.5 = (bf16[2,32,1024]{2,1,0:T(8,128)(2,1)S(1)}, bf16[2,32,1024]{2,1,0:T(8,128)(2,1)S(1)}, u32[]{:S(2)}, u32[]{:S(2)}) collective-permute-start(bf16[2,32,1024]{2,1,0:T(8,128)(2,1)S(1)} %pad_maximum_fusion.2), channel_id=1, source_target_pairs={{0,24},{4,28},{8,16},{12,20},{16,8},{20,12},{24,0},{28,4},{1,25},{... | collective-permute-start | bytes 393224 | tf_op jit(solution)/shard_map/ppermute | solution.py:36
  7.1 11.8 %collective-permute-start.4 = (bf16[2,32,1024]{2,1,0:T(8,128)(2,1)S(1)}, bf16[2,32,1024]{2,1,0:T(8,128)(2,1)S(1)}, u32[]{:S(2)}, u32[]{:S(2)}) collective-permute-start(bf16[2,32,1024]{2,1,0:T(8,128)(2,1)S(1)} %pad_maximum_fusion.2), channel_id=1, source_target_pairs={{0,16},{4,20},{8,24},{12,28},{16,0},{20,4},{24,8},{28,12},{1,17},{... | collective-permute-start | bytes 393224 | tf_op jit(solution)/shard_map/ppermute | solution.py:36
  8.1 18.3 %copy-start.2 = (bf16[2,64,1024]{2,1,0:T(8,128)(2,1)S(1)}, bf16[2,64,1024]{2,1,0:T(8,128)(2,1)}, u32[]{:S(2)}) copy-start(bf16[2,64,1024]{2,1,0:T(8,128)(2,1)} %param.9) | copy-start | bytes 786436
  10.5 10.0 %collective-permute-start.1 = (bf16[128,1024]{1,0:T(8,128)(2,1)}, bf16[128,1024]{1,0:T(8,128)(2,1)S(1)}, u32[]{:S(2)}, u32[]{:S(2)}) collective-permute-start(bf16[128,1024]{1,0:T(8,128)(2,1)} %bitcast.33), channel_id=1, source_target_pairs={{0,2},{1,3},{2,0},{3,1},{4,6},{5,7},{6,4},{7,5},{8,10},{9,11},{10,... | collective-permute-start | bytes 786440 | tf_op jit(solution)/shard_map/ppermute | solution.py:36
  12.2 13.0 %collective-permute-start.2 = (bf16[128,1024]{1,0:T(8,128)(2,1)}, bf16[128,1024]{1,0:T(8,128)(2,1)S(1)}, u32[]{:S(2)}, u32[]{:S(2)}) collective-permute-start(bf16[128,1024]{1,0:T(8,128)(2,1)} %bitcast.34), channel_id=1, source_target_pairs={{0,1},{1,0},{2,3},{3,2},{4,5},{5,4},{6,7},{7,6},{8,9},{9,8},{10,11... | collective-permute-start | bytes 786440 | tf_op jit(solution)/shard_map/ppermute | solution.py:36
  18.9 7.5 %collective-permute-start.6 = (bf16[128,1024]{1,0:T(8,128)(2,1)S(1)}, bf16[128,1024]{1,0:T(8,128)(2,1)S(1)}, u32[]{:S(2)}, u32[]{:S(2)}) collective-permute-start(bf16[128,1024]{1,0:T(8,128)(2,1)S(1)} %pad_maximum_fusion.refs_4_), channel_id=1, source_target_pairs={{0,4},{4,0},{8,12},{12,8},{16,20},{20,16},{24,28},{28,24},{1,5},{5... | collective-permute-start | bytes 786440 | tf_op jit(solution)/shard_map/ppermute | solution.py:36
  20.5 5.9 %collective-permute-start.3 = (bf16[128,1024]{1,0:T(8,128)(2,1)S(1)}, bf16[128,1024]{1,0:T(8,128)(2,1)S(1)}, u32[]{:S(2)}, u32[]{:S(2)}) collective-permute-start(bf16[128,1024]{1,0:T(8,128)(2,1)S(1)} %collective-permute-done.1.refs_1_), channel_id=1, source_target_pairs={{0,1},{1,0},{2,3},{3,2},{4,5},{5,4},{6,7},{7,6},{8,9},{9,8},{10,11... | collective-permute-start | bytes 786440 | tf_op jit(solution)/shard_map/ppermute | solution.py:36
  20.5 19.8 %all-to-all-start = ((bf16[8,128,256]{2,1,0:T(8,128)(2,1)}), bf16[8,128,256]{2,1,0:T(8,128)(2,1)S(1)}, u32[]{:S(2)}, u32[]{:S(2)}) async-start(bf16[8,128,256]{2,1,0:T(8,128)(2,1)} %bitcast.9), calls=%async_computation | async-start | bytes 1048576 | tf_op jit(solution)/shard_map/all_to_all | solution.py:445
  25.2 5.8 %copy-start.4 = (f32[2,64,4]{1,2,0:T(4,128)S(1)}, f32[2,64,4]{1,2,0:T(4,128)}, u32[]{:S(2)}) copy-start(f32[2,64,4]{1,2,0:T(4,128)} %param.12) | copy-start | bytes 6148
  27.3 12.2 %collective-permute-start.10 = (bf16[128,1024]{1,0:T(8,128)(2,1)S(1)}, bf16[128,1024]{1,0:T(8,128)(2,1)S(1)}, u32[]{:S(2)}, u32[]{:S(2)}) collective-permute-start(bf16[128,1024]{1,0:T(8,128)(2,1)S(1)} %pad_maximum_fusion.1.refs_0_), channel_id=1, source_target_pairs={{0,4},{4,0},{8,12},{12,8},{16,20},{20,16},{24,28},{28,24},{1,5},{5... | collective-permute-start | bytes 786440 | tf_op jit(solution)/shard_map/ppermute | solution.py:36
  28.9 4.3 %collective-permute-start.7 = (bf16[128,256]{1,0:T(8,128)(2,1)S(1)}, bf16[128,256]{1,0:T(8,128)(2,1)S(1)}, u32[]{:S(2)}, u32[]{:S(2)}) collective-permute-start(bf16[128,256]{1,0:T(8,128)(2,1)S(1)} %get-tuple-element.42), channel_id=1, source_target_pairs={{0,2},{1,3},{2,0},{3,1},{4,6},{5,7},{6,4},{7,5},{8,10},{9,11},{10,... | collective-permute-start | bytes 196616 | tf_op jit(solution)/shard_map/ppermute | solution.py:36
  30.3 2.8 %collective-permute-start.8 = (bf16[128,256]{1,0:T(8,128)(2,1)S(1)}, bf16[128,256]{1,0:T(8,128)(2,1)S(1)}, u32[]{:S(2)}, u32[]{:S(2)}) collective-permute-start(bf16[128,256]{1,0:T(8,128)(2,1)S(1)} %get-tuple-element.43), channel_id=1, source_target_pairs={{0,1},{1,0},{2,3},{3,2},{4,5},{5,4},{6,7},{7,6},{8,9},{9,8},{10,11... | collective-permute-start | bytes 196616 | tf_op jit(solution)/shard_map/ppermute | solution.py:36
  30.3 3.7 %collective-permute-start.9 = (bf16[128,256]{1,0:T(8,128)(2,1)S(1)}, bf16[128,256]{1,0:T(8,128)(2,1)S(1)}, u32[]{:S(2)}, u32[]{:S(2)}) collective-permute-start(bf16[128,256]{1,0:T(8,128)(2,1)S(1)} %get-tuple-element.44), channel_id=1, source_target_pairs={{0,3},{1,2},{2,1},{3,0},{4,7},{5,6},{6,5},{7,4},{8,11},{9,10},{10,... | collective-permute-start | bytes 196616 | tf_op jit(solution)/shard_map/ppermute | solution.py:36
  40.3 18.4 %all-to-all-start.1 = ((bf16[8,128,256]{2,1,0:T(8,128)(2,1)}), bf16[8,128,256]{2,1,0:T(8,128)(2,1)S(1)}, u32[]{:S(2)}, u32[]{:S(2)}) async-start(bf16[8,128,256]{2,1,0:T(8,128)(2,1)} %bitcast.14), calls=%async_computation.1 | async-start | bytes 1048576 | tf_op jit(solution)/shard_map/all_to_all | solution.py:445
  44.1 5.8 %copy-start = (bf16[256,1024]{1,0:T(8,128)(2,1)}, bf16[256,1024]{1,0:T(8,128)(2,1)S(1)}, u32[]{:S(2)}) copy-start(bf16[256,1024]{1,0:T(8,128)(2,1)S(1)} %shard_map.123.refs_0_) | copy-start | bytes 1572868
  44.1 13.8 %collective-permute-start.11 = (bf16[256,1024]{1,0:T(8,128)(2,1)S(1)}, bf16[256,1024]{1,0:T(8,128)(2,1)}, u32[]{:S(2)}, u32[]{:S(2)}) collective-permute-start(bf16[256,1024]{1,0:T(8,128)(2,1)S(1)} %shard_map.123.refs_0_), channel_id=1, source_target_pairs={{0,2},{1,3},{2,0},{3,1},{4,6},{5,7},{6,4},{7,5},{8,10},{9,11},{10,... | collective-permute-start | bytes 1572872 | tf_op jit(solution)/shard_map/ppermute | solution.py:36
  65.0 18.4 %all-to-all-start.2 = ((bf16[8,128,256]{2,1,0:T(8,128)(2,1)}), bf16[8,128,256]{2,1,0:T(8,128)(2,1)}, u32[]{:S(2)}, u32[]{:S(2)}) async-start(bf16[8,128,256]{2,1,0:T(8,128)(2,1)} %bitcast.43), calls=%async_computation.2 | async-start | bytes 1048576 | tf_op jit(solution)/shard_map/all_to_all | solution.py:445
  72.8 3.6 %collective-permute-start.14 = (bf16[2,64,1536]{2,1,0:T(8,128)(2,1)S(1)}, bf16[2,64,1536]{2,1,0:T(8,128)(2,1)S(1)}, u32[]{:S(2)}, u32[]{:S(2)}) collective-permute-start(bf16[2,64,1536]{2,1,0:T(8,128)(2,1)S(1)} %get-tuple-element.59), channel_id=1, source_target_pairs={{0,1},{1,0},{2,3},{3,2},{4,5},{5,4},{6,7},{7,6},{8,9},{9,8},{10,11... | collective-permute-start | bytes 1179656 | tf_op jit(solution)/shard_map/ppermute | solution.py:36
  72.9 5.7 %collective-permute-start.12 = (bf16[256,1024]{1,0:T(8,128)(2,1)S(1)}, bf16[256,1024]{1,0:T(8,128)(2,1)S(1)}, u32[]{:S(2)}, u32[]{:S(2)}) collective-permute-start(bf16[256,1024]{1,0:T(8,128)(2,1)S(1)} %copy-done.1), channel_id=1, source_target_pairs={{0,1},{1,0},{2,3},{3,2},{4,5},{5,4},{6,7},{7,6},{8,9},{9,8},{10,11... | collective-permute-start | bytes 1572872 | tf_op jit(solution)/shard_map/ppermute | solution.py:36
  73.4 5.2 %collective-permute-start.13 = (bf16[256,1024]{1,0:T(8,128)(2,1)}, bf16[256,1024]{1,0:T(8,128)(2,1)S(1)}, u32[]{:S(2)}, u32[]{:S(2)}) collective-permute-start(bf16[256,1024]{1,0:T(8,128)(2,1)} %collective-permute-done.11.refs_1_), channel_id=1, source_target_pairs={{0,1},{1,0},{2,3},{3,2},{4,5},{5,4},{6,7},{7,6},{8,9},{9,8},{10,11... | collective-permute-start | bytes 1572872 | tf_op jit(solution)/shard_map/ppermute | solution.py:36
  73.5 2.9 %collective-permute-start.15 = (bf16[2,192,256]{2,1,0:T(8,128)(2,1)S(1)}, bf16[2,192,256]{2,1,0:T(8,128)(2,1)S(1)}, u32[]{:S(2)}, u32[]{:S(2)}) collective-permute-start(bf16[2,192,256]{2,1,0:T(8,128)(2,1)S(1)} %get-tuple-element.60), channel_id=1, source_target_pairs={{0,1},{1,0},{2,3},{3,2},{4,5},{5,4},{6,7},{7,6},{8,9},{9,8},{10,11... | collective-permute-start | bytes 589832 | tf_op jit(solution)/shard_map/ppermute | solution.py:36
  76.5 10.2 %collective-permute-start.16 = (bf16[1,64,1536]{2,1,0:T(8,128)(2,1)S(1)}, bf16[1,64,1536]{2,1,0:T(8,128)(2,1)S(1)}, u32[]{:S(2)}, u32[]{:S(2)}) collective-permute-start(bf16[1,64,1536]{2,1,0:T(8,128)(2,1)S(1)} %get-tuple-element.64), channel_id=1, source_target_pairs={{0,2},{1,3},{2,0},{3,1},{4,6},{5,7},{6,4},{7,5},{8,10},{9,11},{10,... | collective-permute-start | bytes 589832 | tf_op jit(solution)/shard_map/ppermute | solution.py:36
  78.1 8.6 %collective-permute-start.17 = (bf16[1,192,256]{2,1,0:T(8,128)(2,1)S(1)}, bf16[1,192,256]{2,1,0:T(8,128)(2,1)S(1)}, u32[]{:S(2)}, u32[]{:S(2)}) collective-permute-start(bf16[1,192,256]{2,1,0:T(8,128)(2,1)S(1)} %get-tuple-element.65), channel_id=1, source_target_pairs={{0,2},{1,3},{2,0},{3,1},{4,6},{5,7},{6,4},{7,5},{8,10},{9,11},{10,... | collective-permute-start | bytes 294920 | tf_op jit(solution)/shard_map/ppermute | solution.py:36
  (2 other events, 3.8 us)

commit v4 on v3

--- a/solution.py
+++ b/solution.py
@@ -199,16 +199,18 @@
 
 
 def forward_kernel(
-    rows, input_ref, gate_ref, up_ref, inputs_out, hidden_out, slope_out, activation_out,
-    inputs_held, gate_held, up_held, hidden, slope, activation_held, sems, weight_sems, out_sems
+    rows, input_ref, gate_ref, up_ref, down_ref, inputs_out, hidden_out, slope_out, activation_out,
+    down_held, inputs_held, gate_held, up_held, hidden, slope, activation_held, sems, weight_sems, out_sems
 ):
     copies = fetch(input_ref, inputs_held, sems, rows)
     weights = [
         pltpu.make_async_copy(gate_ref, gate_held, weight_sems.at[0]),
         pltpu.make_async_copy(up_ref, up_held, weight_sems.at[1]),
     ]
+    down_copy = pltpu.make_async_copy(down_ref, down_held, weight_sems.at[2])
     for copy in weights:
         copy.start()
+    down_copy.start()
     for copy in weights:
         copy.wait()
     outs = []
@@ -232,20 +234,21 @@
             )
         ):
             outs.append(send_out(source, target, part, out_sems.at[place, number]))
+    down_copy.wait()
     for copy in outs:
         copy.wait()
 
 
 def delta_kernel(
-    rows, grad_ref, slope_ref, activation_ref, gate_ref, up_ref, down_ref,
+    rows, grad_ref, slope_ref, activation_ref, gate_ref, up_ref, down_held,
     both_ref, delta_ref, grads_out,
-    grads_held, slope, activation, gate_held, up_held, down_held, out, sems, weight_sems, out_sems
+    grads_held, slope, activation, gate_held, up_held, out, sems, weight_sems, out_sems
 ):
     hidden_width = gate_ref.shape[1]
     weights = [
         pltpu.make_async_copy(source, target, weight_sems.at[number])
         for number, (source, target) in enumerate(
-            ((down_ref, down_held), (gate_ref, gate_held), (up_ref, up_held))
+            ((gate_ref, gate_held), (up_ref, up_held))
         )
     ]
     arriving = {}
@@ -259,11 +262,9 @@
                 )
             ]
 
+    bring(0)
     weights[0].start()
-    bring(0)
     weights[1].start()
-    weights[2].start()
-    weights[0].wait()
     outs = []
     for number, part in enumerate(rows):
         arriving[number][0].wait()
@@ -280,8 +281,8 @@
         both_ref[part, :hidden_width] = delta_gate
         both_ref[part, hidden_width:] = delta_up
         if number == 0:
+            weights[0].wait()
             weights[1].wait()
-            weights[2].wait()
         out[part, :] = (
             transposed(delta_gate, gate_held[...]) + transposed(delta_up, up_held[...])
         ).astype(jnp.bfloat16)
@@ -519,23 +520,23 @@
     def forward_body(*refs):
         forward_kernel(rows, *refs)
 
-    kept_inputs, hidden, slope, activation = pl.pallas_call(
+    kept_inputs, hidden, slope, activation, near_down = pl.pallas_call(
         forward_body,
-        in_specs=[anywhere] * 3,
-        out_specs=(anywhere,) * 4,
-        out_shape=(narrow_out, wide_out, wide_out, wide_out),
+        in_specs=[anywhere] * 4,
+        out_specs=(anywhere,) * 4 + (inside,),
+        out_shape=(narrow_out, wide_out, wide_out, wide_out, lying),
         scratch_shapes=[
-            narrow, upright, upright, wide, wide, wide, sems(steps), sems(2), sems(4, steps),
+            narrow, upright, upright, wide, wide, wide, sems(steps), sems(3), sems(4, steps),
         ],
         compiler_params=params(),
-    )(seen_inputs, *in_hbm(weight_gate, weight_up))
+    )(seen_inputs, *in_hbm(weight_gate, weight_up, weight_down))
 
     def delta_body(*refs):
         delta_kernel(rows, *refs)
 
     both, delta, kept_grads = pl.pallas_call(
         delta_body,
-        in_specs=[anywhere] * 6,
+        in_specs=[anywhere] * 5 + [inside],
         out_specs=(inside, anywhere, anywhere),
         out_shape=(
             pltpu.VMEM((slot_count, 2 * hidden_width), bf16),
@@ -543,11 +544,11 @@
             narrow_out,
         ),
         scratch_shapes=[
-            narrow, wide, wide, upright, upright, lying, narrow,
-            sems(3, steps), sems(3), sems(2, steps),
+            narrow, wide, wide, upright, upright, narrow,
+            sems(3, steps), sems(2), sems(2, steps),
         ],
         compiler_params=params(),
-    )(*in_hbm(seen_grads), *in_hbm(slope, activation, weight_gate, weight_up, weight_down))
+    )(*in_hbm(seen_grads), *in_hbm(slope, activation, weight_gate, weight_up), *in_vmem(near_down))
     returned = exchange(delta)
 
     half = group // 2

time: 88.2 us -> 88 us (level)
  no operation moved by 1% of the time
where the time goes in v4:
time: 88 us; the launch traced here: 87.4 us
  starting transfers between devices  30.6 us (35%)
  waiting for transfers between devices  30.5 us (35%)
  Pallas kernels  22.9 us (26%)
  local copies, waits for them, and re-layouts  2.65 us (3%)
    ppermute x18, waiting for transfers between devices, swap(): lax.ppermute(value, axis, [(index, index ^ offset) for index in range(lax...  25.1 us
    ppermute x18, starting transfers between devices, swap(): lax.ppermute(value, axis, [(index, index ^ offset) for index in range(lax...  17.4 us
    all_to_all x3, starting transfers between devices, exchange(): lax.all_to_all(rows.reshape(expert_count, -1, sub_width), 'expert', 0, 0,...  13.2 us
    all_to_all x3, waiting for transfers between devices, exchange(): lax.all_to_all(rows.reshape(expert_count, -1, sub_width), 'expert', 0, 0,...  5.39 us
    pallas_call x1, Pallas kernels, on_device(): pl.pallas_call(delta_body, in_specs=[anywhere] * 5 + [inside], out_specs=...  5.37 us
    pallas_call x1, Pallas kernels, on_device(): pl.pallas_call(forward_body, in_specs=[anywhere] * 4, out_specs=(anywhere...  4.28 us
    pallas_call x1, Pallas kernels, on_device(): pl.pallas_call(split_kernel, in_specs=[inside, anywhere, inside], out_sha...  3.23 us
    pallas_call x1, Pallas kernels, on_device(): pl.pallas_call(weight_body, in_specs=[anywhere, anywhere, inside, anywher...  2.91 us
  transfers between devices with their start and end apart: 21, of which 12 were waited for; matrix products, arithmetic and copies ran while one was open for 1% of the time, Pallas kernels for 19%

profile of v4, /device:TPU:0, one launch (start us, length us, event | category | flops | bytes accessed | tf_op | source)
XLA Modules:
  0.0 87.4 jit_solution(1322186547569162223)
XLA Ops:
  1.5 3.1 %collective-permute-start = (bf16[2,32,1024]{2,1,0:T(8,128)(2,1)S(1)}, bf16[2,32,1024]{2,1,0:T(8,128)(2,1)S(1)}, u32[]{:S(2)}, u32[]{:S(2)}) collective-permute-start(bf16[2,32,1024]{2,1,0:T(8,128)(2,1)S(1)} %pad_maximum_fusion.2), channel_id=1, source_target_pairs={{0,8},{4,12},{8,0},{12,4},{16,24},{20,28},{24,16},{28,20},{1,9},{5... | collective-permute-start | bytes 393224 | tf_op jit(solution)/shard_map/ppermute | solution.py:36
  4.6 2.5 %collective-permute-start.5 = (bf16[2,32,1024]{2,1,0:T(8,128)(2,1)S(1)}, bf16[2,32,1024]{2,1,0:T(8,128)(2,1)S(1)}, u32[]{:S(2)}, u32[]{:S(2)}) collective-permute-start(bf16[2,32,1024]{2,1,0:T(8,128)(2,1)S(1)} %pad_maximum_fusion.2), channel_id=1, source_target_pairs={{0,24},{4,28},{8,16},{12,20},{16,8},{20,12},{24,0},{28,4},{1,25},{... | collective-permute-start | bytes 393224 | tf_op jit(solution)/shard_map/ppermute | solution.py:36
  8.1 2.4 %shard_map.120 = (bf16[1024,256]{1,0:T(8,128)(2,1)}, s32[4,128]{1,0:T(4,128)S(1)}, s32[128,4]{1,0:T(8,128)S(1)}) custom-call(s32[4,128]{1,0:T(4,128)S(1)} %bitcast.32, bf16[128,1024]{1,0:T(8,128)(2,1)} %bitcast.46), custom_call_target="tpu_custom_call" | custom-call | flops 1 | bytes 1 | tf_op jit(solution)/shard_map/pallas_call | solution.py:428
  10.5 1.7 %collective-permute-start.1 = (bf16[128,1024]{1,0:T(8,128)(2,1)}, bf16[128,1024]{1,0:T(8,128)(2,1)S(1)}, u32[]{:S(2)}, u32[]{:S(2)}) collective-permute-start(bf16[128,1024]{1,0:T(8,128)(2,1)} %bitcast.33), channel_id=1, source_target_pairs={{0,2},{1,3},{2,0},{3,1},{4,6},{5,7},{6,4},{7,5},{8,10},{9,11},{10,... | collective-permute-start | bytes 786440 | tf_op jit(solution)/shard_map/ppermute | solution.py:36
  12.2 2.2 %collective-permute-done.5 = bf16[2,32,1024]{2,1,0:T(8,128)(2,1)S(1)} collective-permute-done((bf16[2,32,1024]{2,1,0:T(8,128)(2,1)S(1)}, bf16[2,32,1024]{2,1,0:T(8,128)(2,1)S(1)}, u32[]{:S(2)}, u32[]{:S(2)}) %collective-permute-start.5) | collective-permute-done | bytes 131104 | tf_op jit(solution)/shard_map/ppermute | solution.py:36
  14.4 4.5 %collective-permute-done.4 = bf16[2,32,1024]{2,1,0:T(8,128)(2,1)S(1)} collective-permute-done((bf16[2,32,1024]{2,1,0:T(8,128)(2,1)S(1)}, bf16[2,32,1024]{2,1,0:T(8,128)(2,1)S(1)}, u32[]{:S(2)}, u32[]{:S(2)}) %collective-permute-start.4) | collective-permute-done | bytes 131104 | tf_op jit(solution)/shard_map/ppermute | solution.py:36
  18.9 1.6 %collective-permute-start.6 = (bf16[128,1024]{1,0:T(8,128)(2,1)S(1)}, bf16[128,1024]{1,0:T(8,128)(2,1)S(1)}, u32[]{:S(2)}, u32[]{:S(2)}) collective-permute-start(bf16[128,1024]{1,0:T(8,128)(2,1)S(1)} %pad_maximum_fusion.refs_4_), channel_id=1, source_target_pairs={{0,4},{4,0},{8,12},{12,8},{16,20},{20,16},{24,28},{28,24},{1,5},{5... | collective-permute-start | bytes 786440 | tf_op jit(solution)/shard_map/ppermute | solution.py:36
  20.5 4.6 %all-to-all-start = ((bf16[8,128,256]{2,1,0:T(8,128)(2,1)}), bf16[8,128,256]{2,1,0:T(8,128)(2,1)S(1)}, u32[]{:S(2)}, u32[]{:S(2)}) async-start(bf16[8,128,256]{2,1,0:T(8,128)(2,1)} %bitcast.9), calls=%async_computation | async-start | bytes 1048576 | tf_op jit(solution)/shard_map/all_to_all | solution.py:446
  27.3 1.6 %collective-permute-start.10 = (bf16[128,1024]{1,0:T(8,128)(2,1)S(1)}, bf16[128,1024]{1,0:T(8,128)(2,1)S(1)}, u32[]{:S(2)}, u32[]{:S(2)}) collective-permute-start(bf16[128,1024]{1,0:T(8,128)(2,1)S(1)} %pad_maximum_fusion.1.refs_0_), channel_id=1, source_target_pairs={{0,4},{4,0},{8,12},{12,8},{16,20},{20,16},{24,28},{28,24},{1,5},{5... | collective-permute-start | bytes 786440 | tf_op jit(solution)/shard_map/ppermute | solution.py:36
  28.9 1.5 %collective-permute-start.7 = (bf16[128,256]{1,0:T(8,128)(2,1)S(1)}, bf16[128,256]{1,0:T(8,128)(2,1)S(1)}, u32[]{:S(2)}, u32[]{:S(2)}) collective-permute-start(bf16[128,256]{1,0:T(8,128)(2,1)S(1)} %get-tuple-element.43), channel_id=1, source_target_pairs={{0,2},{1,3},{2,0},{3,1},{4,6},{5,7},{6,4},{7,5},{8,10},{9,11},{10,... | collective-permute-start | bytes 196616 | tf_op jit(solution)/shard_map/ppermute | solution.py:36
  31.1 2.0 %collective-permute-done.7.refs_3_ = bf16[128,256]{1,0:T(8,128)(2,1)S(1)} collective-permute-done((bf16[128,256]{1,0:T(8,128)(2,1)S(1)}, bf16[128,256]{1,0:T(8,128)(2,1)S(1)}, u32[]{:S(2)}, u32[]{:S(2)}) %collective-permute-start.7) | collective-permute-done | bytes 65568 | tf_op jit(solution)/shard_map/ppermute | solution.py:36
  34.1 1.7 %shard_map.122 = bf16[1024,256]{1,0:T(8,128)(2,1)} custom-call(f32[128,4]{1,0:T(8,128)S(1)} %bitcast.31, s32[4,128]{1,0:T(4,128)S(1)} %get-tuple-element.40.refs_1_, bf16[128,256]{1,0:T(8,128)(2,1)S(1)} %get-tuple-element.42.refs_2_, bf16[128,256]{1,0:T(8,128)(2,1)S(1)} %collective-permute-done.7.refs_3_, ...), custom_call_target="tpu_custom_call" | custom-call | flops 1 | bytes 1 | tf_op jit(solution)/shard_map/pallas_call | solution.py:479
  35.8 3.7 %collective-permute-done.10.refs_1_ = bf16[128,1024]{1,0:T(8,128)(2,1)S(1)} collective-permute-done((bf16[128,1024]{1,0:T(8,128)(2,1)S(1)}, bf16[128,1024]{1,0:T(8,128)(2,1)S(1)}, u32[]{:S(2)}, u32[]{:S(2)}) %collective-permute-start.10) | collective-permute-done | bytes 262176 | tf_op jit(solution)/shard_map/ppermute | solution.py:36
  40.3 3.7 %all-to-all-start.1 = ((bf16[8,128,256]{2,1,0:T(8,128)(2,1)}), bf16[8,128,256]{2,1,0:T(8,128)(2,1)S(1)}, u32[]{:S(2)}, u32[]{:S(2)}) async-start(bf16[8,128,256]{2,1,0:T(8,128)(2,1)} %bitcast.14), calls=%async_computation.1 | async-start | bytes 1048576 | tf_op jit(solution)/shard_map/all_to_all | solution.py:446
  44.1 1.6 %collective-permute-start.11 = (bf16[256,1024]{1,0:T(8,128)(2,1)S(1)}, bf16[256,1024]{1,0:T(8,128)(2,1)}, u32[]{:S(2)}, u32[]{:S(2)}) collective-permute-start(bf16[256,1024]{1,0:T(8,128)(2,1)S(1)} %shard_map.123.refs_0_), channel_id=1, source_target_pairs={{0,2},{1,3},{2,0},{3,1},{4,6},{5,7},{6,4},{7,5},{8,10},{9,11},{10,... | collective-permute-start | bytes 1572872 | tf_op jit(solution)/shard_map/ppermute | solution.py:36
  45.6 4.3 %shard_map.124 = (bf16[1024,256]{1,0:T(8,128)(2,1)}, bf16[1024,768]{1,0:T(8,128)(2,1)}, bf16[1024,768]{1,0:T(8,128)(2,1)}, bf16[1024,768]{1,0:T(8,128)(2,1)}, bf16[768,256]{1,0:T(8,128)(2,1)S(1)}) custom-call(bf16[1024,256]{1,0:T(8,128)(2,1)S(1)} %bitcast.30, bf16[256,768]{1,0:T(8,128)(2,1)} %bitcast.37, bf16[256,768]{1,0:T(8,128)(2,1)} %bitcast.39, ...), custom_call_target="tpu_custom_call" | custom-call | tf_op jit(solution)/shard_map/pallas_call | solution.py:523
  49.9 7.9 %collective-permute-done.11.refs_1_ = bf16[256,1024]{1,0:T(8,128)(2,1)} collective-permute-done((bf16[256,1024]{1,0:T(8,128)(2,1)S(1)}, bf16[256,1024]{1,0:T(8,128)(2,1)}, u32[]{:S(2)}, u32[]{:S(2)}) %collective-permute-start.11) | collective-permute-done | bytes 524320 | tf_op jit(solution)/shard_map/ppermute | solution.py:36
  59.5 5.4 %shard_map.125 = (bf16[1024,1536]{1,0:T(8,128)(2,1)S(1)}, bf16[1024,256]{1,0:T(8,128)(2,1)}, bf16[1024,256]{1,0:T(8,128)(2,1)}) custom-call(bf16[1024,256]{1,0:T(8,128)(2,1)} %bitcast.36, bf16[1024,768]{1,0:T(8,128)(2,1)} %get-tuple-element.51.refs_1_, bf16[1024,768]{1,0:T(8,128)(2,1)} %get-tuple-element.52.refs_2_, bf16[256,768]{1,0:T(8,128)(2,1)} %bitcast.38, ...), custom_call_target="tpu_custom_call" | custom-call | tf_op jit(solution)/shard_map/pallas_call | solution.py:537
  64.9 4.9 %all-to-all-start.2 = ((bf16[8,128,256]{2,1,0:T(8,128)(2,1)}), bf16[8,128,256]{2,1,0:T(8,128)(2,1)}, u32[]{:S(2)}, u32[]{:S(2)}) async-start(bf16[8,128,256]{2,1,0:T(8,128)(2,1)} %bitcast.43), calls=%async_computation.2 | async-start | bytes 1048576 | tf_op jit(solution)/shard_map/all_to_all | solution.py:446
  69.8 2.9 %shard_map.128 = (f32[2,64,1536]{2,1,0:T(8,128)S(1)}, f32[2,192,256]{2,1,0:T(8,128)S(1)}, bf16[2,64,1536]{2,1,0:T(8,128)(2,1)S(1)}, bf16[2,192,256]{2,1,0:T(8,128)(2,1)S(1)}) custom-call(bf16[1024,256]{1,0:T(8,128)(2,1)} %get-tuple-element.55.refs_0_, bf16[1024,256]{1,0:T(8,128)(2,1)} %get-tuple-element.56.refs_1_, ...), custom_call_target="tpu_custom_call" | custom-call | flops 1207959552 | bytes 6291456 | tf_op jit(solution)/shard_map/pallas_call | solution.py:561
  73.8 2.5 %collective-permute-done.15.got_b = bf16[2,192,256]{2,1,0:T(8,128)(2,1)S(1)} collective-permute-done((bf16[2,192,256]{2,1,0:T(8,128)(2,1)S(1)}, bf16[2,192,256]{2,1,0:T(8,128)(2,1)S(1)}, u32[]{:S(2)}, u32[]{:S(2)}) %collective-permute-start.15) | collective-permute-done | bytes 196640 | tf_op jit(solution)/shard_map/ppermute | solution.py:36
  76.4 1.6 %collective-permute-start.16 = (bf16[1,64,1536]{2,1,0:T(8,128)(2,1)S(1)}, bf16[1,64,1536]{2,1,0:T(8,128)(2,1)S(1)}, u32[]{:S(2)}, u32[]{:S(2)}) collective-permute-start(bf16[1,64,1536]{2,1,0:T(8,128)(2,1)S(1)} %get-tuple-element.66), channel_id=1, source_target_pairs={{0,2},{1,3},{2,0},{3,1},{4,6},{5,7},{6,4},{7,5},{8,10},{9,11},{10,... | collective-permute-start | bytes 589832 | tf_op jit(solution)/shard_map/ppermute | solution.py:36
  79.7 3.7 %all-to-all-done.2 = bf16[8,128,256]{2,1,0:T(8,128)(2,1)} async-done(((bf16[8,128,256]{2,1,0:T(8,128)(2,1)}), bf16[8,128,256]{2,1,0:T(8,128)(2,1)}, u32[]{:S(2)}, u32[]{:S(2)}) %all-to-all-start.2) | async-done | bytes 524320 | tf_op jit(solution)/shard_map/all_to_all | solution.py:446
  83.3 3.2 %shard_map.127 = bf16[128,1024]{1,0:T(8,128)(2,1)} custom-call(s32[128,4]{1,0:T(8,128)S(1)} %copy-done.3, bf16[1024,256]{1,0:T(8,128)(2,1)} %bitcast.20.back_ref, bf16[1024,1024]{1,0:T(8,128)(2,1)S(1)} %shard_map.126.weight_ref), custom_call_target="tpu_custom_call" | custom-call | tf_op jit(solution)/shard_map/pallas_call | solution.py:604
  (53 shorter events, 12.2 us)
Async XLA Ops:
  1.5 6.6 %collective-permute-start = (bf16[2,32,1024]{2,1,0:T(8,128)(2,1)S(1)}, bf16[2,32,1024]{2,1,0:T(8,128)(2,1)S(1)}, u32[]{:S(2)}, u32[]{:S(2)}) collective-permute-start(bf16[2,32,1024]{2,1,0:T(8,128)(2,1)S(1)} %pad_maximum_fusion.2), channel_id=1, source_target_pairs={{0,8},{4,12},{8,0},{12,4},{16,24},{20,28},{24,16},{28,20},{1,9},{5... | collective-permute-start | bytes 393224 | tf_op jit(solution)/shard_map/ppermute | solution.py:36
  4.6 9.7 %collective-permute-start.5 = (bf16[2,32,1024]{2,1,0:T(8,128)(2,1)S(1)}, bf16[2,32,1024]{2,1,0:T(8,128)(2,1)S(1)}, u32[]{:S(2)}, u32[]{:S(2)}) collective-permute-start(bf16[2,32,1024]{2,1,0:T(8,128)(2,1)S(1)} %pad_maximum_fusion.2), channel_id=1, source_target_pairs={{0,24},{4,28},{8,16},{12,20},{16,8},{20,12},{24,0},{28,4},{1,25},{... | collective-permute-start | bytes 393224 | tf_op jit(solution)/shard_map/ppermute | solution.py:36
  7.1 11.8 %collective-permute-start.4 = (bf16[2,32,1024]{2,1,0:T(8,128)(2,1)S(1)}, bf16[2,32,1024]{2,1,0:T(8,128)(2,1)S(1)}, u32[]{:S(2)}, u32[]{:S(2)}) collective-permute-start(bf16[2,32,1024]{2,1,0:T(8,128)(2,1)S(1)} %pad_maximum_fusion.2), channel_id=1, source_target_pairs={{0,16},{4,20},{8,24},{12,28},{16,0},{20,4},{24,8},{28,12},{1,17},{... | collective-permute-start | bytes 393224 | tf_op jit(solution)/shard_map/ppermute | solution.py:36
  8.1 18.3 %copy-start.4 = (bf16[2,64,1024]{2,1,0:T(8,128)(2,1)S(1)}, bf16[2,64,1024]{2,1,0:T(8,128)(2,1)}, u32[]{:S(2)}) copy-start(bf16[2,64,1024]{2,1,0:T(8,128)(2,1)} %param.9) | copy-start | bytes 786436
  10.5 8.4 %copy-start.2 = (s32[128,4]{1,0:T(8,128)}, s32[128,4]{1,0:T(8,128)S(1)}, u32[]{:S(2)}) copy-start(s32[128,4]{1,0:T(8,128)S(1)} %get-tuple-element.39.down_ref) | copy-start | bytes 6148
  10.5 10.0 %collective-permute-start.1 = (bf16[128,1024]{1,0:T(8,128)(2,1)}, bf16[128,1024]{1,0:T(8,128)(2,1)S(1)}, u32[]{:S(2)}, u32[]{:S(2)}) collective-permute-start(bf16[128,1024]{1,0:T(8,128)(2,1)} %bitcast.33), channel_id=1, source_target_pairs={{0,2},{1,3},{2,0},{3,1},{4,6},{5,7},{6,4},{7,5},{8,10},{9,11},{10,... | collective-permute-start | bytes 786440 | tf_op jit(solution)/shard_map/ppermute | solution.py:36
  12.2 13.0 %collective-permute-start.2 = (bf16[128,1024]{1,0:T(8,128)(2,1)}, bf16[128,1024]{1,0:T(8,128)(2,1)S(1)}, u32[]{:S(2)}, u32[]{:S(2)}) collective-permute-start(bf16[128,1024]{1,0:T(8,128)(2,1)} %bitcast.34), channel_id=1, source_target_pairs={{0,1},{1,0},{2,3},{3,2},{4,5},{5,4},{6,7},{7,6},{8,9},{9,8},{10,11... | collective-permute-start | bytes 786440 | tf_op jit(solution)/shard_map/ppermute | solution.py:36
  18.9 7.5 %collective-permute-start.6 = (bf16[128,1024]{1,0:T(8,128)(2,1)S(1)}, bf16[128,1024]{1,0:T(8,128)(2,1)S(1)}, u32[]{:S(2)}, u32[]{:S(2)}) collective-permute-start(bf16[128,1024]{1,0:T(8,128)(2,1)S(1)} %pad_maximum_fusion.refs_4_), channel_id=1, source_target_pairs={{0,4},{4,0},{8,12},{12,8},{16,20},{20,16},{24,28},{28,24},{1,5},{5... | collective-permute-start | bytes 786440 | tf_op jit(solution)/shard_map/ppermute | solution.py:36
  20.5 5.9 %collective-permute-start.3 = (bf16[128,1024]{1,0:T(8,128)(2,1)S(1)}, bf16[128,1024]{1,0:T(8,128)(2,1)S(1)}, u32[]{:S(2)}, u32[]{:S(2)}) collective-permute-start(bf16[128,1024]{1,0:T(8,128)(2,1)S(1)} %collective-permute-done.1.refs_1_), channel_id=1, source_target_pairs={{0,1},{1,0},{2,3},{3,2},{4,5},{5,4},{6,7},{7,6},{8,9},{9,8},{10,11... | collective-permute-start | bytes 786440 | tf_op jit(solution)/shard_map/ppermute | solution.py:36
  20.5 19.8 %all-to-all-start = ((bf16[8,128,256]{2,1,0:T(8,128)(2,1)}), bf16[8,128,256]{2,1,0:T(8,128)(2,1)S(1)}, u32[]{:S(2)}, u32[]{:S(2)}) async-start(bf16[8,128,256]{2,1,0:T(8,128)(2,1)} %bitcast.9), calls=%async_computation | async-start | bytes 1048576 | tf_op jit(solution)/shard_map/all_to_all | solution.py:446
  27.3 12.2 %collective-permute-start.10 = (bf16[128,1024]{1,0:T(8,128)(2,1)S(1)}, bf16[128,1024]{1,0:T(8,128)(2,1)S(1)}, u32[]{:S(2)}, u32[]{:S(2)}) collective-permute-start(bf16[128,1024]{1,0:T(8,128)(2,1)S(1)} %pad_maximum_fusion.1.refs_0_), channel_id=1, source_target_pairs={{0,4},{4,0},{8,12},{12,8},{16,20},{20,16},{24,28},{28,24},{1,5},{5... | collective-permute-start | bytes 786440 | tf_op jit(solution)/shard_map/ppermute | solution.py:36
  28.9 4.3 %collective-permute-start.7 = (bf16[128,256]{1,0:T(8,128)(2,1)S(1)}, bf16[128,256]{1,0:T(8,128)(2,1)S(1)}, u32[]{:S(2)}, u32[]{:S(2)}) collective-permute-start(bf16[128,256]{1,0:T(8,128)(2,1)S(1)} %get-tuple-element.43), channel_id=1, source_target_pairs={{0,2},{1,3},{2,0},{3,1},{4,6},{5,7},{6,4},{7,5},{8,10},{9,11},{10,... | collective-permute-start | bytes 196616 | tf_op jit(solution)/shard_map/ppermute | solution.py:36
  30.4 2.8 %collective-permute-start.8 = (bf16[128,256]{1,0:T(8,128)(2,1)S(1)}, bf16[128,256]{1,0:T(8,128)(2,1)S(1)}, u32[]{:S(2)}, u32[]{:S(2)}) collective-permute-start(bf16[128,256]{1,0:T(8,128)(2,1)S(1)} %get-tuple-element.44), channel_id=1, source_target_pairs={{0,1},{1,0},{2,3},{3,2},{4,5},{5,4},{6,7},{7,6},{8,9},{9,8},{10,11... | collective-permute-start | bytes 196616 | tf_op jit(solution)/shard_map/ppermute | solution.py:36
  30.4 3.7 %collective-permute-start.9 = (bf16[128,256]{1,0:T(8,128)(2,1)S(1)}, bf16[128,256]{1,0:T(8,128)(2,1)S(1)}, u32[]{:S(2)}, u32[]{:S(2)}) collective-permute-start(bf16[128,256]{1,0:T(8,128)(2,1)S(1)} %get-tuple-element.45), channel_id=1, source_target_pairs={{0,3},{1,2},{2,1},{3,0},{4,7},{5,6},{6,5},{7,4},{8,11},{9,10},{10,... | collective-permute-start | bytes 196616 | tf_op jit(solution)/shard_map/ppermute | solution.py:36
  40.3 18.4 %all-to-all-start.1 = ((bf16[8,128,256]{2,1,0:T(8,128)(2,1)}), bf16[8,128,256]{2,1,0:T(8,128)(2,1)S(1)}, u32[]{:S(2)}, u32[]{:S(2)}) async-start(bf16[8,128,256]{2,1,0:T(8,128)(2,1)} %bitcast.14), calls=%async_computation.1 | async-start | bytes 1048576 | tf_op jit(solution)/shard_map/all_to_all | solution.py:446
  44.0 5.9 %copy-start = (bf16[256,1024]{1,0:T(8,128)(2,1)}, bf16[256,1024]{1,0:T(8,128)(2,1)S(1)}, u32[]{:S(2)}) copy-start(bf16[256,1024]{1,0:T(8,128)(2,1)S(1)} %shard_map.123.refs_0_) | copy-start | bytes 1572868
  44.1 13.8 %collective-permute-start.11 = (bf16[256,1024]{1,0:T(8,128)(2,1)S(1)}, bf16[256,1024]{1,0:T(8,128)(2,1)}, u32[]{:S(2)}, u32[]{:S(2)}) collective-permute-start(bf16[256,1024]{1,0:T(8,128)(2,1)S(1)} %shard_map.123.refs_0_), channel_id=1, source_target_pairs={{0,2},{1,3},{2,0},{3,1},{4,6},{5,7},{6,4},{7,5},{8,10},{9,11},{10,... | collective-permute-start | bytes 1572872 | tf_op jit(solution)/shard_map/ppermute | solution.py:36
  64.9 18.4 %all-to-all-start.2 = ((bf16[8,128,256]{2,1,0:T(8,128)(2,1)}), bf16[8,128,256]{2,1,0:T(8,128)(2,1)}, u32[]{:S(2)}, u32[]{:S(2)}) async-start(bf16[8,128,256]{2,1,0:T(8,128)(2,1)} %bitcast.43), calls=%async_computation.2 | async-start | bytes 1048576 | tf_op jit(solution)/shard_map/all_to_all | solution.py:446
  72.7 3.6 %collective-permute-start.14 = (bf16[2,64,1536]{2,1,0:T(8,128)(2,1)S(1)}, bf16[2,64,1536]{2,1,0:T(8,128)(2,1)S(1)}, u32[]{:S(2)}, u32[]{:S(2)}) collective-permute-start(bf16[2,64,1536]{2,1,0:T(8,128)(2,1)S(1)} %get-tuple-element.61), channel_id=1, source_target_pairs={{0,1},{1,0},{2,3},{3,2},{4,5},{5,4},{6,7},{7,6},{8,9},{9,8},{10,11... | collective-permute-start | bytes 1179656 | tf_op jit(solution)/shard_map/ppermute | solution.py:36
  72.8 5.7 %collective-permute-start.12 = (bf16[256,1024]{1,0:T(8,128)(2,1)S(1)}, bf16[256,1024]{1,0:T(8,128)(2,1)S(1)}, u32[]{:S(2)}, u32[]{:S(2)}) collective-permute-start(bf16[256,1024]{1,0:T(8,128)(2,1)S(1)} %copy-done.1), channel_id=1, source_target_pairs={{0,1},{1,0},{2,3},{3,2},{4,5},{5,4},{6,7},{7,6},{8,9},{9,8},{10,11... | collective-permute-start | bytes 1572872 | tf_op jit(solution)/shard_map/ppermute | solution.py:36
  73.3 5.2 %collective-permute-start.13 = (bf16[256,1024]{1,0:T(8,128)(2,1)}, bf16[256,1024]{1,0:T(8,128)(2,1)S(1)}, u32[]{:S(2)}, u32[]{:S(2)}) collective-permute-start(bf16[256,1024]{1,0:T(8,128)(2,1)} %collective-permute-done.11.refs_1_), channel_id=1, source_target_pairs={{0,1},{1,0},{2,3},{3,2},{4,5},{5,4},{6,7},{7,6},{8,9},{9,8},{10,11... | collective-permute-start | bytes 1572872 | tf_op jit(solution)/shard_map/ppermute | solution.py:36
  73.4 2.9 %collective-permute-start.15 = (bf16[2,192,256]{2,1,0:T(8,128)(2,1)S(1)}, bf16[2,192,256]{2,1,0:T(8,128)(2,1)S(1)}, u32[]{:S(2)}, u32[]{:S(2)}) collective-permute-start(bf16[2,192,256]{2,1,0:T(8,128)(2,1)S(1)} %get-tuple-element.62), channel_id=1, source_target_pairs={{0,1},{1,0},{2,3},{3,2},{4,5},{5,4},{6,7},{7,6},{8,9},{9,8},{10,11... | collective-permute-start | bytes 589832 | tf_op jit(solution)/shard_map/ppermute | solution.py:36
  76.4 10.2 %collective-permute-start.16 = (bf16[1,64,1536]{2,1,0:T(8,128)(2,1)S(1)}, bf16[1,64,1536]{2,1,0:T(8,128)(2,1)S(1)}, u32[]{:S(2)}, u32[]{:S(2)}) collective-permute-start(bf16[1,64,1536]{2,1,0:T(8,128)(2,1)S(1)} %get-tuple-element.66), channel_id=1, source_target_pairs={{0,2},{1,3},{2,0},{3,1},{4,6},{5,7},{6,4},{7,5},{8,10},{9,11},{10,... | collective-permute-start | bytes 589832 | tf_op jit(solution)/shard_map/ppermute | solution.py:36
  77.9 8.6 %collective-permute-start.17 = (bf16[1,192,256]{2,1,0:T(8,128)(2,1)S(1)}, bf16[1,192,256]{2,1,0:T(8,128)(2,1)S(1)}, u32[]{:S(2)}, u32[]{:S(2)}) collective-permute-start(bf16[1,192,256]{2,1,0:T(8,128)(2,1)S(1)} %get-tuple-element.67), channel_id=1, source_target_pairs={{0,2},{1,3},{2,0},{3,1},{4,6},{5,7},{6,4},{7,5},{8,10},{9,11},{10,... | collective-permute-start | bytes 294920 | tf_op jit(solution)/shard_map/ppermute | solution.py:36
  (4 other events, 15.1 us)
